TPU v7x, 32 devices: a whole 2x2x4 slice. The times are simulated.
32 devices in a mesh: groups: 2 (over y), row: 8 (over z, x), col: 2 (over core).
Axes of the slice: x: 2, y: 2, z: 4, core: 2. Of those that a mesh axis runs over, the one named last changes fastest.
Arguments:
- tokens: bfloat16 [1024, 4096], P(('groups', 'row'), 'col'), parts along dimension 0, may hold values from -6 to 6
- up_weight: bfloat16 [4096, 32768], P('col', 'row'), may hold values from -0.09375 to 0.09375
- down_weight: bfloat16 [32768, 4096], P('row', 'col'), may hold values from -0.03125 to 0.03125
- cotangent: bfloat16 [1024, 4096], P(('groups', 'row'), 'col'), parts along dimension 0, may hold values from -6 to 6
Outputs:
- grad_input: bfloat16 [1024, 4096], P(('groups', 'row'), 'col'), parts along dimension 0
- grad_up: bfloat16 [8192, 32768], P(('groups', 'col'), 'row'), parts along dimension 0
- grad_down: bfloat16 [65536, 4096], P(('groups', 'row'), 'col'), parts along dimension 0
There are 2 independent parts, one for each index of `groups`. A program takes and returns all parts, laid end to end along the dimension named above; an argument that names none is the same for every part. Nothing has to cross between parts.
All inputs are finite; a program needn't handle non-finite values.
Results may differ from a plain program's by a relative error of at most 0.0051.
Values may be sent and summed in bfloat16 or wider, within the bound.
No kernel may reach another device: no remote copies, remote signals or barrier semaphores. Data moves between devices by JAX's collectives and lax.ppermute only.
A program may use at most 192 MiB of HBM per device.

v0:
```python
import jax
import jax.numpy as jnp
from jax import lax
from jax.sharding import PartitionSpec as P


def gelu_parts(preact):
    argument = 0.7978845608 * (preact + 0.044715 * preact * preact * preact)
    curve_term = jnp.tanh(argument)
    activated = 0.5 * preact * (1.0 + curve_term)
    factor = 0.5 * (1.0 + curve_term) + 0.5 * preact * (
        1.0 - curve_term * curve_term
    ) * 0.7978845608 * (1.0 + 3.0 * 0.044715 * preact * preact)
    return (activated, factor)


def times_transposed(left, right):
    return lax.dot_general(
        left, right, (((1,), (1,)), ((), ())), preferred_element_type=jnp.float32
    )


def transposed_times(left, right):
    return lax.dot_general(
        left, right, (((0,), (0,)), ((), ())), preferred_element_type=jnp.float32
    )


def per_device(tokens, up_weight, down_weight, cotangent):
    panel_tokens, panel_cotangent = (
        lax.all_gather(tokens, "row", axis=0, tiled=True),
        lax.all_gather(cotangent, "row", axis=0, tiled=True),
    )
    pre_part = jnp.dot(panel_tokens, up_weight, preferred_element_type=jnp.float32)
    back_part = times_transposed(panel_cotangent, down_weight)
    preact, back_grad = lax.psum((pre_part, back_part), "col")
    activated, factor = gelu_parts(preact)
    activated = activated.astype(jnp.bfloat16)
    delta = (back_grad * factor).astype(jnp.bfloat16)
    grad_down = transposed_times(activated, panel_cotangent)
    grad_up = transposed_times(panel_tokens, delta)
    grad_input = lax.psum_scatter(
        times_transposed(delta, up_weight), "row", scatter_dimension=0, tiled=True
    ).astype(jnp.bfloat16)
    return (grad_input, grad_up.astype(jnp.bfloat16), grad_down.astype(jnp.bfloat16))


def solution(mesh):
    in_specs = (
        P(("groups", "row"), "col"),
        P("col", "row"),
        P("row", "col"),
        P(("groups", "row"), "col"),
    )
    out_specs = (
        P(("groups", "row"), "col"),
        P(("groups", "col"), "row"),
        P(("groups", "row"), "col"),
    )
    return jax.shard_map(
        per_device, mesh=mesh, in_specs=in_specs, out_specs=out_specs, check_vma=False
    )
```

profile of v0, /device:TPU:0, one launch (start us, length us, event | category | flops | bytes accessed | tf_op | source)
XLA Modules:
  0.0 308.1 jit_solution(14770046936682174747)
XLA Ops:
  7.2 0.0 all-gather.3.cloned.1.call-start
  7.2 0.7 all-gather.3.cloned.1.call-update
  7.9 0.0 all-gather.5.cloned.1.call-start
  7.9 0.7 all-gather.5.cloned.1.call-update
  8.6 0.0 all-reduce.3.cloned.1.call-start
  8.7 53.4 %all-gather.3.cloned.1.call-done = bf16[512,2048]{1,0:T(8,128)(2,1)} async-done(((bf16[64,2048]{1,0:T(8,128)(2,1)}), bf16[512,2048]{1,0:T(8,128)(2,1)}) %all-gather.3.cloned.1.call-update) | async-done | bytes 2097168 | tf_op jit(solution)/shard_map/all_gather | solution.py:32
  62.1 15.1 %fusion.15 = f32[512,4096]{1,0:T(8,128)} fusion(bf16[512,2048]{1,0:T(8,128)(2,1)} %all-gather.3.cloned.1.call-done, bf16[4096,2048]{1,0:T(8,128)(2,1)} %param.6), kind=kOutput, calls=%fused_computation.20 | convolution fusion | flops 8589934592 | bytes 27262976 | tf_op jit(solution)/shard_map/dot_general | solution.py:18
  77.2 34.9 %all-gather.5.cloned.1.call-done = bf16[512,2048]{1,0:T(8,128)(2,1)} async-done(((bf16[64,2048]{1,0:T(8,128)(2,1)}), bf16[512,2048]{1,0:T(8,128)(2,1)}) %all-gather.5.cloned.1.call-update) | async-done | bytes 2097168 | tf_op jit(solution)/shard_map/all_gather | solution.py:31
  112.1 15.0 %fusion.16 = f32[512,4096]{1,0:T(8,128)} fusion(bf16[512,2048]{1,0:T(8,128)(2,1)} %all-gather.5.cloned.1.call-done, bf16[2048,4096]{1,0:T(8,128)(2,1)} %param.5), kind=kOutput, calls=%fused_computation.21 | convolution fusion | flops 8589934592 | bytes 27262976 | tf_op jit(solution)/shard_map/dot_general | solution.py:34
  127.1 0.0 all-reduce.3.cloned.1.call-update
  127.1 0.2 reduce-scatter.2.cloned.1.call-start
  127.3 58.4 %all-reduce.3.cloned.1.call-done = (f32[512,4096]{1,0:T(8,128)}, f32[512,4096]{1,0:T(8,128)}) async-done(((f32[512,4096]{1,0:T(8,128)}, f32[512,4096]{1,0:T(8,128)}), (f32[512,4096]{1,0:T(8,128)}, f32[512,4096]{1,0:T(8,128)})) %all-reduce.3.cloned.1.call-update) | async-done | bytes 16777232 | tf_op jit(solution)/shard_map/psum | solution.py:36
  185.8 8.8 %fusion.6 = bf16[512,4096]{1,0:T(8,128)(2,1)S(1)} fusion(f32[512,4096]{1,0:T(8,128)} %get-tuple-element.6, f32[512,4096]{1,0:T(8,128)} %get-tuple-element.7), kind=kLoop, calls=%fused_computation.10 | loop fusion | flops 39845888 | bytes 20971520 | tf_op jit(solution)/shard_map/convert_element_type | solution.py:39
  194.5 0.0 copy-start
  194.6 2.0 copy-done
  196.6 13.9 %fusion.17 = f32[512,2048]{1,0:T(8,128)} fusion(bf16[512,4096]{1,0:T(8,128)(2,1)S(1)} %fusion.6, bf16[2048,4096]{1,0:T(8,128)(2,1)} %param.5), kind=kOutput, calls=%fused_computation.22 | convolution fusion | flops 8589934592 | bytes 25165824 | tf_op jit(solution)/shard_map/dot_general | solution.py:18
  210.5 0.0 reduce-scatter.2.cloned.1.call-update
  210.5 0.0 copy-done.2
  210.5 14.8 %convert_bitcast_fusion = bf16[2048,4096]{0,1:T(8,128)(2,1)} fusion(bf16[512,4096]{1,0:T(8,128)(2,1)} %copy-done, bf16[512,2048]{1,0:T(8,128)(2,1)S(1)} %copy-done.2), kind=kOutput, calls=%fused_computation | convolution fusion | flops 8598323200 | bytes 23068672 | tf_op jit(solution)/shard_map/dot_general | solution.py:24
  225.3 21.4 %copy.7 = bf16[2048,4096]{1,0:T(8,128)(2,1)} copy(bf16[2048,4096]{0,1:T(8,128)(2,1)} %convert_bitcast_fusion) | data formatting | bytes 33554432
  246.7 0.0 copy-done.1
  246.7 19.0 %convolution_convert_fusion = bf16[4096,2048]{1,0:T(8,128)(2,1)} fusion(bf16[512,2048]{1,0:T(8,128)(2,1)S(1)} %copy-done.1, f32[512,4096]{1,0:T(8,128)} %get-tuple-element.7), kind=kOutput, calls=%fused_computation.1 | convolution fusion | flops 8617197568 | bytes 27262976 | tf_op jit(solution)/shard_map/dot_general | solution.py:24
  265.7 34.1 %reduce-scatter.2.cloned.1.call-done = f32[64,2048]{1,0:T(8,128)} async-done(((f32[512,2048]{1,0:T(8,128)}), f32[64,2048]{1,0:T(8,128)}) %reduce-scatter.2.cloned.1.call-update) | async-done | bytes 524304 | tf_op jit(solution)/shard_map/reduce_scatter | solution.py:42
  299.8 1.8 convert_element_type.19
  (2 shorter events, 0.0 us)
Async XLA Ops:
  7.2 55.0 %all-gather.3.cloned.1.call-start = ((), (), s32[]{:S(2)}) async-start(), calls=%async_computation.1 | async-start | bytes 2359296 | tf_op jit(solution)/shard_map/all_gather | solution.py:32
  7.9 104.2 %all-gather.5.cloned.1.call-start = ((), (), s32[]{:S(2)}) async-start(), calls=%async_computation.2 | async-start | bytes 2359296 | tf_op jit(solution)/shard_map/all_gather | solution.py:31
  8.6 177.1 %all-reduce.3.cloned.1.call-start = ((), (), s32[]{:S(2)}) async-start(), calls=%async_computation.4 | async-start | bytes 33554432 | tf_op jit(solution)/shard_map/psum | solution.py:36
  127.1 172.7 %reduce-scatter.2.cloned.1.call-start = ((), (), s32[]{:S(2)}) async-start(), calls=%async_computation.3 | async-start | bytes 4718592 | tf_op jit(solution)/shard_map/reduce_scatter | solution.py:42
  194.5 2.0 copy-start
  196.6 14.0 %copy-start.2 = (bf16[512,2048]{1,0:T(8,128)(2,1)S(1)}, bf16[512,2048]{1,0:T(8,128)(2,1)}, u32[]{:S(2)}) copy-start(bf16[512,2048]{1,0:T(8,128)(2,1)} %all-gather.5.cloned.1.call-done) | copy-start | bytes 6291460
  225.3 21.4 %copy-start.1 = (bf16[512,2048]{1,0:T(8,128)(2,1)S(1)}, bf16[512,2048]{1,0:T(8,128)(2,1)}, u32[]{:S(2)}) copy-start(bf16[512,2048]{1,0:T(8,128)(2,1)} %all-gather.3.cloned.1.call-done) | copy-start | bytes 6291460
Sparse Core Ops, SparseCore 0:
  10.1 51.9 all-gather.2
  64.3 47.7 all-gather.4
  127.2 58.5 all-reduce.2
  210.6 89.1 reduce-scatter.1
where the time goes:
time: 309 us; the launch traced here: 308 us
  waiting for transfers between devices  182 us (59%)
  matrix products  77.8 us (25%)
  local copies, waits for them, and re-layouts  23.4 us (8%)
  between operations  13.8 us (4%)
  other arithmetic  10.5 us (3%)
    psum x1, waiting for transfers between devices, per_device(): preact, back_grad = lax.psum((pre_part, back_part), 'col')  58.4 us
    all_gather x1, waiting for transfers between devices, per_device(): lax.all_gather(cotangent, 'row', axis=0, tiled=True)  53.4 us
    all_gather x1, waiting for transfers between devices, per_device(): lax.all_gather(tokens, 'row', axis=0, tiled=True)  34.9 us
    reduce_scatter x1, waiting for transfers between devices, per_device(): lax.psum_scatter(times_transposed(delta, up_weight), 'row', scatter_dimen...  34.1 us
    dot_general x2, matrix products, transposed_times(): lax.dot_general(left, right, (((0,), (0,)), ((), ())), preferred_element_...  33.8 us
    dot_general x2, matrix products, times_transposed(): lax.dot_general(left, right, (((1,), (1,)), ((), ())), preferred_element_...  29 us
    unnamed x7, local copies, waits for them, and re-layouts  23.4 us
    dot_general x1, matrix products, per_device(): jnp.dot(panel_tokens, up_weight, preferred_element_type=jnp.float32)  15 us
  transfers between devices with their start and end apart: 4, of which 4 were waited for; matrix products, arithmetic and copies ran while one was open for 23% of the time, Pallas kernels for 0%

commit v1 on v0

v1 whole, which is shorter than its diff:
```python
import functools

import jax
import jax.numpy as jnp
from jax import lax
from jax.experimental import pallas as pl
from jax.experimental.pallas import tpu as pltpu
from jax.sharding import PartitionSpec as P

F32 = jnp.float32
BF16 = jnp.bfloat16
VMEM_LIMIT = 56 * 1024 * 1024
NX = 2
NT = (((1,), (1,)), ((), ()))
TN = (((0,), (0,)), ((), ()))


def gelu_parts(preact):
    argument = 0.7978845608 * (preact + 0.044715 * preact * preact * preact)
    curve_term = jnp.tanh(argument)
    activated = 0.5 * preact * (1.0 + curve_term)
    factor = 0.5 * (1.0 + curve_term) + 0.5 * preact * (
        1.0 - curve_term * curve_term
    ) * 0.7978845608 * (1.0 + 3.0 * 0.044715 * preact * preact)
    return (activated, factor)


def params():
    return pltpu.CompilerParams(vmem_limit_bytes=VMEM_LIMIT)


def cost(flops, moved, transcendentals=0):
    return pl.CostEstimate(
        flops=flops, bytes_accessed=moved, transcendentals=transcendentals
    )


def stacked(refs, which):
    return jnp.concatenate([r[which] for r in refs], axis=0)


def hidden_pass(core, own, other, up, up_other, down, down_other):
    n = len(own)
    rows, feats = own[0].shape[1:]
    m = n * rows
    half = up_other.shape[1]
    tile = min(512, half)
    steps = half // tile

    def kernel(core_ref, *refs):
        own_refs, other_refs = refs[:n], refs[n : 2 * n]
        up_ref, up2_ref, down_ref, down2_ref, act_ref, delta_ref = refs[2 * n :]
        tok, tok2 = stacked(own_refs, 0), stacked(other_refs, 0)
        cot, cot2 = stacked(own_refs, 1), stacked(other_refs, 1)
        preact = jnp.dot(tok, up_ref[...], preferred_element_type=F32) + jnp.dot(
            tok2, up2_ref[...], preferred_element_type=F32
        )
        back = lax.dot_general(
            cot, down_ref[...], NT, preferred_element_type=F32
        ) + lax.dot_general(cot2, down2_ref[...], NT, preferred_element_type=F32)
        activated, factor = gelu_parts(preact)
        act_ref[...] = activated.astype(BF16)
        delta_ref[...] = (back * factor).astype(BF16)

    piece = pl.BlockSpec((2, rows, feats), lambda i, c: (0, 0, 0))
    out = pl.BlockSpec((m, tile), lambda i, c: (0, i))
    return pl.pallas_call(
        kernel,
        grid_spec=pltpu.PrefetchScalarGridSpec(
            num_scalar_prefetch=1,
            grid=(steps,),
            in_specs=[piece] * (2 * n)
            + [
                pl.BlockSpec((feats, tile), lambda i, c: (0, c[0] * steps + i)),
                pl.BlockSpec((feats, tile), lambda i, c: (0, i)),
                pl.BlockSpec((tile, feats), lambda i, c: (c[0] * steps + i, 0)),
                pl.BlockSpec((tile, feats), lambda i, c: (i, 0)),
            ],
            out_specs=[out, out],
        ),
        out_shape=[jax.ShapeDtypeStruct((m, half), BF16)] * 2,
        compiler_params=params(),
        cost_estimate=cost(
            8 * m * feats * half, 8 * half * feats + 16 * m * feats, m * half
        ),
    )(core, *own, *other, up, up_other, down, down_other)


def input_pass(core, delta, delta_other, up, first, count):
    m, half = delta.shape
    tile = min(512, count)
    steps = count // tile
    base = first // tile
    keep = m // NX

    def kernel(core_ref, d_ref, d2_ref, up_ref, up2_ref, keep_ref, send_ref):
        total = lax.dot_general(
            d_ref[...], up_ref[...], NT, preferred_element_type=F32
        ) + lax.dot_general(d2_ref[...], up2_ref[...], NT, preferred_element_type=F32)
        keep_ref[...] = total[:keep]
        send_ref[...] = total[keep:].astype(BF16)

    rows = pl.BlockSpec((m, half), lambda i, c: (0, 0))
    return pl.pallas_call(
        kernel,
        grid_spec=pltpu.PrefetchScalarGridSpec(
            num_scalar_prefetch=1,
            grid=(steps,),
            in_specs=[
                rows,
                rows,
                pl.BlockSpec((tile, half), lambda i, c: (base + i, c[0])),
                pl.BlockSpec((tile, half), lambda i, c: (base + i, 1 - c[0])),
            ],
            out_specs=[
                pl.BlockSpec((keep, tile), lambda i, c: (0, i)),
                pl.BlockSpec((m - keep, tile), lambda i, c: (0, i)),
            ],
        ),
        out_shape=[
            jax.ShapeDtypeStruct((keep, count), F32),
            jax.ShapeDtypeStruct((m - keep, count), BF16),
        ],
        compiler_params=params(),
        cost_estimate=cost(4 * m * half * count, 4 * count * half + 4 * m * half),
    )(core, delta, delta_other, up, up)


def down_pass(core, acts, pieces, hidden, flip, into=None):
    parts, n = len(acts), len(pieces)
    m, half = acts[0].shape
    rows, feats = pieces[0].shape[1:]
    tile = min(512, half)
    steps = half // tile

    def kernel(core_ref, *refs):
        act = jnp.concatenate([r[...] for r in refs[:parts]], axis=0)
        cot = stacked(refs[parts : parts + n], 0)
        refs[-1][...] = lax.dot_general(
            act, cot, TN, preferred_element_type=F32
        ).astype(BF16)

    extra = [] if into is None else [into]

    def place(i, c):
        side = 1 - c[0] if flip else c[0]
        return (side * steps + i, 0)

    return pl.pallas_call(
        kernel,
        grid_spec=pltpu.PrefetchScalarGridSpec(
            num_scalar_prefetch=1,
            grid=(steps,),
            in_specs=[pl.BlockSpec((m, tile), lambda i, c: (0, i))] * parts
            + [pl.BlockSpec((1, rows, feats), lambda i, c: (1, 0, 0))] * n
            + [pl.BlockSpec(memory_space=pl.ANY)] * len(extra),
            out_specs=pl.BlockSpec((tile, feats), place),
        ),
        out_shape=jax.ShapeDtypeStruct((hidden, feats), BF16),
        input_output_aliases={1 + parts + n: 0} if extra else {},
        compiler_params=params(),
        cost_estimate=cost(
            2 * parts * m * half * feats, 2 * half * feats + 2 * parts * m * (half + feats)
        ),
    )(core, *acts, *pieces, *extra)


def up_pass(core, deltas, deltas_other, pieces, hidden):
    parts, n = len(deltas), len(pieces)
    m, half = deltas[0].shape
    rows, feats = pieces[0].shape[1:]
    tile = min(512, half)
    steps = half // tile

    def kernel(core_ref, *refs):
        tok = stacked(refs[2 * parts : 2 * parts + n], 0)

        def emit(these):
            delta = jnp.concatenate([r[...] for r in these], axis=0)
            refs[-1][...] = lax.dot_general(
                tok, delta, TN, preferred_element_type=F32
            ).astype(BF16)

        @pl.when(pl.program_id(0) < steps)
        def _():
            emit(refs[:parts])

        @pl.when(pl.program_id(0) >= steps)
        def _():
            emit(refs[parts : 2 * parts])

    def place(i, c):
        side = jnp.where(i < steps, c[0], 1 - c[0])
        return (0, side * steps + i % steps)

    return pl.pallas_call(
        kernel,
        grid_spec=pltpu.PrefetchScalarGridSpec(
            num_scalar_prefetch=1,
            grid=(2 * steps,),
            in_specs=[
                pl.BlockSpec((m, tile), lambda i, c: (0, jnp.minimum(i, steps - 1)))
            ]
            * parts
            + [pl.BlockSpec((m, tile), lambda i, c: (0, jnp.maximum(i - steps, 0)))]
            * parts
            + [pl.BlockSpec((1, rows, feats), lambda i, c: (0, 0, 0))] * n,
            out_specs=pl.BlockSpec((feats, tile), place),
        ),
        out_shape=jax.ShapeDtypeStruct((feats, hidden), BF16),
        compiler_params=params(),
        cost_estimate=cost(
            4 * parts * m * half * feats,
            4 * half * feats + 2 * parts * m * (2 * half + feats),
        ),
    )(core, *deltas, *deltas_other, *pieces)


def split_plan(row, tokens, up_weight, down_weight, cotangent):
    nz = row // NX
    mine, feats = tokens.shape
    hidden = up_weight.shape[1]
    half = hidden // 2
    core_at = lax.axis_index("col")
    core = core_at.astype(jnp.int32)[None]

    def swap(x):
        return lax.ppermute(x, "col", [(0, 1), (1, 0)])

    def across(x):
        return lax.ppermute(x, "row", [(r, r ^ 1) for r in range(row)])

    def shift(x, k):
        return lax.ppermute(
            x, "row", [(r, (r + k * NX) % row) for r in range(row)]
        )

    own_piece = jnp.stack([tokens, cotangent])
    order = [0] + [k for j in range(1, nz // 2 + 1) for k in sorted({j, nz - j})]
    chunks = [order[: nz // 2], order[nz // 2 :]]
    same = {k: own_piece if k == 0 else shift(own_piece, k) for k in order}
    facing = {k: across(same[k]) for k in order}

    other_half = (1 - core_at) * half
    up_other = swap(lax.dynamic_slice(up_weight, (0, other_half), (feats, half)))
    down_other = swap(lax.dynamic_slice(down_weight, (other_half, 0), (half, feats)))

    all_pieces, acts, acts2, deltas, deltas2 = [], [], [], [], []
    for ks in chunks:
        pieces = [same[k] for k in ks] + [facing[k] for k in ks]
        all_pieces += pieces
        act, delta = hidden_pass(
            core,
            pieces,
            [swap(p) for p in pieces],
            up_weight,
            up_other,
            down_weight,
            down_other,
        )
        deltas.append(delta)
        acts.append(act)
        deltas2.append(swap(delta))
        acts2.append(swap(act))

    grad_down = down_pass(core, acts, all_pieces, hidden, False)

    splits = 2
    width = feats // splits
    columns = [[None, []] for _ in range(splits)]
    for ks, delta, delta2 in zip(chunks, deltas, deltas2):
        for s in range(splits):
            kept, sent = input_pass(core, delta, delta2, up_weight, s * width, width)
            total = kept + across(sent).astype(F32)
            for at, k in enumerate(ks):
                block = total[at * mine : (at + 1) * mine]
                if k == 0:
                    columns[s][0] = block
                else:
                    columns[s][1].append(shift(block.astype(BF16), -k))

    grad_up = up_pass(core, deltas, deltas2, all_pieces, hidden)
    grad_down = down_pass(core, acts2, all_pieces, hidden, True, grad_down)
    done = []
    for first, rest in columns:
        for block in rest:
            first = first + block.astype(F32)
        done.append(first.astype(BF16))
    return (jnp.concatenate(done, axis=1), grad_up, grad_down)


def whole_plan(tokens, up_weight, down_weight, cotangent):
    gathered = functools.partial(lax.all_gather, axis_name="row", axis=0, tiled=True)
    panel_tokens, panel_cotangent = gathered(tokens), gathered(cotangent)
    pre_part = jnp.dot(panel_tokens, up_weight, preferred_element_type=F32)
    back_part = lax.dot_general(
        panel_cotangent, down_weight, NT, preferred_element_type=F32
    )
    preact, back_grad = lax.psum((pre_part, back_part), "col")
    activated, factor = gelu_parts(preact)
    activated = activated.astype(BF16)
    delta = (back_grad * factor).astype(BF16)
    grad_down = lax.dot_general(
        activated, panel_cotangent, TN, preferred_element_type=F32
    )
    grad_up = lax.dot_general(panel_tokens, delta, TN, preferred_element_type=F32)
    grad_input = lax.psum_scatter(
        lax.dot_general(delta, up_weight, NT, preferred_element_type=F32),
        "row",
        scatter_dimension=0,
        tiled=True,
    )
    return (grad_input.astype(BF16), grad_up.astype(BF16), grad_down.astype(BF16))


def solution(mesh):
    row, col = mesh.shape["row"], mesh.shape["col"]

    def per_device(tokens, up_weight, down_weight, cotangent):
        args = (tokens, up_weight, down_weight, cotangent)
        short = row == 8 and tokens.shape[0] % 16 == 0
        if col == 2 and short:
            return split_plan(row, *args)
        return whole_plan(*args)

    in_specs = (
        P(("groups", "row"), "col"),
        P("col", "row"),
        P("row", "col"),
        P(("groups", "row"), "col"),
    )
    out_specs = (
        P(("groups", "row"), "col"),
        P(("groups", "col"), "row"),
        P(("groups", "row"), "col"),
    )
    return jax.shard_map(
        per_device, mesh=mesh, in_specs=in_specs, out_specs=out_specs, check_vma=False
    )
```

time: 309 us -> 232 us (0.75)
  Pallas kernels: 0 us -> 91.4 us
  waiting for transfers between devices: 182 us -> 90.9 us
  matrix products: 77.8 us -> 0 us
  starting transfers between devices: 0.34 us -> 25.4 us
  between operations: 13.8 us -> 1.03 us
  other arithmetic: 10.5 us -> 1.13 us
    pallas_call x0 -> x9, Pallas kernels: none -> 91.4 us  [the longest x2 34.7 us: hidden_pass(): pl.pallas_call(kernel, grid_spec=pltpu.PrefetchScalarGridSpec(num_scalar_...]
    ppermute x0 -> x31, waiting for transfers between devices: none -> 90.9 us  [the longest x9 58.7 us: shift(): return lax.ppermute(x, 'row', [(r, (r + k * NX) % row) for r in range(row)])]
    all_gather x2 -> x0, waiting for transfers between devices: 88.3 us -> none  [the longest x1 53.4 us: per_device(): lax.all_gather(cotangent, 'row', axis=0, tiled=True)]
    dot_general x5 -> x0, matrix products: 77.8 us -> none  [the longest x2 33.8 us: transposed_times(): lax.dot_general(left, right, (((0,), (0,)), ((), ())), preferred_element_...]
    psum x1 -> x0, waiting for transfers between devices: 58.4 us -> none  [per_device(): preact, back_grad = lax.psum((pre_part, back_part), 'col')]
    reduce_scatter x1 -> x0, waiting for transfers between devices: 34.1 us -> none  [per_device(): lax.psum_scatter(times_transposed(delta, up_weight), 'row', scatter_dimen...]
    ppermute x0 -> x31, starting transfers between devices: none -> 25.4 us  [the longest x9 13.1 us: shift(): return lax.ppermute(x, 'row', [(r, (r + k * NX) % row) for r in range(row)])]
    unnamed x7 -> x54, local copies, waits for them, and re-layouts: 23.4 us -> 4.76 us
  transfers between devices with their start and end apart: 4 -> 31, of which waited for: 4 -> 9; matrix products, arithmetic and copies ran while one was open for 23% -> 4% of each run, Pallas kernels for 0% -> 39%
where the time goes in v1:
time: 232 us
  Pallas kernels  91.4 us (39%)
  waiting for transfers between devices  90.9 us (39%)
  starting transfers between devices  25.4 us (11%)
  local copies, waits for them, and re-layouts  21.8 us (9%)
    ppermute x9, waiting for transfers between devices, shift(): return lax.ppermute(x, 'row', [(r, (r + k * NX) % row) for r in range(row)])  58.7 us
    pallas_call x2, Pallas kernels, hidden_pass(): pl.pallas_call(kernel, grid_spec=pltpu.PrefetchScalarGridSpec(num_scalar_...  34.7 us
    ppermute x8, waiting for transfers between devices, across(): return lax.ppermute(x, 'row', [(r, r ^ 1) for r in range(row)])  32.2 us
    pallas_call x4, Pallas kernels, input_pass(): pl.pallas_call(kernel, grid_spec=pltpu.PrefetchScalarGridSpec(num_scalar_...  24.6 us
    pallas_call x2, Pallas kernels, down_pass(): pl.pallas_call(kernel, grid_spec=pltpu.PrefetchScalarGridSpec(num_scalar_...  16.7 us
    pallas_call x1, Pallas kernels, up_pass(): pl.pallas_call(kernel, grid_spec=pltpu.PrefetchScalarGridSpec(num_scalar_...  15.3 us
    ppermute x9, starting transfers between devices, shift(): return lax.ppermute(x, 'row', [(r, (r + k * NX) % row) for r in range(row)])  13.1 us
    ppermute x8, starting transfers between devices, across(): return lax.ppermute(x, 'row', [(r, r ^ 1) for r in range(row)])  9.14 us
  transfers between devices with their start and end apart: 31, of which 9 were waited for; matrix products, arithmetic and copies ran while one was open for 4% of the time, Pallas kernels for 39%

profile of v1, /device:TPU:0, one launch (start us, length us, event | category | flops | bytes accessed | tf_op | source)
XLA Modules:
  0.0 231.6 jit_solution(5203395759744351712)
XLA Ops:
  0.7 8.5 %constant_dynamic-slice_fusion.1 = bf16[2048,2048]{1,0:T(8,128)(2,1)} fusion(bf16[2048,4096]{1,0:T(8,128)(2,1)} %up2_ref.7, s32[]{:T(128)S(6)} %select_n.4), kind=kLoop, calls=%fused_computation.17 | loop fusion | bytes 16777220 | tf_op jit(solution)/shard_map/dynamic_slice | solution.py:245
  9.6 8.4 %constant_dynamic-slice_fusion = bf16[2048,2048]{1,0:T(8,128)(2,1)} fusion(bf16[4096,2048]{1,0:T(8,128)(2,1)} %refs_10_.3, s32[]{:T(128)S(6)} %select_n.4), kind=kLoop, calls=%fused_computation.16 | loop fusion | bytes 16777220 | tf_op jit(solution)/shard_map/dynamic_slice | solution.py:246
  18.2 5.1 %collective-permute-start.12 = (bf16[2,64,2048]{2,1,0:T(8,128)(2,1)S(1)}, bf16[2,64,2048]{2,1,0:T(8,128)(2,1)S(1)}, u32[]{:S(2)}, u32[]{:S(2)}) collective-permute-start(bf16[2,64,2048]{2,1,0:T(8,128)(2,1)S(1)} %pad_maximum_fusion.refs_0_.refs_4_.refs_2_), channel_id=1, source_target_pairs={{0,12},{2,14},{4,0},{6,2},{8,4},{10,6},{12,8},{14,10},{1,13},{3,15... | collective-permute-start | bytes 1572872 | tf_op jit(solution)/shard_map/ppermute | solution.py:234
  24.3 11.4 %collective-permute-done.12.refs_0_.refs_8_.refs_6_ = bf16[2,64,2048]{2,1,0:T(8,128)(2,1)S(1)} collective-permute-done((bf16[2,64,2048]{2,1,0:T(8,128)(2,1)S(1)}, bf16[2,64,2048]{2,1,0:T(8,128)(2,1)S(1)}, u32[]{:S(2)}, u32[]{:S(2)}) %collective-permute-start.12) | collective-permute-done | bytes 524320 | tf_op jit(solution)/shard_map/ppermute | solution.py:234
  37.2 31.1 %collective-permute-done.13.refs_1_.refs_9_.refs_7_ = bf16[2,64,2048]{2,1,0:T(8,128)(2,1)S(1)} collective-permute-done((bf16[2,64,2048]{2,1,0:T(8,128)(2,1)S(1)}, bf16[2,64,2048]{2,1,0:T(8,128)(2,1)S(1)}, u32[]{:S(2)}, u32[]{:S(2)}) %collective-permute-start.13) | collective-permute-done | bytes 524320 | tf_op jit(solution)/shard_map/ppermute | solution.py:234
  70.3 12.8 %collective-permute-done.14.refs_2_.refs_10_.refs_8_ = bf16[2,64,2048]{2,1,0:T(8,128)(2,1)S(1)} collective-permute-done((bf16[2,64,2048]{2,1,0:T(8,128)(2,1)S(1)}, bf16[2,64,2048]{2,1,0:T(8,128)(2,1)S(1)}, u32[]{:S(2)}, u32[]{:S(2)}) %collective-permute-start.14) | collective-permute-done | bytes 524320 | tf_op jit(solution)/shard_map/ppermute | solution.py:231
  83.1 9.3 %collective-permute-done.15.refs_3_.refs_11_.refs_9_ = bf16[2,64,2048]{2,1,0:T(8,128)(2,1)S(1)} collective-permute-done((bf16[2,64,2048]{2,1,0:T(8,128)(2,1)S(1)}, bf16[2,64,2048]{2,1,0:T(8,128)(2,1)S(1)}, u32[]{:S(2)}, u32[]{:S(2)}) %collective-permute-start.15) | collective-permute-done | bytes 524320 | tf_op jit(solution)/shard_map/ppermute | solution.py:231
  94.5 10.0 %collective-permute-done.2.refs_3_.refs_7_.refs_5_ = bf16[2,64,2048]{2,1,0:T(8,128)(2,1)S(1)} collective-permute-done((bf16[2,64,2048]{2,1,0:T(8,128)(2,1)S(1)}, bf16[2,64,2048]{2,1,0:T(8,128)(2,1)S(1)}, u32[]{:S(2)}, u32[]{:S(2)}) %collective-permute-start.2) | collective-permute-done | bytes 524320 | tf_op jit(solution)/shard_map/ppermute | solution.py:231
  105.8 17.4 %shard_map.69 = (bf16[256,2048]{1,0:T(8,128)(2,1)}, bf16[256,2048]{1,0:T(8,128)(2,1)}) custom-call(s32[1]{0:T(128)} %bitcast.core_ref, bf16[2,64,2048]{2,1,0:T(8,128)(2,1)} %copy-done.1, bf16[2,64,2048]{2,1,0:T(8,128)(2,1)} %copy-done.2, bf16[2,64,2048]{2,1,0:T(8,128)(2,1)} %copy-done.5, bf16[2,64,2048]{2,1,0:T(8,128)(2,1)} %copy-done.6, ...), custom_call_target="tpu_custom_call" | custom-call | flops 8589934592 | bytes 41943040 | tf_op jit(solution)/shard_map/pallas_call | solution.py:67
  124.6 17.3 %shard_map.67 = (bf16[256,2048]{1,0:T(8,128)(2,1)}, bf16[256,2048]{1,0:T(8,128)(2,1)}) custom-call(s32[1]{0:T(128)} %bitcast.core_ref, bf16[2,64,2048]{2,1,0:T(8,128)(2,1)} %copy-done, bf16[2,64,2048]{2,1,0:T(8,128)(2,1)} %copy-done.3, bf16[2,64,2048]{2,1,0:T(8,128)(2,1)} %copy-done.4, bf16[2,64,2048]{2,1,0:T(8,128)(2,1)} %copy-done.7, ...), custom_call_target="tpu_custom_call" | custom-call | flops 8589934592 | bytes 41943040 | tf_op jit(solution)/shard_map/pallas_call | solution.py:67
  142.9 8.4 %shard_map.74.refs_10_ = bf16[4096,2048]{1,0:T(8,128)(2,1)} custom-call(s32[1]{0:T(128)} %bitcast.core_ref, bf16[256,2048]{1,0:T(8,128)(2,1)} %get-tuple-element.25.refs_0_, bf16[256,2048]{1,0:T(8,128)(2,1)} %get-tuple-element.26.refs_1_, bf16[2,64,2048]{2,1,0:T(8,128)(2,1)} %copy-done, bf16[2,64,2048]{2,1,0:T(8,128)(2,1)} %copy-done.3, ...), custom_call_target="tpu_custom_call" | custom-call | flops 4294967296 | bytes 12582912 | tf_op jit(solution)/shard_map/pallas_call | solution.py:149
  152.2 6.1 %shard_map.70 = (f32[128,1024]{1,0:T(8,128)}, bf16[128,1024]{1,0:T(8,128)(2,1)}) custom-call(s32[1]{0:T(128)} %bitcast.core_ref, bf16[256,2048]{1,0:T(8,128)(2,1)} %get-tuple-element.18.d_ref.refs_1_, bf16[256,2048]{1,0:T(8,128)(2,1)} %copy-done.8, bf16[2048,4096]{1,0:T(8,128)(2,1)} %up2_ref.7, bf16[2048,4096]{1,0:T(8,128)(2,1)} %up2_ref.7), custom_call_target="tpu_custom_call" | custom-call | flops 2147483648 | bytes 10485760 | tf_op jit(solution)/shard_map/pallas_call | solution.py:104
  158.4 1.5 collective-permute-start.21
  160.9 6.2 %shard_map.68 = (f32[128,1024]{1,0:T(8,128)}, bf16[128,1024]{1,0:T(8,128)(2,1)}) custom-call(s32[1]{0:T(128)} %bitcast.core_ref, bf16[256,2048]{1,0:T(8,128)(2,1)} %get-tuple-element.15.d_ref.refs_0_, bf16[256,2048]{1,0:T(8,128)(2,1)} %copy-done.9, bf16[2048,4096]{1,0:T(8,128)(2,1)} %up2_ref.7, bf16[2048,4096]{1,0:T(8,128)(2,1)} %up2_ref.7), custom_call_target="tpu_custom_call" | custom-call | flops 2147483648 | bytes 10485760 | tf_op jit(solution)/shard_map/pallas_call | solution.py:104
  167.6 6.2 %shard_map.72 = (f32[128,1024]{1,0:T(8,128)}, bf16[128,1024]{1,0:T(8,128)(2,1)}) custom-call(s32[1]{0:T(128)} %bitcast.core_ref, bf16[256,2048]{1,0:T(8,128)(2,1)} %get-tuple-element.18.d_ref.refs_1_, bf16[256,2048]{1,0:T(8,128)(2,1)} %copy-done.8, bf16[2048,4096]{1,0:T(8,128)(2,1)} %up2_ref.7, bf16[2048,4096]{1,0:T(8,128)(2,1)} %up2_ref.7), custom_call_target="tpu_custom_call" | custom-call | flops 2147483648 | bytes 10485760 | tf_op jit(solution)/shard_map/pallas_call | solution.py:104
  173.8 1.5 collective-permute-start.26
  175.3 6.1 %shard_map.71 = (f32[128,1024]{1,0:T(8,128)}, bf16[128,1024]{1,0:T(8,128)(2,1)}) custom-call(s32[1]{0:T(128)} %bitcast.core_ref, bf16[256,2048]{1,0:T(8,128)(2,1)} %get-tuple-element.15.d_ref.refs_0_, bf16[256,2048]{1,0:T(8,128)(2,1)} %copy-done.9, bf16[2048,4096]{1,0:T(8,128)(2,1)} %up2_ref.7, bf16[2048,4096]{1,0:T(8,128)(2,1)} %up2_ref.7), custom_call_target="tpu_custom_call" | custom-call | flops 2147483648 | bytes 10485760 | tf_op jit(solution)/shard_map/pallas_call | solution.py:104
  181.4 15.3 %shard_map.73 = bf16[2048,4096]{1,0:T(8,128)(2,1)} custom-call(s32[1]{0:T(128)} %bitcast.core_ref, bf16[256,2048]{1,0:T(8,128)(2,1)} %get-tuple-element.15.d_ref.refs_0_, bf16[256,2048]{1,0:T(8,128)(2,1)} %get-tuple-element.18.d_ref.refs_1_, bf16[256,2048]{1,0:T(8,128)(2,1)} %copy-done.9, bf16[256,2048]{1,0:T(8,128)(2,1)} %copy-done.8, ...), custom_call_target="tpu_custom_call" | custom-call | flops 8589934592 | bytes 23068672 | tf_op jit(solution)/shard_map/pallas_call | solution.py:196
  198.8 8.4 %shard_map.75 = bf16[4096,2048]{1,0:T(8,128)(2,1)} custom-call(s32[1]{0:T(128)} %bitcast.core_ref, bf16[256,2048]{1,0:T(8,128)(2,1)} %copy-done.12, bf16[256,2048]{1,0:T(8,128)(2,1)} %copy-done.11, bf16[2,64,2048]{2,1,0:T(8,128)(2,1)} %copy-done, bf16[2,64,2048]{2,1,0:T(8,128)(2,1)} %copy-done.3, ...), custom_call_target="tpu_custom_call", output_to_operand_aliasing={{}: (11, {})} | custom-call | flops 4294967296 | bytes 12582912 | tf_op jit(solution)/shard_map/pallas_call | solution.py:149
  207.5 3.8 %collective-permute-start.11 = (bf16[64,1024]{1,0:T(8,128)(2,1)S(1)}, bf16[64,1024]{1,0:T(8,128)(2,1)S(1)}, u32[]{:S(2)}, u32[]{:S(2)}) collective-permute-start(bf16[64,1024]{1,0:T(8,128)(2,1)S(1)} %slice.63), channel_id=1, source_target_pairs={{0,12},{2,14},{4,0},{6,2},{8,4},{10,6},{12,8},{14,10},{1,13},{3,15... | collective-permute-start | bytes 393224 | tf_op jit(solution)/shard_map/ppermute | solution.py:234
  212.0 1.5 collective-permute-start.28
  213.6 2.0 collective-permute-done.22
  216.5 7.1 %collective-permute-done.23 = bf16[64,1024]{1,0:T(8,128)(2,1)S(1)} collective-permute-done((bf16[64,1024]{1,0:T(8,128)(2,1)S(1)}, bf16[64,1024]{1,0:T(8,128)(2,1)S(1)}, u32[]{:S(2)}, u32[]{:S(2)}) %collective-permute-start.23) | collective-permute-done | bytes 131104 | tf_op jit(solution)/shard_map/ppermute | solution.py:234
  223.9 6.9 %collective-permute-done.28 = bf16[64,1024]{1,0:T(8,128)(2,1)S(1)} collective-permute-done((bf16[64,1024]{1,0:T(8,128)(2,1)S(1)}, bf16[64,1024]{1,0:T(8,128)(2,1)S(1)}, u32[]{:S(2)}, u32[]{:S(2)}) %collective-permute-start.28) | collective-permute-done | bytes 131104 | tf_op jit(solution)/shard_map/ppermute | solution.py:234
  (115 shorter events, 18.2 us)
Async XLA Ops:
  9.2 96.0 %collective-permute-start.7 = (bf16[2048,2048]{1,0:T(8,128)(2,1)}, bf16[2048,2048]{1,0:T(8,128)(2,1)}, u32[]{:S(2)}, u32[]{:S(2)}) collective-permute-start(bf16[2048,2048]{1,0:T(8,128)(2,1)} %constant_dynamic-slice_fusion.1), channel_id=1, source_target_pairs={{0,1},{1,0},{2,3},{3,2},{4,5},{5,4},{6,7},{7,6},{8,9},{9,8},{10,11... | collective-permute-start | bytes 25165832 | tf_op jit(solution)/shard_map/ppermute | solution.py:228
  18.1 87.5 %collective-permute-start.8 = (bf16[2048,2048]{1,0:T(8,128)(2,1)}, bf16[2048,2048]{1,0:T(8,128)(2,1)}, u32[]{:S(2)}, u32[]{:S(2)}) collective-permute-start(bf16[2048,2048]{1,0:T(8,128)(2,1)} %constant_dynamic-slice_fusion), channel_id=1, source_target_pairs={{0,1},{1,0},{2,3},{3,2},{4,5},{5,4},{6,7},{7,6},{8,9},{9,8},{10,11... | collective-permute-start | bytes 25165832 | tf_op jit(solution)/shard_map/ppermute | solution.py:228
  18.2 17.5 %collective-permute-start.12 = (bf16[2,64,2048]{2,1,0:T(8,128)(2,1)S(1)}, bf16[2,64,2048]{2,1,0:T(8,128)(2,1)S(1)}, u32[]{:S(2)}, u32[]{:S(2)}) collective-permute-start(bf16[2,64,2048]{2,1,0:T(8,128)(2,1)S(1)} %pad_maximum_fusion.refs_0_.refs_4_.refs_2_), channel_id=1, source_target_pairs={{0,12},{2,14},{4,0},{6,2},{8,4},{10,6},{12,8},{14,10},{1,13},{3,15... | collective-permute-start | bytes 1572872 | tf_op jit(solution)/shard_map/ppermute | solution.py:234
  23.3 45.0 %collective-permute-start.13 = (bf16[2,64,2048]{2,1,0:T(8,128)(2,1)S(1)}, bf16[2,64,2048]{2,1,0:T(8,128)(2,1)S(1)}, u32[]{:S(2)}, u32[]{:S(2)}) collective-permute-start(bf16[2,64,2048]{2,1,0:T(8,128)(2,1)S(1)} %pad_maximum_fusion.refs_0_.refs_4_.refs_2_), channel_id=1, source_target_pairs={{0,8},{2,10},{4,12},{6,14},{8,0},{10,2},{12,4},{14,6},{1,9},{3,11}... | collective-permute-start | bytes 1572872 | tf_op jit(solution)/shard_map/ppermute | solution.py:234
  23.3 46.4 %collective-permute-start = (bf16[2,64,2048]{2,1,0:T(8,128)(2,1)S(1)}, bf16[2,64,2048]{2,1,0:T(8,128)(2,1)S(1)}, u32[]{:S(2)}, u32[]{:S(2)}) collective-permute-start(bf16[2,64,2048]{2,1,0:T(8,128)(2,1)S(1)} %pad_maximum_fusion.refs_0_.refs_4_.refs_2_), channel_id=1, source_target_pairs={{0,4},{2,6},{4,8},{6,10},{8,12},{10,14},{12,0},{14,2},{1,5},{3,7},... | collective-permute-start | bytes 1572872 | tf_op jit(solution)/shard_map/ppermute | solution.py:234
  35.7 34.6 %collective-permute-start.1 = (bf16[2,64,2048]{2,1,0:T(8,128)(2,1)S(1)}, bf16[2,64,2048]{2,1,0:T(8,128)(2,1)S(1)}, u32[]{:S(2)}, u32[]{:S(2)}) collective-permute-start(bf16[2,64,2048]{2,1,0:T(8,128)(2,1)S(1)} %pad_maximum_fusion.refs_0_.refs_4_.refs_2_), channel_id=1, source_target_pairs={{0,2},{2,0},{4,6},{6,4},{8,10},{10,8},{12,14},{14,12},{1,3},{3,1},... | collective-permute-start | bytes 1572872 | tf_op jit(solution)/shard_map/ppermute | solution.py:231
  69.7 22.7 %collective-permute-start.15 = (bf16[2,64,2048]{2,1,0:T(8,128)(2,1)S(1)}, bf16[2,64,2048]{2,1,0:T(8,128)(2,1)S(1)}, u32[]{:S(2)}, u32[]{:S(2)}) collective-permute-start(bf16[2,64,2048]{2,1,0:T(8,128)(2,1)S(1)} %collective-permute-done.13.refs_1_.refs_9_.refs_7_), channel_id=1, source_target_pairs={{0,2},{2,0},{4,6},{6,4},{8,10},{10,8},{12,14},{14,12},{1,3},{3,1},... | collective-permute-start | bytes 1572872 | tf_op jit(solution)/shard_map/ppermute | solution.py:231
  70.3 23.7 %collective-permute-start.16 = (bf16[2,64,2048]{2,1,0:T(8,128)(2,1)S(1)}, bf16[2,64,2048]{2,1,0:T(8,128)(2,1)S(1)}, u32[]{:S(2)}, u32[]{:S(2)}) collective-permute-start(bf16[2,64,2048]{2,1,0:T(8,128)(2,1)S(1)} %collective-permute-done.12.refs_0_.refs_8_.refs_6_), channel_id=1, source_target_pairs={{0,1},{1,0},{2,3},{3,2},{4,5},{5,4},{6,7},{7,6},{8,9},{9,8},{10,11... | collective-permute-start | bytes 1572872 | tf_op jit(solution)/shard_map/ppermute | solution.py:228
  104.5 19.0 %collective-permute-start.3 = (bf16[2,64,2048]{2,1,0:T(8,128)(2,1)S(1)}, bf16[2,64,2048]{2,1,0:T(8,128)(2,1)S(1)}, u32[]{:S(2)}, u32[]{:S(2)}) collective-permute-start(bf16[2,64,2048]{2,1,0:T(8,128)(2,1)S(1)} %pad_maximum_fusion.refs_0_.refs_4_.refs_2_), channel_id=1, source_target_pairs={{0,1},{1,0},{2,3},{3,2},{4,5},{5,4},{6,7},{7,6},{8,9},{9,8},{10,11... | collective-permute-start | bytes 1572872 | tf_op jit(solution)/shard_map/ppermute | solution.py:228
  104.5 19.0 %collective-permute-start.4 = (bf16[2,64,2048]{2,1,0:T(8,128)(2,1)S(1)}, bf16[2,64,2048]{2,1,0:T(8,128)(2,1)S(1)}, u32[]{:S(2)}, u32[]{:S(2)}) collective-permute-start(bf16[2,64,2048]{2,1,0:T(8,128)(2,1)S(1)} %collective-permute-done.refs_1_.refs_5_.refs_3_), channel_id=1, source_target_pairs={{0,1},{1,0},{2,3},{3,2},{4,5},{5,4},{6,7},{7,6},{8,9},{9,8},{10,11... | collective-permute-start | bytes 1572872 | tf_op jit(solution)/shard_map/ppermute | solution.py:228
  105.0 18.5 %collective-permute-start.5 = (bf16[2,64,2048]{2,1,0:T(8,128)(2,1)S(1)}, bf16[2,64,2048]{2,1,0:T(8,128)(2,1)S(1)}, u32[]{:S(2)}, u32[]{:S(2)}) collective-permute-start(bf16[2,64,2048]{2,1,0:T(8,128)(2,1)S(1)} %collective-permute-done.1.refs_2_.refs_6_.refs_4_), channel_id=1, source_target_pairs={{0,1},{1,0},{2,3},{3,2},{4,5},{5,4},{6,7},{7,6},{8,9},{9,8},{10,11... | collective-permute-start | bytes 1572872 | tf_op jit(solution)/shard_map/ppermute | solution.py:228
  105.1 18.4 %collective-permute-start.6 = (bf16[2,64,2048]{2,1,0:T(8,128)(2,1)S(1)}, bf16[2,64,2048]{2,1,0:T(8,128)(2,1)}, u32[]{:S(2)}, u32[]{:S(2)}) collective-permute-start(bf16[2,64,2048]{2,1,0:T(8,128)(2,1)S(1)} %collective-permute-done.2.refs_3_.refs_7_.refs_5_), channel_id=1, source_target_pairs={{0,1},{1,0},{2,3},{3,2},{4,5},{5,4},{6,7},{7,6},{8,9},{9,8},{10,11... | collective-permute-start | bytes 1572872 | tf_op jit(solution)/shard_map/ppermute | solution.py:228
  123.2 28.0 %collective-permute-start.20 = (bf16[256,2048]{1,0:T(8,128)(2,1)}, bf16[256,2048]{1,0:T(8,128)(2,1)S(1)}, u32[]{:S(2)}, u32[]{:S(2)}) collective-permute-start(bf16[256,2048]{1,0:T(8,128)(2,1)} %get-tuple-element.18.d_ref.refs_1_), channel_id=1, source_target_pairs={{0,1},{1,0},{2,3},{3,2},{4,5},{5,4},{6,7},{7,6},{8,9},{9,8},{10,11... | collective-permute-start | bytes 3145736 | tf_op jit(solution)/shard_map/ppermute | solution.py:228
  142.0 17.9 %collective-permute-start.9 = (bf16[256,2048]{1,0:T(8,128)(2,1)}, bf16[256,2048]{1,0:T(8,128)(2,1)S(1)}, u32[]{:S(2)}, u32[]{:S(2)}) collective-permute-start(bf16[256,2048]{1,0:T(8,128)(2,1)} %get-tuple-element.15.d_ref.refs_0_), channel_id=1, source_target_pairs={{0,1},{1,0},{2,3},{3,2},{4,5},{5,4},{6,7},{7,6},{8,9},{9,8},{10,11... | collective-permute-start | bytes 3145736 | tf_op jit(solution)/shard_map/ppermute | solution.py:228
  142.3 54.4 %collective-permute-start.30 = (bf16[256,2048]{1,0:T(8,128)(2,1)S(1)}, bf16[256,2048]{1,0:T(8,128)(2,1)S(1)}, u32[]{:S(2)}, u32[]{:S(2)}) collective-permute-start(bf16[256,2048]{1,0:T(8,128)(2,1)S(1)} %copy-done.10), channel_id=1, source_target_pairs={{0,1},{1,0},{2,3},{3,2},{4,5},{5,4},{6,7},{7,6},{8,9},{9,8},{10,11... | collective-permute-start | bytes 3145736 | tf_op jit(solution)/shard_map/ppermute | solution.py:228
  142.5 54.9 %collective-permute-start.29 = (bf16[256,2048]{1,0:T(8,128)(2,1)}, bf16[256,2048]{1,0:T(8,128)(2,1)S(1)}, u32[]{:S(2)}, u32[]{:S(2)}) collective-permute-start(bf16[256,2048]{1,0:T(8,128)(2,1)} %get-tuple-element.25.refs_0_), channel_id=1, source_target_pairs={{0,1},{1,0},{2,3},{3,2},{4,5},{5,4},{6,7},{7,6},{8,9},{9,8},{10,11... | collective-permute-start | bytes 3145736 | tf_op jit(solution)/shard_map/ppermute | solution.py:228
  158.4 48.7 %collective-permute-start.21 = (bf16[128,1024]{1,0:T(8,128)(2,1)}, bf16[128,1024]{1,0:T(8,128)(2,1)S(1)}, u32[]{:S(2)}, u32[]{:S(2)}) collective-permute-start(bf16[128,1024]{1,0:T(8,128)(2,1)} %get-tuple-element.20), channel_id=1, source_target_pairs={{0,2},{2,0},{4,6},{6,4},{8,10},{10,8},{12,14},{14,12},{1,3},{3,1},... | collective-permute-start | bytes 786440 | tf_op jit(solution)/shard_map/ppermute | solution.py:231
  167.0 40.3 %collective-permute-start.10 = (bf16[128,1024]{1,0:T(8,128)(2,1)}, bf16[128,1024]{1,0:T(8,128)(2,1)S(1)}, u32[]{:S(2)}, u32[]{:S(2)}) collective-permute-start(bf16[128,1024]{1,0:T(8,128)(2,1)} %get-tuple-element.17), channel_id=1, source_target_pairs={{0,2},{2,0},{4,6},{6,4},{8,10},{10,8},{12,14},{14,12},{1,3},{3,1},... | collective-permute-start | bytes 786440 | tf_op jit(solution)/shard_map/ppermute | solution.py:231
  173.8 37.5 %collective-permute-start.26 = (bf16[128,1024]{1,0:T(8,128)(2,1)}, bf16[128,1024]{1,0:T(8,128)(2,1)S(1)}, u32[]{:S(2)}, u32[]{:S(2)}) collective-permute-start(bf16[128,1024]{1,0:T(8,128)(2,1)} %get-tuple-element.24), channel_id=1, source_target_pairs={{0,2},{2,0},{4,6},{6,4},{8,10},{10,8},{12,14},{14,12},{1,3},{3,1},... | collective-permute-start | bytes 786440 | tf_op jit(solution)/shard_map/ppermute | solution.py:231
  196.8 15.2 %collective-permute-start.24 = (bf16[128,1024]{1,0:T(8,128)(2,1)S(1)}, bf16[128,1024]{1,0:T(8,128)(2,1)S(1)}, u32[]{:S(2)}, u32[]{:S(2)}) collective-permute-start(bf16[128,1024]{1,0:T(8,128)(2,1)S(1)} %copy-done.26), channel_id=1, source_target_pairs={{0,2},{2,0},{4,6},{6,4},{8,10},{10,8},{12,14},{14,12},{1,3},{3,1},... | collective-permute-start | bytes 786440 | tf_op jit(solution)/shard_map/ppermute | solution.py:231
  207.3 16.3 %collective-permute-start.23 = (bf16[64,1024]{1,0:T(8,128)(2,1)S(1)}, bf16[64,1024]{1,0:T(8,128)(2,1)S(1)}, u32[]{:S(2)}, u32[]{:S(2)}) collective-permute-start(bf16[64,1024]{1,0:T(8,128)(2,1)S(1)} %get-tuple-element.28), channel_id=1, source_target_pairs={{0,8},{2,10},{4,12},{6,14},{8,0},{10,2},{12,4},{14,6},{1,9},{3,11}... | collective-permute-start | bytes 393224 | tf_op jit(solution)/shard_map/ppermute | solution.py:234
  207.5 16.2 %collective-permute-start.11 = (bf16[64,1024]{1,0:T(8,128)(2,1)S(1)}, bf16[64,1024]{1,0:T(8,128)(2,1)S(1)}, u32[]{:S(2)}, u32[]{:S(2)}) collective-permute-start(bf16[64,1024]{1,0:T(8,128)(2,1)S(1)} %slice.63), channel_id=1, source_target_pairs={{0,12},{2,14},{4,0},{6,2},{8,4},{10,6},{12,8},{14,10},{1,13},{3,15... | collective-permute-start | bytes 393224 | tf_op jit(solution)/shard_map/ppermute | solution.py:234
  212.0 18.8 %collective-permute-start.28 = (bf16[64,1024]{1,0:T(8,128)(2,1)S(1)}, bf16[64,1024]{1,0:T(8,128)(2,1)S(1)}, u32[]{:S(2)}, u32[]{:S(2)}) collective-permute-start(bf16[64,1024]{1,0:T(8,128)(2,1)S(1)} %get-tuple-element.30), channel_id=1, source_target_pairs={{0,8},{2,10},{4,12},{6,14},{8,0},{10,2},{12,4},{14,6},{1,9},{3,11}... | collective-permute-start | bytes 393224 | tf_op jit(solution)/shard_map/ppermute | solution.py:234
  215.6 15.2 %collective-permute-start.25 = (bf16[64,1024]{1,0:T(8,128)(2,1)S(1)}, bf16[64,1024]{1,0:T(8,128)(2,1)S(1)}, u32[]{:S(2)}, u32[]{:S(2)}) collective-permute-start(bf16[64,1024]{1,0:T(8,128)(2,1)S(1)} %slice.62), channel_id=1, source_target_pairs={{0,12},{2,14},{4,0},{6,2},{8,4},{10,6},{12,8},{14,10},{1,13},{3,15... | collective-permute-start | bytes 393224 | tf_op jit(solution)/shard_map/ppermute | solution.py:234
  (34 other events, 606.9 us)

commit v2 on v0

v2 whole, which is shorter than its diff:
```python
import functools

import jax
import jax.numpy as jnp
from jax import lax
from jax.experimental import pallas as pl
from jax.experimental.pallas import tpu as pltpu
from jax.sharding import PartitionSpec as P

F32 = jnp.float32
BF16 = jnp.bfloat16
VMEM_LIMIT = 36 * 1024 * 1024
NX = 2
PARTS = 2
SPLITS = 2
Z_AHEAD = 3
X_AHEAD = 2
PRE_TILE = 1024
BACK_TILE = 1024
IN_TILE = 256
NT = (((1,), (1,)), ((), ()))
TN = (((0,), (0,)), ((), ()))


def gelu_parts(preact):
    square = preact * preact
    curve_term = jnp.tanh(preact * (0.7978845608 + (0.7978845608 * 0.044715) * square))
    gate = 0.5 + 0.5 * curve_term
    slope = 0.5 * 0.7978845608 + (1.5 * 0.044715 * 0.7978845608) * square
    factor = gate + preact * (1.0 - curve_term * curve_term) * slope
    return (preact * gate, factor)


def params():
    return pltpu.CompilerParams(vmem_limit_bytes=VMEM_LIMIT)


def cost(flops, moved, transcendentals=0):
    return pl.CostEstimate(
        flops=flops // 20, bytes_accessed=moved // 20, transcendentals=0
    )


def joined(refs):
    return jnp.concatenate([r[...] for r in refs], axis=0)


def call(kernel, steps, in_specs, out_specs, out_shape, estimate, args, scratch=()):
    return pl.pallas_call(
        kernel,
        grid=(steps,),
        in_specs=in_specs,
        out_specs=out_specs,
        out_shape=out_shape,
        scratch_shapes=list(scratch),
        compiler_params=params(),
        cost_estimate=estimate,
    )(*args)


def whole(x):
    return pl.BlockSpec(x.shape, lambda i: (0, 0))


def pre_pass(tokens, up, first, hidden):
    n = len(tokens)
    rows, feats = tokens[0].shape
    m = n * rows
    tile = min(PRE_TILE, hidden)
    base = first // tile

    def kernel(*refs):
        up_ref, out_ref = refs[n:]
        out_ref[...] = jnp.dot(
            joined(refs[:n]), up_ref[...], preferred_element_type=F32
        ).astype(BF16)

    return call(
        kernel,
        hidden // tile,
        [whole(t) for t in tokens]
        + [pl.BlockSpec((feats, tile), lambda i: (0, base + i))],
        pl.BlockSpec((m, tile), lambda i: (0, i)),
        jax.ShapeDtypeStruct((m, hidden), BF16),
        cost(2 * m * feats * hidden, 2 * feats * hidden + m * (2 * feats + 2 * hidden)),
        (*tokens, up),
    )


def back_pass(cots, down, pre, pre_other, first):
    n = len(cots)
    rows, feats = cots[0].shape
    m, hidden = pre.shape
    tile = min(BACK_TILE, hidden)
    base = first // tile

    def kernel(*refs):
        down_ref, pre_ref, pre2_ref, act_ref, delta_ref = refs[n:]
        back = lax.dot_general(
            joined(refs[:n]), down_ref[...], NT, preferred_element_type=F32
        )
        activated, factor = gelu_parts(
            pre_ref[...].astype(F32) + pre2_ref[...].astype(F32)
        )
        act_ref[...] = activated.astype(BF16)
        delta_ref[...] = (back * factor).astype(BF16)

    column = pl.BlockSpec((m, tile), lambda i: (0, i))
    return call(
        kernel,
        hidden // tile,
        [whole(c) for c in cots]
        + [pl.BlockSpec((tile, feats), lambda i: (base + i, 0)), column, column],
        [column, column],
        [jax.ShapeDtypeStruct((m, hidden), BF16)] * 2,
        cost(
            2 * m * feats * hidden,
            2 * feats * hidden + m * (2 * feats + 8 * hidden),
            m * hidden,
        ),
        (*cots, down, pre, pre_other),
    )


def summed(left, right):
    return (left.astype(F32) + right.astype(F32)).astype(BF16)


def input_pass(deltas, up, first, count):
    parts = len(deltas) // 2
    m, each = deltas[0].shape
    hidden = max(parts, 1) * each
    tile = min(IN_TILE, count)
    base = first // tile
    keep = m // NX

    def kernel(*refs):
        up_ref, keep_ref, send_ref = refs[len(deltas) : len(deltas) + 3]
        if parts:
            total_ref = refs[-1]

            @pl.when(pl.program_id(0) == 0)
            def _():
                for p in range(parts):
                    total_ref[:, p * each : (p + 1) * each] = summed(
                        refs[p][...], refs[parts + p][...]
                    )

        else:
            total_ref = refs[0]
        out = lax.dot_general(
            total_ref[...], up_ref[...], NT, preferred_element_type=F32
        )
        keep_ref[...] = out[:keep]
        send_ref[...] = out[keep:].astype(BF16)

    out_specs = [
        pl.BlockSpec((keep, tile), lambda i: (0, i)),
        pl.BlockSpec((m - keep, tile), lambda i: (0, i)),
    ]
    out_shape = [
        jax.ShapeDtypeStruct((keep, count), F32),
        jax.ShapeDtypeStruct((m - keep, count), BF16),
    ]
    if parts:
        out_specs.append(pl.BlockSpec((m, hidden), lambda i: (0, 0)))
        out_shape.append(jax.ShapeDtypeStruct((m, hidden), BF16))
    got = call(
        kernel,
        count // tile,
        [whole(d) for d in deltas]
        + [pl.BlockSpec((tile, hidden), lambda i: (base + i, 0))],
        out_specs,
        out_shape,
        cost(2 * m * hidden * count, 2 * count * hidden + 4 * m * hidden),
        (*deltas, up),
    )
    return got if parts else (*got, deltas[0])


def down_pass(act, cots, part, parts, into=None):
    n = len(cots)
    m, each = act.shape
    rows, feats = cots[0].shape
    tile = min(512, each)
    steps = each // tile
    extra = [] if into is None else [into]

    def kernel(*refs):
        refs[-1][...] = lax.dot_general(
            refs[0][...], joined(refs[1 : 1 + n]), TN, preferred_element_type=F32
        ).astype(BF16)

    return pl.pallas_call(
        kernel,
        grid=(steps,),
        in_specs=[pl.BlockSpec((m, tile), lambda i: (0, i))]
        + [whole(c) for c in cots]
        + [pl.BlockSpec(memory_space=pl.ANY)] * len(extra),
        out_specs=pl.BlockSpec((tile, feats), lambda i: (part * steps + i, 0)),
        out_shape=jax.ShapeDtypeStruct((parts * each, feats), BF16),
        input_output_aliases={1 + n: 0} if extra else {},
        compiler_params=params(),
        cost_estimate=cost(
            2 * m * each * feats, 2 * each * feats + 2 * m * (each + feats)
        ),
    )(act, *cots, *extra)


def up_pass(delta, tokens, part, parts, into=None):
    n = len(tokens)
    m, hidden = delta.shape
    rows, feats = tokens[0].shape
    each = hidden // parts
    tile = min(512, each)
    steps = each // tile
    extra = [] if into is None else [into]

    def kernel(*refs):
        refs[-1][...] = lax.dot_general(
            joined(refs[1 : 1 + n]), refs[0][...], TN, preferred_element_type=F32
        ).astype(BF16)

    return pl.pallas_call(
        kernel,
        grid=(steps,),
        in_specs=[pl.BlockSpec((m, tile), lambda i: (0, part * steps + i))]
        + [whole(t) for t in tokens]
        + [pl.BlockSpec(memory_space=pl.ANY)] * len(extra),
        out_specs=pl.BlockSpec((feats, tile), lambda i: (0, part * steps + i)),
        out_shape=jax.ShapeDtypeStruct((feats, hidden), BF16),
        input_output_aliases={1 + n: 0} if extra else {},
        compiler_params=params(),
        cost_estimate=cost(
            2 * m * each * feats, 2 * each * feats + 2 * m * (each + feats)
        ),
    )(delta, *tokens, *extra)


def tied(x, *after):
    return lax.optimization_barrier((x,) + after)[0] if after else x


def split_plan(row, tokens, up_weight, down_weight, cotangent):
    nz = row // NX
    mine, feats = tokens.shape

    def swap(x):
        return lax.ppermute(x, "col", [(0, 1), (1, 0)])

    def across(x):
        return lax.ppermute(x, "row", [(r, r ^ 1) for r in range(row)])

    def shift(x, k):
        return lax.ppermute(x, "row", [(r, (r + k * NX) % row) for r in range(row)])

    order = [0] + [k for j in range(1, nz // 2 + 1) for k in sorted({j, nz - j})]
    near, far = order[1:-1], order[-1]
    same = {("t", 0): tokens, ("c", 0): cotangent}
    facing, sent, crossed = {}, [], []
    for name, block, ks in (
        ("t", tokens, near + [far]),
        ("c", cotangent, near + [far]),
    ):
        for k in ks:
            tie = sent[-Z_AHEAD:][:1] if len(sent) >= Z_AHEAD else ()
            same[name, k] = shift(tied(block, *tie), k)
            sent.append(same[name, k])
    queue = [("t", 0), ("t", near[0]), ("c", 0)]
    queue += [("t", k) for k in near[1:] + [far]]
    queue += [("c", k) for k in near + [far]]
    for at in queue:
        tie = crossed[-X_AHEAD:][:1] if len(crossed) >= X_AHEAD else ()
        facing[at] = across(tied(same[at], *tie))
        crossed.append(facing[at])

    def pieces(name):
        return [same[name, k] for k in order] + [facing[name, k] for k in order]

    def after(blocks, *events):
        return [tied(blocks[0], *events)] + list(blocks[1:])

    hidden = up_weight.shape[1]
    each = hidden // 2
    all_tokens, all_cots = pieces("t"), pieces("c")
    pre0 = pre_pass(all_tokens, up_weight, 0, each)
    events = [pre0] + sent[len(near) + 1 :] + crossed[-1 - len(near) : -1]
    pre1 = pre_pass(after(all_tokens, *events), up_weight, each, each)
    other0, other1 = swap(pre0), swap(pre1)
    act0, delta0 = back_pass(after(all_cots, pre1), down_weight, pre0, other0, 0)
    act1, delta1 = back_pass(after(all_cots, delta0), down_weight, pre1, other1, each)
    deltas = [delta0, delta1, swap(delta0), swap(delta1)]
    grad_down = down_pass(tied(act0, delta1), all_cots, 0, 2)

    width = feats // SPLITS
    kepts, gones = [], []
    last = grad_down
    for s in range(SPLITS):
        kept, gone, delta = input_pass(
            after(deltas, last), up_weight, s * width, width
        )
        deltas, last = [delta], kept
        kepts.append(kept)
        gones.append(across(gone))
    grad_down = down_pass(tied(act1, last), all_cots, 1, 2, grad_down)
    last = grad_down
    grad_up = None
    columns = []
    for s in range(SPLITS):
        kept, gone, _ = lax.optimization_barrier((kepts[s], gones[s], last))
        total = kept + gone.astype(F32)
        blocks = [total[at * mine : (at + 1) * mine] for at in range(nz)]
        sends = [b.astype(BF16) for b in blocks[1:]]
        columns.append((blocks[0], [shift(b, -k) for k, b in zip(order[1:], sends)]))
        grad_up = up_pass(tied(delta, *sends), all_tokens, s, SPLITS, grad_up)
        last = grad_up
    done = []
    for first, rest in columns:
        for block in rest:
            first = first + block.astype(F32)
        done.append(first.astype(BF16))
    return (jnp.concatenate(done, axis=1), grad_up, grad_down)


def whole_plan(tokens, up_weight, down_weight, cotangent):
    gathered = functools.partial(lax.all_gather, axis_name="row", axis=0, tiled=True)
    panel_tokens, panel_cotangent = gathered(tokens), gathered(cotangent)
    pre_part = jnp.dot(panel_tokens, up_weight, preferred_element_type=F32)
    back_part = lax.dot_general(
        panel_cotangent, down_weight, NT, preferred_element_type=F32
    )
    preact, back_grad = lax.psum((pre_part, back_part), "col")
    activated, factor = gelu_parts(preact)
    activated = activated.astype(BF16)
    delta = (back_grad * factor).astype(BF16)
    grad_down = lax.dot_general(
        activated, panel_cotangent, TN, preferred_element_type=F32
    )
    grad_up = lax.dot_general(panel_tokens, delta, TN, preferred_element_type=F32)
    grad_input = lax.psum_scatter(
        lax.dot_general(delta, up_weight, NT, preferred_element_type=F32),
        "row",
        scatter_dimension=0,
        tiled=True,
    )
    return (grad_input.astype(BF16), grad_up.astype(BF16), grad_down.astype(BF16))


def solution(mesh):
    row, col = mesh.shape["row"], mesh.shape["col"]

    def per_device(tokens, up_weight, down_weight, cotangent):
        args = (tokens, up_weight, down_weight, cotangent)
        short = row == 8 and tokens.shape[0] % 16 == 0
        if col == 2 and short:
            return split_plan(row, *args)
        return whole_plan(*args)

    in_specs = (
        P(("groups", "row"), "col"),
        P("col", "row"),
        P("row", "col"),
        P(("groups", "row"), "col"),
    )
    out_specs = (
        P(("groups", "row"), "col"),
        P(("groups", "col"), "row"),
        P(("groups", "row"), "col"),
    )
    return jax.shard_map(
        per_device, mesh=mesh, in_specs=in_specs, out_specs=out_specs, check_vma=False
    )
```

time: 309 us -> 156 us (0.50)
  waiting for transfers between devices: 182 us -> 34.7 us
  matrix products: 77.8 us -> 0 us
  Pallas kernels: 0 us -> 74.4 us
  starting transfers between devices: 0.34 us -> 42.7 us
  local copies, waits for them, and re-layouts: 23.4 us -> 1.7 us
  between operations: 13.8 us -> 0.8 us
  other arithmetic: 10.5 us -> 1.28 us
    all_gather x2 -> x0, waiting for transfers between devices: 88.3 us -> none  [the longest x1 53.4 us: per_device(): lax.all_gather(cotangent, 'row', axis=0, tiled=True)]
    dot_general x5 -> x0, matrix products: 77.8 us -> none  [the longest x2 33.8 us: transposed_times(): lax.dot_general(left, right, (((0,), (0,)), ((), ())), preferred_element_...]
    pallas_call x0 -> x10, Pallas kernels: none -> 74.4 us  [the longest x6 47.7 us: call(): pl.pallas_call(kernel, grid=(steps,), in_specs=in_specs, out_specs=out_sp...]
    psum x1 -> x0, waiting for transfers between devices: 58.4 us -> none  [per_device(): preact, back_grad = lax.psum((pre_part, back_part), 'col')]
    ppermute x0 -> x26, starting transfers between devices: none -> 42.7 us  [the longest x12 28.4 us: shift(): return lax.ppermute(x, 'row', [(r, (r + k * NX) % row) for r in range(row)])]
    ppermute x0 -> x26, waiting for transfers between devices: none -> 34.7 us  [the longest x12 19.2 us: shift(): return lax.ppermute(x, 'row', [(r, (r + k * NX) % row) for r in range(row)])]
    reduce_scatter x1 -> x0, waiting for transfers between devices: 34.1 us -> none  [per_device(): lax.psum_scatter(times_transposed(delta, up_weight), 'row', scatter_dimen...]
    unnamed x7 -> x6, local copies, waits for them, and re-layouts: 23.4 us -> 1.64 us
  transfers between devices with their start and end apart: 4 -> 26, of which waited for: 4 -> 8; matrix products, arithmetic and copies ran while one was open for 23% -> 0% of each run, Pallas kernels for 0% -> 43%
where the time goes in v2:
time: 156 us
  Pallas kernels  74.4 us (48%)
  starting transfers between devices  42.7 us (27%)
  waiting for transfers between devices  34.7 us (22%)
  local copies, waits for them, and re-layouts  1.7 us (1%)
    pallas_call x6, Pallas kernels, call(): pl.pallas_call(kernel, grid=(steps,), in_specs=in_specs, out_specs=out_sp...  47.7 us
    ppermute x12, starting transfers between devices, shift(): return lax.ppermute(x, 'row', [(r, (r + k * NX) % row) for r in range(row)])  28.4 us
    ppermute x12, waiting for transfers between devices, shift(): return lax.ppermute(x, 'row', [(r, (r + k * NX) % row) for r in range(row)])  19.2 us
    ppermute x10, waiting for transfers between devices, across(): return lax.ppermute(x, 'row', [(r, r ^ 1) for r in range(row)])  15.5 us
    pallas_call x2, Pallas kernels, up_pass(): pl.pallas_call(kernel, grid=(steps,), in_specs=[pl.BlockSpec((m, tile), l...  13.4 us
    pallas_call x2, Pallas kernels, down_pass(): pl.pallas_call(kernel, grid=(steps,), in_specs=[pl.BlockSpec((m, tile), l...  13.4 us
    ppermute x10, starting transfers between devices, across(): return lax.ppermute(x, 'row', [(r, r ^ 1) for r in range(row)])  13.3 us
  transfers between devices with their start and end apart: 26, of which 8 were waited for; matrix products, arithmetic and copies ran while one was open for 0% of the time, Pallas kernels for 43%

profile of v2, /device:TPU:0, one launch (start us, length us, event | category | flops | bytes accessed | tf_op | source)
XLA Modules:
  0.0 155.6 jit_solution(12790860094973741159)
XLA Ops:
  0.6 3.1 %collective-permute-start = (bf16[64,2048]{1,0:T(8,128)(2,1)}, bf16[64,2048]{1,0:T(8,128)(2,1)S(1)}, u32[]{:S(2)}, u32[]{:S(2)}) collective-permute-start(bf16[64,2048]{1,0:T(8,128)(2,1)} %refs_1_.9), channel_id=1, source_target_pairs={{0,4},{2,6},{4,8},{6,10},{8,12},{10,14},{12,0},{14,2},{1,5},{3,7},... | collective-permute-start | bytes 786440 | tf_op jit(solution)/shard_map/ppermute | solution.py:255
  5.2 2.2 %collective-permute-start.1 = (bf16[64,2048]{1,0:T(8,128)(2,1)}, bf16[64,2048]{1,0:T(8,128)(2,1)S(1)}, u32[]{:S(2)}, u32[]{:S(2)}) collective-permute-start(bf16[64,2048]{1,0:T(8,128)(2,1)} %refs_1_.9), channel_id=1, source_target_pairs={{0,12},{2,14},{4,0},{6,2},{8,4},{10,6},{12,8},{14,10},{1,13},{3,15... | collective-permute-start | bytes 786440 | tf_op jit(solution)/shard_map/ppermute | solution.py:255
  8.2 4.9 %collective-permute-done.refs_1_.refs_2_ = bf16[64,2048]{1,0:T(8,128)(2,1)S(1)} collective-permute-done((bf16[64,2048]{1,0:T(8,128)(2,1)}, bf16[64,2048]{1,0:T(8,128)(2,1)S(1)}, u32[]{:S(2)}, u32[]{:S(2)}) %collective-permute-start) | collective-permute-done | bytes 262176 | tf_op jit(solution)/shard_map/ppermute | solution.py:255
  15.2 10.0 %collective-permute-start.8 = (bf16[64,2048]{1,0:T(8,128)(2,1)}, bf16[64,2048]{1,0:T(8,128)(2,1)S(1)}, u32[]{:S(2)}, u32[]{:S(2)}) collective-permute-start(bf16[64,2048]{1,0:T(8,128)(2,1)} %refs_1_.7), channel_id=1, source_target_pairs={{0,4},{2,6},{4,8},{6,10},{8,12},{10,14},{12,0},{14,2},{1,5},{3,7},... | collective-permute-start | bytes 786440 | tf_op jit(solution)/shard_map/ppermute | solution.py:255
  26.7 8.2 %collective-permute-done.2.refs_3_.refs_4_ = bf16[64,2048]{1,0:T(8,128)(2,1)S(1)} collective-permute-done((bf16[64,2048]{1,0:T(8,128)(2,1)}, bf16[64,2048]{1,0:T(8,128)(2,1)S(1)}, u32[]{:S(2)}, u32[]{:S(2)}) %collective-permute-start.2) | collective-permute-done | bytes 262176 | tf_op jit(solution)/shard_map/ppermute | solution.py:255
  34.9 2.4 %collective-permute-start.7 = (bf16[64,2048]{1,0:T(8,128)(2,1)S(1)}, bf16[64,2048]{1,0:T(8,128)(2,1)S(1)}, u32[]{:S(2)}, u32[]{:S(2)}) collective-permute-start(bf16[64,2048]{1,0:T(8,128)(2,1)S(1)} %collective-permute-done.2.refs_3_.refs_4_), channel_id=1, source_target_pairs={{0,2},{2,0},{4,6},{6,4},{8,10},{10,8},{12,14},{14,12},{1,3},{3,1},... | collective-permute-start | bytes 786440 | tf_op jit(solution)/shard_map/ppermute | solution.py:252
  37.5 6.9 %collective-permute-done.7.refs_7_.refs_8_ = bf16[64,2048]{1,0:T(8,128)(2,1)S(1)} collective-permute-done((bf16[64,2048]{1,0:T(8,128)(2,1)S(1)}, bf16[64,2048]{1,0:T(8,128)(2,1)S(1)}, u32[]{:S(2)}, u32[]{:S(2)}) %collective-permute-start.7) | collective-permute-done | bytes 262176 | tf_op jit(solution)/shard_map/ppermute | solution.py:252
  44.4 2.1 %collective-permute-start.12 = (bf16[64,2048]{1,0:T(8,128)(2,1)S(1)}, bf16[64,2048]{1,0:T(8,128)(2,1)S(1)}, u32[]{:S(2)}, u32[]{:S(2)}) collective-permute-start(bf16[64,2048]{1,0:T(8,128)(2,1)S(1)} %collective-permute-done.9.refs_2_.refs_3_), channel_id=1, source_target_pairs={{0,2},{2,0},{4,6},{6,4},{8,10},{10,8},{12,14},{14,12},{1,3},{3,1},... | collective-permute-start | bytes 786440 | tf_op jit(solution)/shard_map/ppermute | solution.py:252
  47.4 7.0 %shard_map.67.refs_9_ = bf16[512,2048]{1,0:T(8,128)(2,1)S(1)} custom-call(bf16[64,2048]{1,0:T(8,128)(2,1)S(1)} %copy-done.1, bf16[64,2048]{1,0:T(8,128)(2,1)S(1)} %collective-permute-done.refs_1_.refs_2_, bf16[64,2048]{1,0:T(8,128)(2,1)S(1)} %collective-permute-done.1.refs_2_.refs_3_, bf16[64,2048]{1,0:T(8,128)(2,1)S(1)} %collective-permute-done.2.refs_3_.refs_4_, ...), custom_call_target="tpu_custom_call" | custom-call | flops 214748368 | bytes 629145 | tf_op jit(solution)/shard_map/pallas_call | solution.py:49
  54.7 7.0 %shard_map.68.refs_9_ = bf16[512,2048]{1,0:T(8,128)(2,1)S(1)} custom-call(bf16[64,2048]{1,0:T(8,128)(2,1)S(1)} %copy-done.1, bf16[64,2048]{1,0:T(8,128)(2,1)S(1)} %collective-permute-done.refs_1_.refs_2_, bf16[64,2048]{1,0:T(8,128)(2,1)S(1)} %collective-permute-done.1.refs_2_.refs_3_, bf16[64,2048]{1,0:T(8,128)(2,1)S(1)} %collective-permute-done.2.refs_3_.refs_4_, ...), custom_call_target="tpu_custom_call" | custom-call | flops 214748368 | bytes 629145 | tf_op jit(solution)/shard_map/pallas_call | solution.py:49
  63.6 6.9 %collective-permute-done.13.refs_7_.refs_8_ = bf16[64,2048]{1,0:T(8,128)(2,1)S(1)} collective-permute-done((bf16[64,2048]{1,0:T(8,128)(2,1)S(1)}, bf16[64,2048]{1,0:T(8,128)(2,1)S(1)}, u32[]{:S(2)}, u32[]{:S(2)}) %collective-permute-start.13) | collective-permute-done | bytes 262176 | tf_op jit(solution)/shard_map/ppermute | solution.py:252
  70.5 9.1 %shard_map.69 = (bf16[512,2048]{1,0:T(8,128)(2,1)S(1)}, bf16[512,2048]{1,0:T(8,128)(2,1)S(1)}) custom-call(bf16[64,2048]{1,0:T(8,128)(2,1)S(1)} %copy-done, bf16[64,2048]{1,0:T(8,128)(2,1)S(1)} %collective-permute-done.8.refs_1_.refs_2_, bf16[64,2048]{1,0:T(8,128)(2,1)S(1)} %collective-permute-done.9.refs_2_.refs_3_, ...), custom_call_target="tpu_custom_call" | custom-call | flops 214748368 | bytes 943718 | tf_op jit(solution)/shard_map/pallas_call | solution.py:49
  79.7 9.1 %shard_map.70 = (bf16[512,2048]{1,0:T(8,128)(2,1)S(1)}, bf16[512,2048]{1,0:T(8,128)(2,1)S(1)}) custom-call(bf16[64,2048]{1,0:T(8,128)(2,1)S(1)} %copy-done, bf16[64,2048]{1,0:T(8,128)(2,1)S(1)} %collective-permute-done.8.refs_1_.refs_2_, bf16[64,2048]{1,0:T(8,128)(2,1)S(1)} %collective-permute-done.9.refs_2_.refs_3_, ...), custom_call_target="tpu_custom_call" | custom-call | flops 214748368 | bytes 943718 | tf_op jit(solution)/shard_map/pallas_call | solution.py:49
  89.4 6.7 %shard_map.71.refs_9_ = bf16[4096,2048]{1,0:T(8,128)(2,1)} custom-call(bf16[512,2048]{1,0:T(8,128)(2,1)S(1)} %get-tuple-element.49.refs_0_, bf16[64,2048]{1,0:T(8,128)(2,1)S(1)} %copy-done, bf16[64,2048]{1,0:T(8,128)(2,1)S(1)} %collective-permute-done.8.refs_1_.refs_2_, bf16[64,2048]{1,0:T(8,128)(2,1)S(1)} %collective-permute-done.9.refs_2_.refs_3_, ...), custom_call_target="tpu_custom_call" | custom-call | flops 214748368 | bytes 629145 | tf_op jit(solution)/shard_map/pallas_call | solution.py:194
  96.1 8.3 %shard_map.72 = (f32[256,1024]{1,0:T(8,128)S(1)}, bf16[256,1024]{1,0:T(8,128)(2,1)S(1)}, bf16[512,4096]{1,0:T(8,128)(2,1)S(1)}) custom-call(bf16[512,2048]{1,0:T(8,128)(2,1)S(1)} %get-tuple-element.50.refs_0_, bf16[512,2048]{1,0:T(8,128)(2,1)S(1)} %get-tuple-element.48.refs_1_, bf16[512,2048]{1,0:T(8,128)(2,1)S(1)} %collective-permute-done.16.refs_2_, ...), custom_call_target="tpu_custom_call" | custom-call | flops 214748368 | bytes 838860 | tf_op jit(solution)/shard_map/pallas_call | solution.py:49
  104.4 1.8 %collective-permute-start.18 = (bf16[256,1024]{1,0:T(8,128)(2,1)S(1)}, bf16[256,1024]{1,0:T(8,128)(2,1)S(1)}, u32[]{:S(2)}, u32[]{:S(2)}) collective-permute-start(bf16[256,1024]{1,0:T(8,128)(2,1)S(1)} %get-tuple-element.52), channel_id=1, source_target_pairs={{0,2},{2,0},{4,6},{6,4},{8,10},{10,8},{12,14},{14,12},{1,3},{3,1},... | collective-permute-start | bytes 1572872 | tf_op jit(solution)/shard_map/ppermute | solution.py:252
  106.2 7.2 %shard_map.73 = (f32[256,1024]{1,0:T(8,128)S(1)}, bf16[256,1024]{1,0:T(8,128)(2,1)S(1)}) custom-call(bf16[512,4096]{1,0:T(8,128)(2,1)S(1)} %get-tuple-element.64.refs_0_, bf16[2048,4096]{1,0:T(8,128)(2,1)} %refs_1_.6), custom_call_target="tpu_custom_call" | custom-call | flops 214748368 | bytes 838860 | tf_op jit(solution)/shard_map/pallas_call | solution.py:49
  113.8 6.7 %shard_map.74 = bf16[4096,2048]{1,0:T(8,128)(2,1)} custom-call(bf16[512,2048]{1,0:T(8,128)(2,1)S(1)} %get-tuple-element.57.refs_0_, bf16[64,2048]{1,0:T(8,128)(2,1)S(1)} %copy-done, bf16[64,2048]{1,0:T(8,128)(2,1)S(1)} %collective-permute-done.8.refs_1_.refs_2_, ...), custom_call_target="tpu_custom_call", output_to_operand_aliasing={{}: (9, {})} | custom-call | flops 214748368 | bytes 629145 | tf_op jit(solution)/shard_map/pallas_call | solution.py:194
  121.4 6.7 %shard_map.75.refs_9_ = bf16[2048,4096]{1,0:T(8,128)(2,1)} custom-call(bf16[512,4096]{1,0:T(8,128)(2,1)S(1)} %get-tuple-element.64.refs_0_, bf16[64,2048]{1,0:T(8,128)(2,1)S(1)} %copy-done.2, bf16[64,2048]{1,0:T(8,128)(2,1)S(1)} %collective-permute-done.refs_1_.refs_2_, bf16[64,2048]{1,0:T(8,128)(2,1)S(1)} %collective-permute-done.1.refs_2_.refs_3_, ...), custom_call_target="tpu_custom_call" | custom-call | flops 214748368 | bytes 629145 | tf_op jit(solution)/shard_map/pallas_call | solution.py:224
  129.9 4.6 %collective-permute-start.25 = (bf16[64,1024]{1,0:T(8,128)(2,1)S(1)}, bf16[64,1024]{1,0:T(8,128)(2,1)S(1)}, u32[]{:S(2)}, u32[]{:S(2)}) collective-permute-start(bf16[64,1024]{1,0:T(8,128)(2,1)S(1)} %get-tuple-element.70), channel_id=1, source_target_pairs={{0,8},{2,10},{4,12},{6,14},{8,0},{10,2},{12,4},{14,6},{1,9},{3,11}... | collective-permute-start | bytes 393224 | tf_op jit(solution)/shard_map/ppermute | solution.py:255
  134.5 3.8 %collective-permute-start.23 = (bf16[64,1024]{1,0:T(8,128)(2,1)S(1)}, bf16[64,1024]{1,0:T(8,128)(2,1)S(1)}, u32[]{:S(2)}, u32[]{:S(2)}) collective-permute-start(bf16[64,1024]{1,0:T(8,128)(2,1)S(1)} %get-tuple-element.69), channel_id=1, source_target_pairs={{0,12},{2,14},{4,0},{6,2},{8,4},{10,6},{12,8},{14,10},{1,13},{3,15... | collective-permute-start | bytes 393224 | tf_op jit(solution)/shard_map/ppermute | solution.py:255
  138.9 6.7 %shard_map.76 = bf16[2048,4096]{1,0:T(8,128)(2,1)} custom-call(bf16[512,4096]{1,0:T(8,128)(2,1)S(1)} %get-tuple-element.64.refs_0_, bf16[64,2048]{1,0:T(8,128)(2,1)S(1)} %copy-done.2, bf16[64,2048]{1,0:T(8,128)(2,1)S(1)} %collective-permute-done.refs_1_.refs_2_, ...), custom_call_target="tpu_custom_call", output_to_operand_aliasing={{}: (9, {})} | custom-call | flops 214748368 | bytes 629145 | tf_op jit(solution)/shard_map/pallas_call | solution.py:224
  145.5 3.3 %collective-permute-start.19 = (bf16[64,1024]{1,0:T(8,128)(2,1)S(1)}, bf16[64,1024]{1,0:T(8,128)(2,1)S(1)}, u32[]{:S(2)}, u32[]{:S(2)}) collective-permute-start(bf16[64,1024]{1,0:T(8,128)(2,1)S(1)} %get-tuple-element.74), channel_id=1, source_target_pairs={{0,12},{2,14},{4,0},{6,2},{8,4},{10,6},{12,8},{14,10},{1,13},{3,15... | collective-permute-start | bytes 393224 | tf_op jit(solution)/shard_map/ppermute | solution.py:255
  148.9 5.9 %collective-permute-done.21 = bf16[64,1024]{1,0:T(8,128)(2,1)S(1)} collective-permute-done((bf16[64,1024]{1,0:T(8,128)(2,1)S(1)}, bf16[64,1024]{1,0:T(8,128)(2,1)S(1)}, u32[]{:S(2)}, u32[]{:S(2)}) %collective-permute-start.21) | collective-permute-done | bytes 131104 | tf_op jit(solution)/shard_map/ppermute | solution.py:255
  (51 shorter events, 14.4 us)
Async XLA Ops:
  0.6 12.5 %collective-permute-start = (bf16[64,2048]{1,0:T(8,128)(2,1)}, bf16[64,2048]{1,0:T(8,128)(2,1)S(1)}, u32[]{:S(2)}, u32[]{:S(2)}) collective-permute-start(bf16[64,2048]{1,0:T(8,128)(2,1)} %refs_1_.9), channel_id=1, source_target_pairs={{0,4},{2,6},{4,8},{6,10},{8,12},{10,14},{12,0},{14,2},{1,5},{3,7},... | collective-permute-start | bytes 786440 | tf_op jit(solution)/shard_map/ppermute | solution.py:255
  3.7 11.2 %collective-permute-start.3 = (bf16[64,2048]{1,0:T(8,128)(2,1)}, bf16[64,2048]{1,0:T(8,128)(2,1)S(1)}, u32[]{:S(2)}, u32[]{:S(2)}) collective-permute-start(bf16[64,2048]{1,0:T(8,128)(2,1)} %refs_1_.9), channel_id=1, source_target_pairs={{0,2},{2,0},{4,6},{6,4},{8,10},{10,8},{12,14},{14,12},{1,3},{3,1},... | collective-permute-start | bytes 786440 | tf_op jit(solution)/shard_map/ppermute | solution.py:252
  5.2 19.9 %collective-permute-start.1 = (bf16[64,2048]{1,0:T(8,128)(2,1)}, bf16[64,2048]{1,0:T(8,128)(2,1)S(1)}, u32[]{:S(2)}, u32[]{:S(2)}) collective-permute-start(bf16[64,2048]{1,0:T(8,128)(2,1)} %refs_1_.9), channel_id=1, source_target_pairs={{0,12},{2,14},{4,0},{6,2},{8,4},{10,6},{12,8},{14,10},{1,13},{3,15... | collective-permute-start | bytes 786440 | tf_op jit(solution)/shard_map/ppermute | solution.py:255
  7.4 27.4 %collective-permute-start.2 = (bf16[64,2048]{1,0:T(8,128)(2,1)}, bf16[64,2048]{1,0:T(8,128)(2,1)S(1)}, u32[]{:S(2)}, u32[]{:S(2)}) collective-permute-start(bf16[64,2048]{1,0:T(8,128)(2,1)} %refs_1_.9), channel_id=1, source_target_pairs={{0,8},{2,10},{4,12},{6,14},{8,0},{10,2},{12,4},{14,6},{1,9},{3,11}... | collective-permute-start | bytes 786440 | tf_op jit(solution)/shard_map/ppermute | solution.py:255
  13.1 12.0 %collective-permute-start.4 = (bf16[64,2048]{1,0:T(8,128)(2,1)S(1)}, bf16[64,2048]{1,0:T(8,128)(2,1)S(1)}, u32[]{:S(2)}, u32[]{:S(2)}) collective-permute-start(bf16[64,2048]{1,0:T(8,128)(2,1)S(1)} %collective-permute-done.refs_1_.refs_2_), channel_id=1, source_target_pairs={{0,2},{2,0},{4,6},{6,4},{8,10},{10,8},{12,14},{14,12},{1,3},{3,1},... | collective-permute-start | bytes 786440 | tf_op jit(solution)/shard_map/ppermute | solution.py:252
  14.9 20.0 %collective-permute-start.6 = (bf16[64,2048]{1,0:T(8,128)(2,1)}, bf16[64,2048]{1,0:T(8,128)(2,1)S(1)}, u32[]{:S(2)}, u32[]{:S(2)}) collective-permute-start(bf16[64,2048]{1,0:T(8,128)(2,1)} %refs_1_.7), channel_id=1, source_target_pairs={{0,2},{2,0},{4,6},{6,4},{8,10},{10,8},{12,14},{14,12},{1,3},{3,1},... | collective-permute-start | bytes 786440 | tf_op jit(solution)/shard_map/ppermute | solution.py:252
  15.2 22.1 %collective-permute-start.8 = (bf16[64,2048]{1,0:T(8,128)(2,1)}, bf16[64,2048]{1,0:T(8,128)(2,1)S(1)}, u32[]{:S(2)}, u32[]{:S(2)}) collective-permute-start(bf16[64,2048]{1,0:T(8,128)(2,1)} %refs_1_.7), channel_id=1, source_target_pairs={{0,4},{2,6},{4,8},{6,10},{8,12},{10,14},{12,0},{14,2},{1,5},{3,7},... | collective-permute-start | bytes 786440 | tf_op jit(solution)/shard_map/ppermute | solution.py:255
  25.1 12.4 %collective-permute-start.9 = (bf16[64,2048]{1,0:T(8,128)(2,1)}, bf16[64,2048]{1,0:T(8,128)(2,1)S(1)}, u32[]{:S(2)}, u32[]{:S(2)}) collective-permute-start(bf16[64,2048]{1,0:T(8,128)(2,1)} %refs_1_.7), channel_id=1, source_target_pairs={{0,12},{2,14},{4,0},{6,2},{8,4},{10,6},{12,8},{14,10},{1,13},{3,15... | collective-permute-start | bytes 786440 | tf_op jit(solution)/shard_map/ppermute | solution.py:255
  25.2 12.1 %collective-permute-start.5 = (bf16[64,2048]{1,0:T(8,128)(2,1)S(1)}, bf16[64,2048]{1,0:T(8,128)(2,1)S(1)}, u32[]{:S(2)}, u32[]{:S(2)}) collective-permute-start(bf16[64,2048]{1,0:T(8,128)(2,1)S(1)} %collective-permute-done.1.refs_2_.refs_3_), channel_id=1, source_target_pairs={{0,2},{2,0},{4,6},{6,4},{8,10},{10,8},{12,14},{14,12},{1,3},{3,1},... | collective-permute-start | bytes 786440 | tf_op jit(solution)/shard_map/ppermute | solution.py:252
  34.9 9.5 %collective-permute-start.7 = (bf16[64,2048]{1,0:T(8,128)(2,1)S(1)}, bf16[64,2048]{1,0:T(8,128)(2,1)S(1)}, u32[]{:S(2)}, u32[]{:S(2)}) collective-permute-start(bf16[64,2048]{1,0:T(8,128)(2,1)S(1)} %collective-permute-done.2.refs_3_.refs_4_), channel_id=1, source_target_pairs={{0,2},{2,0},{4,6},{6,4},{8,10},{10,8},{12,14},{14,12},{1,3},{3,1},... | collective-permute-start | bytes 786440 | tf_op jit(solution)/shard_map/ppermute | solution.py:252
  37.3 17.2 %collective-permute-start.10 = (bf16[64,2048]{1,0:T(8,128)(2,1)}, bf16[64,2048]{1,0:T(8,128)(2,1)S(1)}, u32[]{:S(2)}, u32[]{:S(2)}) collective-permute-start(bf16[64,2048]{1,0:T(8,128)(2,1)} %refs_1_.7), channel_id=1, source_target_pairs={{0,8},{2,10},{4,12},{6,14},{8,0},{10,2},{12,4},{14,6},{1,9},{3,11}... | collective-permute-start | bytes 786440 | tf_op jit(solution)/shard_map/ppermute | solution.py:255
  37.3 17.2 %collective-permute-start.11 = (bf16[64,2048]{1,0:T(8,128)(2,1)S(1)}, bf16[64,2048]{1,0:T(8,128)(2,1)S(1)}, u32[]{:S(2)}, u32[]{:S(2)}) collective-permute-start(bf16[64,2048]{1,0:T(8,128)(2,1)S(1)} %collective-permute-done.8.refs_1_.refs_2_), channel_id=1, source_target_pairs={{0,2},{2,0},{4,6},{6,4},{8,10},{10,8},{12,14},{14,12},{1,3},{3,1},... | collective-permute-start | bytes 786440 | tf_op jit(solution)/shard_map/ppermute | solution.py:252
  44.4 10.3 %collective-permute-start.12 = (bf16[64,2048]{1,0:T(8,128)(2,1)S(1)}, bf16[64,2048]{1,0:T(8,128)(2,1)S(1)}, u32[]{:S(2)}, u32[]{:S(2)}) collective-permute-start(bf16[64,2048]{1,0:T(8,128)(2,1)S(1)} %collective-permute-done.9.refs_2_.refs_3_), channel_id=1, source_target_pairs={{0,2},{2,0},{4,6},{6,4},{8,10},{10,8},{12,14},{14,12},{1,3},{3,1},... | collective-permute-start | bytes 786440 | tf_op jit(solution)/shard_map/ppermute | solution.py:252
  54.4 16.1 %collective-permute-start.14 = (bf16[512,2048]{1,0:T(8,128)(2,1)S(1)}, bf16[512,2048]{1,0:T(8,128)(2,1)S(1)}, u32[]{:S(2)}, u32[]{:S(2)}) collective-permute-start(bf16[512,2048]{1,0:T(8,128)(2,1)S(1)} %shard_map.67.refs_9_), channel_id=1, source_target_pairs={{0,1},{1,0},{2,3},{3,2},{4,5},{5,4},{6,7},{7,6},{8,9},{9,8},{10,11... | collective-permute-start | bytes 6291464 | tf_op jit(solution)/shard_map/ppermute | solution.py:249
  61.7 18.0 %collective-permute-start.15 = (bf16[512,2048]{1,0:T(8,128)(2,1)S(1)}, bf16[512,2048]{1,0:T(8,128)(2,1)S(1)}, u32[]{:S(2)}, u32[]{:S(2)}) collective-permute-start(bf16[512,2048]{1,0:T(8,128)(2,1)S(1)} %shard_map.68.refs_9_), channel_id=1, source_target_pairs={{0,1},{1,0},{2,3},{3,2},{4,5},{5,4},{6,7},{7,6},{8,9},{9,8},{10,11... | collective-permute-start | bytes 6291464 | tf_op jit(solution)/shard_map/ppermute | solution.py:249
  79.7 16.4 %collective-permute-start.16 = (bf16[512,2048]{1,0:T(8,128)(2,1)S(1)}, bf16[512,2048]{1,0:T(8,128)(2,1)S(1)}, u32[]{:S(2)}, u32[]{:S(2)}) collective-permute-start(bf16[512,2048]{1,0:T(8,128)(2,1)S(1)} %get-tuple-element.50.refs_0_), channel_id=1, source_target_pairs={{0,1},{1,0},{2,3},{3,2},{4,5},{5,4},{6,7},{7,6},{8,9},{9,8},{10,11... | collective-permute-start | bytes 6291464 | tf_op jit(solution)/shard_map/ppermute | solution.py:249
  104.4 16.0 %collective-permute-start.18 = (bf16[256,1024]{1,0:T(8,128)(2,1)S(1)}, bf16[256,1024]{1,0:T(8,128)(2,1)S(1)}, u32[]{:S(2)}, u32[]{:S(2)}) collective-permute-start(bf16[256,1024]{1,0:T(8,128)(2,1)S(1)} %get-tuple-element.52), channel_id=1, source_target_pairs={{0,2},{2,0},{4,6},{6,4},{8,10},{10,8},{12,14},{14,12},{1,3},{3,1},... | collective-permute-start | bytes 1572872 | tf_op jit(solution)/shard_map/ppermute | solution.py:252
  113.4 16.2 %collective-permute-start.22 = (bf16[256,1024]{1,0:T(8,128)(2,1)S(1)}, bf16[256,1024]{1,0:T(8,128)(2,1)S(1)}, u32[]{:S(2)}, u32[]{:S(2)}) collective-permute-start(bf16[256,1024]{1,0:T(8,128)(2,1)S(1)} %get-tuple-element.60), channel_id=1, source_target_pairs={{0,2},{2,0},{4,6},{6,4},{8,10},{10,8},{12,14},{14,12},{1,3},{3,1},... | collective-permute-start | bytes 1572872 | tf_op jit(solution)/shard_map/ppermute | solution.py:252
  129.9 15.7 %collective-permute-start.25 = (bf16[64,1024]{1,0:T(8,128)(2,1)S(1)}, bf16[64,1024]{1,0:T(8,128)(2,1)S(1)}, u32[]{:S(2)}, u32[]{:S(2)}) collective-permute-start(bf16[64,1024]{1,0:T(8,128)(2,1)S(1)} %get-tuple-element.70), channel_id=1, source_target_pairs={{0,8},{2,10},{4,12},{6,14},{8,0},{10,2},{12,4},{14,6},{1,9},{3,11}... | collective-permute-start | bytes 393224 | tf_op jit(solution)/shard_map/ppermute | solution.py:255
  134.5 14.3 %collective-permute-start.24 = (bf16[64,1024]{1,0:T(8,128)(2,1)S(1)}, bf16[64,1024]{1,0:T(8,128)(2,1)S(1)}, u32[]{:S(2)}, u32[]{:S(2)}) collective-permute-start(bf16[64,1024]{1,0:T(8,128)(2,1)S(1)} %get-tuple-element.71), channel_id=1, source_target_pairs={{0,4},{2,6},{4,8},{6,10},{8,12},{10,14},{12,0},{14,2},{1,5},{3,7},... | collective-permute-start | bytes 393224 | tf_op jit(solution)/shard_map/ppermute | solution.py:255
  134.5 14.3 %collective-permute-start.23 = (bf16[64,1024]{1,0:T(8,128)(2,1)S(1)}, bf16[64,1024]{1,0:T(8,128)(2,1)S(1)}, u32[]{:S(2)}, u32[]{:S(2)}) collective-permute-start(bf16[64,1024]{1,0:T(8,128)(2,1)S(1)} %get-tuple-element.69), channel_id=1, source_target_pairs={{0,12},{2,14},{4,0},{6,2},{8,4},{10,6},{12,8},{14,10},{1,13},{3,15... | collective-permute-start | bytes 393224 | tf_op jit(solution)/shard_map/ppermute | solution.py:255
  138.3 16.5 %collective-permute-start.21 = (bf16[64,1024]{1,0:T(8,128)(2,1)S(1)}, bf16[64,1024]{1,0:T(8,128)(2,1)S(1)}, u32[]{:S(2)}, u32[]{:S(2)}) collective-permute-start(bf16[64,1024]{1,0:T(8,128)(2,1)S(1)} %get-tuple-element.72), channel_id=1, source_target_pairs={{0,8},{2,10},{4,12},{6,14},{8,0},{10,2},{12,4},{14,6},{1,9},{3,11}... | collective-permute-start | bytes 393224 | tf_op jit(solution)/shard_map/ppermute | solution.py:255
  138.3 16.5 %collective-permute-start.20 = (bf16[64,1024]{1,0:T(8,128)(2,1)S(1)}, bf16[64,1024]{1,0:T(8,128)(2,1)S(1)}, u32[]{:S(2)}, u32[]{:S(2)}) collective-permute-start(bf16[64,1024]{1,0:T(8,128)(2,1)S(1)} %get-tuple-element.73), channel_id=1, source_target_pairs={{0,4},{2,6},{4,8},{6,10},{8,12},{10,14},{12,0},{14,2},{1,5},{3,7},... | collective-permute-start | bytes 393224 | tf_op jit(solution)/shard_map/ppermute | solution.py:255
  145.5 9.3 %collective-permute-start.19 = (bf16[64,1024]{1,0:T(8,128)(2,1)S(1)}, bf16[64,1024]{1,0:T(8,128)(2,1)S(1)}, u32[]{:S(2)}, u32[]{:S(2)}) collective-permute-start(bf16[64,1024]{1,0:T(8,128)(2,1)S(1)} %get-tuple-element.74), channel_id=1, source_target_pairs={{0,12},{2,14},{4,0},{6,2},{8,4},{10,6},{12,8},{14,10},{1,13},{3,15... | collective-permute-start | bytes 393224 | tf_op jit(solution)/shard_map/ppermute | solution.py:255
  (5 other events, 33.7 us)

commit v3 on v2

--- a/solution.py
+++ b/solution.py
@@ -15,8 +15,8 @@
 SPLITS = 2
 Z_AHEAD = 3
 X_AHEAD = 2
-PRE_TILE = 1024
-BACK_TILE = 1024
+PRE_TILE = 512
+BACK_TILE = 512
 IN_TILE = 256
 NT = (((1,), (1,)), ((), ()))
 TN = (((0,), (0,)), ((), ()))
@@ -35,9 +35,11 @@
     return pltpu.CompilerParams(vmem_limit_bytes=VMEM_LIMIT)
 
 
-def cost(flops, moved, transcendentals=0):
+def cost(flops, moved, weight=1):
     return pl.CostEstimate(
-        flops=flops // 20, bytes_accessed=moved // 20, transcendentals=0
+        flops=flops * weight // 20,
+        bytes_accessed=moved * weight // 20,
+        transcendentals=0,
     )
 
 
@@ -62,7 +64,7 @@
     return pl.BlockSpec(x.shape, lambda i: (0, 0))
 
 
-def pre_pass(tokens, up, first, hidden):
+def pre_pass(tokens, up, first, hidden, weight):
     n = len(tokens)
     rows, feats = tokens[0].shape
     m = n * rows
@@ -82,12 +84,12 @@
         + [pl.BlockSpec((feats, tile), lambda i: (0, base + i))],
         pl.BlockSpec((m, tile), lambda i: (0, i)),
         jax.ShapeDtypeStruct((m, hidden), BF16),
-        cost(2 * m * feats * hidden, 2 * feats * hidden + m * (2 * feats + 2 * hidden)),
+        cost(2 * m * feats * hidden, 2 * feats * hidden + m * (2 * feats + 2 * hidden), weight),
         (*tokens, up),
     )
 
 
-def back_pass(cots, down, pre, pre_other, first):
+def back_pass(cots, down, pre, pre_other, first, weight):
     n = len(cots)
     rows, feats = cots[0].shape
     m, hidden = pre.shape
@@ -116,7 +118,7 @@
         cost(
             2 * m * feats * hidden,
             2 * feats * hidden + m * (2 * feats + 8 * hidden),
-            m * hidden,
+            weight,
         ),
         (*cots, down, pre, pre_other),
     )
@@ -263,7 +265,7 @@
         ("c", cotangent, near + [far]),
     ):
         for k in ks:
-            tie = sent[-Z_AHEAD:][:1] if len(sent) >= Z_AHEAD else ()
+            tie = [same["t", far]] if name == "c" else []
             same[name, k] = shift(tied(block, *tie), k)
             sent.append(same[name, k])
     queue = [("t", 0), ("t", near[0]), ("c", 0)]
@@ -283,12 +285,12 @@
     hidden = up_weight.shape[1]
     each = hidden // 2
     all_tokens, all_cots = pieces("t"), pieces("c")
-    pre0 = pre_pass(all_tokens, up_weight, 0, each)
-    events = [pre0] + sent[len(near) + 1 :] + crossed[-1 - len(near) : -1]
-    pre1 = pre_pass(after(all_tokens, *events), up_weight, each, each)
+    pre0 = pre_pass(after(all_tokens, same["c", near[0]], same["c", near[1]]), up_weight, 0, each, 1)
+    events = [pre0, *[same["c", k] for k in near+[far]], facing["c", near[0]], facing["c", near[1]]]
+    pre1 = pre_pass(after(all_tokens, *events), up_weight, each, each, 100)
     other0, other1 = swap(pre0), swap(pre1)
-    act0, delta0 = back_pass(after(all_cots, pre1), down_weight, pre0, other0, 0)
-    act1, delta1 = back_pass(after(all_cots, delta0), down_weight, pre1, other1, each)
+    act0, delta0 = back_pass(after(all_cots, pre1), down_weight, pre0, other0, 0, 100)
+    act1, delta1 = back_pass(after(all_cots, delta0), down_weight, pre1, other1, each, 1)
     deltas = [delta0, delta1, swap(delta0), swap(delta1)]
     grad_down = down_pass(tied(act0, delta1), all_cots, 0, 2)
 
@@ -311,11 +313,14 @@
         total = kept + gone.astype(F32)
         blocks = [total[at * mine : (at + 1) * mine] for at in range(nz)]
         sends = [b.astype(BF16) for b in blocks[1:]]
+        if columns:
+            sends[0] = tied(sends[0], columns[-1][1][0])
         columns.append((blocks[0], [shift(b, -k) for k, b in zip(order[1:], sends)]))
         grad_up = up_pass(tied(delta, *sends), all_tokens, s, SPLITS, grad_up)
         last = grad_up
     done = []
     for first, rest in columns:
+        first = tied(first, grad_up)
         for block in rest:
             first = first + block.astype(F32)
         done.append(first.astype(BF16))

time: 156 us -> 139 us (0.89)
  waiting for transfers between devices: 34.7 us -> 15.9 us
  starting transfers between devices: 42.7 us -> 45.2 us
    ppermute x10, waiting for transfers between devices: 15.5 us -> 0.16 us  [across(): return lax.ppermute(x, 'row', [(r, r ^ 1) for r in range(row)])]
    ppermute x12, waiting for transfers between devices: 19.2 us -> 15.7 us  [shift(): return lax.ppermute(x, 'row', [(r, (r + k * NX) % row) for r in range(row)])]
    ppermute x12, starting transfers between devices: 28.4 us -> 31.2 us  [shift(): return lax.ppermute(x, 'row', [(r, (r + k * NX) % row) for r in range(row)])]
  transfers between devices with their start and end apart: 26 -> 26, of which waited for: 8 -> 7; matrix products, arithmetic and copies ran while one was open for 0% -> 0% of each run, Pallas kernels for 43% -> 48%
where the time goes in v3:
time: 139 us
  Pallas kernels  74.5 us (54%)
  starting transfers between devices  45.2 us (33%)
  waiting for transfers between devices  15.9 us (11%)
    pallas_call x6, Pallas kernels, call(): pl.pallas_call(kernel, grid=(steps,), in_specs=in_specs, out_specs=out_sp...  47.7 us
    ppermute x12, starting transfers between devices, shift(): return lax.ppermute(x, 'row', [(r, (r + k * NX) % row) for r in range(row)])  31.2 us
    ppermute x12, waiting for transfers between devices, shift(): return lax.ppermute(x, 'row', [(r, (r + k * NX) % row) for r in range(row)])  15.7 us
    pallas_call x2, Pallas kernels, up_pass(): pl.pallas_call(kernel, grid=(steps,), in_specs=[pl.BlockSpec((m, tile), l...  13.4 us
    pallas_call x2, Pallas kernels, down_pass(): pl.pallas_call(kernel, grid=(steps,), in_specs=[pl.BlockSpec((m, tile), l...  13.4 us
    ppermute x10, starting transfers between devices, across(): return lax.ppermute(x, 'row', [(r, r ^ 1) for r in range(row)])  13.2 us
  transfers between devices with their start and end apart: 26, of which 7 were waited for; matrix products, arithmetic and copies ran while one was open for 0% of the time, Pallas kernels for 48%

profile of v3, /device:TPU:0, one launch (start us, length us, event | category | flops | bytes accessed | tf_op | source)
XLA Modules:
  0.0 138.7 jit_solution(1326265967241227041)
XLA Ops:
  0.6 3.1 %collective-permute-start.3 = (bf16[64,2048]{1,0:T(8,128)(2,1)}, bf16[64,2048]{1,0:T(8,128)(2,1)S(1)}, u32[]{:S(2)}, u32[]{:S(2)}) collective-permute-start(bf16[64,2048]{1,0:T(8,128)(2,1)} %refs_1_.9), channel_id=1, source_target_pairs={{0,4},{2,6},{4,8},{6,10},{8,12},{10,14},{12,0},{14,2},{1,5},{3,7},... | collective-permute-start | bytes 786440 | tf_op jit(solution)/shard_map/ppermute | solution.py:257
  5.2 2.6 %collective-permute-start = (bf16[64,2048]{1,0:T(8,128)(2,1)}, bf16[64,2048]{1,0:T(8,128)(2,1)S(1)}, u32[]{:S(2)}, u32[]{:S(2)}) collective-permute-start(bf16[64,2048]{1,0:T(8,128)(2,1)} %refs_1_.9), channel_id=1, source_target_pairs={{0,8},{2,10},{4,12},{6,14},{8,0},{10,2},{12,4},{14,6},{1,9},{3,11}... | collective-permute-start | bytes 786440 | tf_op jit(solution)/shard_map/ppermute | solution.py:257
  9.1 4.1 %collective-permute-done.3.refs_1_.refs_2_ = bf16[64,2048]{1,0:T(8,128)(2,1)S(1)} collective-permute-done((bf16[64,2048]{1,0:T(8,128)(2,1)}, bf16[64,2048]{1,0:T(8,128)(2,1)S(1)}, u32[]{:S(2)}, u32[]{:S(2)}) %collective-permute-start.3) | collective-permute-done | bytes 262176 | tf_op jit(solution)/shard_map/ppermute | solution.py:257
  13.2 1.7 %collective-permute-start.6 = (bf16[64,2048]{1,0:T(8,128)(2,1)S(1)}, bf16[64,2048]{1,0:T(8,128)(2,1)S(1)}, u32[]{:S(2)}, u32[]{:S(2)}) collective-permute-start(bf16[64,2048]{1,0:T(8,128)(2,1)S(1)} %collective-permute-done.3.refs_1_.refs_2_), channel_id=1, source_target_pairs={{0,2},{2,0},{4,6},{6,4},{8,10},{10,8},{12,14},{14,12},{1,3},{3,1},... | collective-permute-start | bytes 786440 | tf_op jit(solution)/shard_map/ppermute | solution.py:254
  15.3 8.4 %collective-permute-done.refs_3_.refs_4_ = bf16[64,2048]{1,0:T(8,128)(2,1)S(1)} collective-permute-done((bf16[64,2048]{1,0:T(8,128)(2,1)}, bf16[64,2048]{1,0:T(8,128)(2,1)S(1)}, u32[]{:S(2)}, u32[]{:S(2)}) %collective-permute-start) | collective-permute-done | bytes 262176 | tf_op jit(solution)/shard_map/ppermute | solution.py:257
  23.6 4.7 %collective-permute-start.1 = (bf16[64,2048]{1,0:T(8,128)(2,1)}, bf16[64,2048]{1,0:T(8,128)(2,1)S(1)}, u32[]{:S(2)}, u32[]{:S(2)}) collective-permute-start(bf16[64,2048]{1,0:T(8,128)(2,1)} %refs_1_.7), channel_id=1, source_target_pairs={{0,4},{2,6},{4,8},{6,10},{8,12},{10,14},{12,0},{14,2},{1,5},{3,7},... | collective-permute-start | bytes 786440 | tf_op jit(solution)/shard_map/ppermute | solution.py:257
  29.8 2.8 %collective-permute-start.2 = (bf16[64,2048]{1,0:T(8,128)(2,1)}, bf16[64,2048]{1,0:T(8,128)(2,1)S(1)}, u32[]{:S(2)}, u32[]{:S(2)}) collective-permute-start(bf16[64,2048]{1,0:T(8,128)(2,1)} %refs_1_.7), channel_id=1, source_target_pairs={{0,12},{2,14},{4,0},{6,2},{8,4},{10,6},{12,8},{14,10},{1,13},{3,15... | collective-permute-start | bytes 786440 | tf_op jit(solution)/shard_map/ppermute | solution.py:257
  33.1 4.8 %collective-permute-start.10 = (bf16[64,2048]{1,0:T(8,128)(2,1)}, bf16[64,2048]{1,0:T(8,128)(2,1)S(1)}, u32[]{:S(2)}, u32[]{:S(2)}) collective-permute-start(bf16[64,2048]{1,0:T(8,128)(2,1)} %refs_1_.7), channel_id=1, source_target_pairs={{0,8},{2,10},{4,12},{6,14},{8,0},{10,2},{12,4},{14,6},{1,9},{3,11}... | collective-permute-start | bytes 786440 | tf_op jit(solution)/shard_map/ppermute | solution.py:257
  38.4 1.5 %collective-permute-start.11 = (bf16[64,2048]{1,0:T(8,128)(2,1)S(1)}, bf16[64,2048]{1,0:T(8,128)(2,1)S(1)}, u32[]{:S(2)}, u32[]{:S(2)}) collective-permute-start(bf16[64,2048]{1,0:T(8,128)(2,1)S(1)} %collective-permute-done.1.refs_1_.refs_2_), channel_id=1, source_target_pairs={{0,2},{2,0},{4,6},{6,4},{8,10},{10,8},{12,14},{14,12},{1,3},{3,1},... | collective-permute-start | bytes 786440 | tf_op jit(solution)/shard_map/ppermute | solution.py:254
  40.0 2.0 %collective-permute-done.2.refs_2_.refs_3_ = bf16[64,2048]{1,0:T(8,128)(2,1)S(1)} collective-permute-done((bf16[64,2048]{1,0:T(8,128)(2,1)}, bf16[64,2048]{1,0:T(8,128)(2,1)S(1)}, u32[]{:S(2)}, u32[]{:S(2)}) %collective-permute-start.2) | collective-permute-done | bytes 262176 | tf_op jit(solution)/shard_map/ppermute | solution.py:257
  42.1 2.5 %collective-permute-start.12 = (bf16[64,2048]{1,0:T(8,128)(2,1)S(1)}, bf16[64,2048]{1,0:T(8,128)(2,1)S(1)}, u32[]{:S(2)}, u32[]{:S(2)}) collective-permute-start(bf16[64,2048]{1,0:T(8,128)(2,1)S(1)} %collective-permute-done.2.refs_2_.refs_3_), channel_id=1, source_target_pairs={{0,2},{2,0},{4,6},{6,4},{8,10},{10,8},{12,14},{14,12},{1,3},{3,1},... | collective-permute-start | bytes 786440 | tf_op jit(solution)/shard_map/ppermute | solution.py:254
  45.6 7.1 %shard_map.67.refs_9_ = bf16[512,2048]{1,0:T(8,128)(2,1)S(1)} custom-call(bf16[64,2048]{1,0:T(8,128)(2,1)S(1)} %copy-done.1, bf16[64,2048]{1,0:T(8,128)(2,1)S(1)} %collective-permute-done.3.refs_1_.refs_2_, bf16[64,2048]{1,0:T(8,128)(2,1)S(1)} %collective-permute-done.4.refs_2_.refs_3_, bf16[64,2048]{1,0:T(8,128)(2,1)S(1)} %collective-permute-done.refs_3_.refs_4_, ...), custom_call_target="tpu_custom_call" | custom-call | flops 214748368 | bytes 629145 | tf_op jit(solution)/shard_map/pallas_call | solution.py:51
  54.7 7.1 %shard_map.68.refs_9_ = bf16[512,2048]{1,0:T(8,128)(2,1)S(1)} custom-call(bf16[64,2048]{1,0:T(8,128)(2,1)S(1)} %copy-done.1, bf16[64,2048]{1,0:T(8,128)(2,1)S(1)} %collective-permute-done.3.refs_1_.refs_2_, bf16[64,2048]{1,0:T(8,128)(2,1)S(1)} %collective-permute-done.4.refs_2_.refs_3_, bf16[64,2048]{1,0:T(8,128)(2,1)S(1)} %collective-permute-done.refs_3_.refs_4_, ...), custom_call_target="tpu_custom_call" | custom-call | flops 21474836480 | bytes 62914560 | tf_op jit(solution)/shard_map/pallas_call | solution.py:51
  62.0 9.1 %shard_map.69 = (bf16[512,2048]{1,0:T(8,128)(2,1)S(1)}, bf16[512,2048]{1,0:T(8,128)(2,1)S(1)}) custom-call(bf16[64,2048]{1,0:T(8,128)(2,1)S(1)} %copy-done, bf16[64,2048]{1,0:T(8,128)(2,1)S(1)} %collective-permute-done.1.refs_1_.refs_2_, bf16[64,2048]{1,0:T(8,128)(2,1)S(1)} %collective-permute-done.2.refs_2_.refs_3_, ...), custom_call_target="tpu_custom_call" | custom-call | flops 21474836480 | bytes 94371840 | tf_op jit(solution)/shard_map/pallas_call | solution.py:51
  71.6 9.1 %shard_map.70 = (bf16[512,2048]{1,0:T(8,128)(2,1)S(1)}, bf16[512,2048]{1,0:T(8,128)(2,1)S(1)}) custom-call(bf16[64,2048]{1,0:T(8,128)(2,1)S(1)} %copy-done, bf16[64,2048]{1,0:T(8,128)(2,1)S(1)} %collective-permute-done.1.refs_1_.refs_2_, bf16[64,2048]{1,0:T(8,128)(2,1)S(1)} %collective-permute-done.2.refs_2_.refs_3_, ...), custom_call_target="tpu_custom_call" | custom-call | flops 214748368 | bytes 943718 | tf_op jit(solution)/shard_map/pallas_call | solution.py:51
  80.8 6.7 %shard_map.71.refs_9_ = bf16[4096,2048]{1,0:T(8,128)(2,1)} custom-call(bf16[512,2048]{1,0:T(8,128)(2,1)S(1)} %get-tuple-element.50.refs_0_, bf16[64,2048]{1,0:T(8,128)(2,1)S(1)} %copy-done, bf16[64,2048]{1,0:T(8,128)(2,1)S(1)} %collective-permute-done.1.refs_1_.refs_2_, bf16[64,2048]{1,0:T(8,128)(2,1)S(1)} %collective-permute-done.2.refs_2_.refs_3_, ...), custom_call_target="tpu_custom_call" | custom-call | flops 214748368 | bytes 629145 | tf_op jit(solution)/shard_map/pallas_call | solution.py:196
  87.5 8.1 %shard_map.72 = (f32[256,1024]{1,0:T(8,128)S(1)}, bf16[256,1024]{1,0:T(8,128)(2,1)S(1)}, bf16[512,4096]{1,0:T(8,128)(2,1)S(1)}) custom-call(bf16[512,2048]{1,0:T(8,128)(2,1)S(1)} %get-tuple-element.51.refs_0_, bf16[512,2048]{1,0:T(8,128)(2,1)S(1)} %get-tuple-element.49.refs_1_, bf16[512,2048]{1,0:T(8,128)(2,1)S(1)} %collective-permute-done.16.refs_2_, ...), custom_call_target="tpu_custom_call" | custom-call | flops 214748368 | bytes 838860 | tf_op jit(solution)/shard_map/pallas_call | solution.py:51
  96.7 7.2 %shard_map.73 = (f32[256,1024]{1,0:T(8,128)S(1)}, bf16[256,1024]{1,0:T(8,128)(2,1)S(1)}) custom-call(bf16[512,4096]{1,0:T(8,128)(2,1)S(1)} %get-tuple-element.66.refs_0_, bf16[2048,4096]{1,0:T(8,128)(2,1)} %refs_1_.6), custom_call_target="tpu_custom_call" | custom-call | flops 214748368 | bytes 838860 | tf_op jit(solution)/shard_map/pallas_call | solution.py:51
  105.0 6.7 %shard_map.74 = bf16[4096,2048]{1,0:T(8,128)(2,1)} custom-call(bf16[512,2048]{1,0:T(8,128)(2,1)S(1)} %get-tuple-element.58.refs_0_, bf16[64,2048]{1,0:T(8,128)(2,1)S(1)} %copy-done, bf16[64,2048]{1,0:T(8,128)(2,1)S(1)} %collective-permute-done.1.refs_1_.refs_2_, ...), custom_call_target="tpu_custom_call", output_to_operand_aliasing={{}: (9, {})} | custom-call | flops 214748368 | bytes 629145 | tf_op jit(solution)/shard_map/pallas_call | solution.py:196
  112.0 4.1 %collective-permute-start.22 = (bf16[64,1024]{1,0:T(8,128)(2,1)S(1)}, bf16[64,1024]{1,0:T(8,128)(2,1)S(1)}, u32[]{:S(2)}, u32[]{:S(2)}) collective-permute-start(bf16[64,1024]{1,0:T(8,128)(2,1)S(1)} %get-tuple-element.76), channel_id=1, source_target_pairs={{0,8},{2,10},{4,12},{6,14},{8,0},{10,2},{12,4},{14,6},{1,9},{3,11}... | collective-permute-start | bytes 393224 | tf_op jit(solution)/shard_map/ppermute | solution.py:257
  116.2 3.7 %collective-permute-start.20 = (bf16[64,1024]{1,0:T(8,128)(2,1)S(1)}, bf16[64,1024]{1,0:T(8,128)(2,1)S(1)}, u32[]{:S(2)}, u32[]{:S(2)}) collective-permute-start(bf16[64,1024]{1,0:T(8,128)(2,1)S(1)} %get-tuple-element.78), channel_id=1, source_target_pairs={{0,12},{2,14},{4,0},{6,2},{8,4},{10,6},{12,8},{14,10},{1,13},{3,15... | collective-permute-start | bytes 393224 | tf_op jit(solution)/shard_map/ppermute | solution.py:257
  119.9 6.7 %shard_map.75.refs_9_ = bf16[2048,4096]{1,0:T(8,128)(2,1)} custom-call(bf16[512,4096]{1,0:T(8,128)(2,1)S(1)} %get-tuple-element.66.refs_0_, bf16[64,2048]{1,0:T(8,128)(2,1)S(1)} %copy-done.2, bf16[64,2048]{1,0:T(8,128)(2,1)S(1)} %collective-permute-done.3.refs_1_.refs_2_, bf16[64,2048]{1,0:T(8,128)(2,1)S(1)} %collective-permute-done.4.refs_2_.refs_3_, ...), custom_call_target="tpu_custom_call" | custom-call | flops 214748368 | bytes 629145 | tf_op jit(solution)/shard_map/pallas_call | solution.py:226
  128.2 2.7 %collective-permute-start.23 = (bf16[64,1024]{1,0:T(8,128)(2,1)S(1)}, bf16[64,1024]{1,0:T(8,128)(2,1)S(1)}, u32[]{:S(2)}, u32[]{:S(2)}) collective-permute-start(bf16[64,1024]{1,0:T(8,128)(2,1)S(1)} %get-tuple-element.65), channel_id=1, source_target_pairs={{0,12},{2,14},{4,0},{6,2},{8,4},{10,6},{12,8},{14,10},{1,13},{3,15... | collective-permute-start | bytes 393224 | tf_op jit(solution)/shard_map/ppermute | solution.py:257
  130.9 6.7 %shard_map.76 = bf16[2048,4096]{1,0:T(8,128)(2,1)} custom-call(bf16[512,4096]{1,0:T(8,128)(2,1)S(1)} %get-tuple-element.66.refs_0_, bf16[64,2048]{1,0:T(8,128)(2,1)S(1)} %copy-done.2, bf16[64,2048]{1,0:T(8,128)(2,1)S(1)} %collective-permute-done.3.refs_1_.refs_2_, ...), custom_call_target="tpu_custom_call", output_to_operand_aliasing={{}: (9, {})} | custom-call | flops 214748368 | bytes 629145 | tf_op jit(solution)/shard_map/pallas_call | solution.py:226
  (53 shorter events, 14.7 us)
Async XLA Ops:
  0.6 12.6 %collective-permute-start.3 = (bf16[64,2048]{1,0:T(8,128)(2,1)}, bf16[64,2048]{1,0:T(8,128)(2,1)S(1)}, u32[]{:S(2)}, u32[]{:S(2)}) collective-permute-start(bf16[64,2048]{1,0:T(8,128)(2,1)} %refs_1_.9), channel_id=1, source_target_pairs={{0,4},{2,6},{4,8},{6,10},{8,12},{10,14},{12,0},{14,2},{1,5},{3,7},... | collective-permute-start | bytes 786440 | tf_op jit(solution)/shard_map/ppermute | solution.py:257
  3.7 11.3 %collective-permute-start.5 = (bf16[64,2048]{1,0:T(8,128)(2,1)}, bf16[64,2048]{1,0:T(8,128)(2,1)S(1)}, u32[]{:S(2)}, u32[]{:S(2)}) collective-permute-start(bf16[64,2048]{1,0:T(8,128)(2,1)} %refs_1_.9), channel_id=1, source_target_pairs={{0,2},{2,0},{4,6},{6,4},{8,10},{10,8},{12,14},{14,12},{1,3},{3,1},... | collective-permute-start | bytes 786440 | tf_op jit(solution)/shard_map/ppermute | solution.py:254
  5.2 18.4 %collective-permute-start = (bf16[64,2048]{1,0:T(8,128)(2,1)}, bf16[64,2048]{1,0:T(8,128)(2,1)S(1)}, u32[]{:S(2)}, u32[]{:S(2)}) collective-permute-start(bf16[64,2048]{1,0:T(8,128)(2,1)} %refs_1_.9), channel_id=1, source_target_pairs={{0,8},{2,10},{4,12},{6,14},{8,0},{10,2},{12,4},{14,6},{1,9},{3,11}... | collective-permute-start | bytes 786440 | tf_op jit(solution)/shard_map/ppermute | solution.py:257
  7.8 20.5 %collective-permute-start.4 = (bf16[64,2048]{1,0:T(8,128)(2,1)}, bf16[64,2048]{1,0:T(8,128)(2,1)S(1)}, u32[]{:S(2)}, u32[]{:S(2)}) collective-permute-start(bf16[64,2048]{1,0:T(8,128)(2,1)} %refs_1_.9), channel_id=1, source_target_pairs={{0,12},{2,14},{4,0},{6,2},{8,4},{10,6},{12,8},{14,10},{1,13},{3,15... | collective-permute-start | bytes 786440 | tf_op jit(solution)/shard_map/ppermute | solution.py:257
  13.2 15.1 %collective-permute-start.6 = (bf16[64,2048]{1,0:T(8,128)(2,1)S(1)}, bf16[64,2048]{1,0:T(8,128)(2,1)S(1)}, u32[]{:S(2)}, u32[]{:S(2)}) collective-permute-start(bf16[64,2048]{1,0:T(8,128)(2,1)S(1)} %collective-permute-done.3.refs_1_.refs_2_), channel_id=1, source_target_pairs={{0,2},{2,0},{4,6},{6,4},{8,10},{10,8},{12,14},{14,12},{1,3},{3,1},... | collective-permute-start | bytes 786440 | tf_op jit(solution)/shard_map/ppermute | solution.py:254
  15.0 17.6 %collective-permute-start.8 = (bf16[64,2048]{1,0:T(8,128)(2,1)}, bf16[64,2048]{1,0:T(8,128)(2,1)S(1)}, u32[]{:S(2)}, u32[]{:S(2)}) collective-permute-start(bf16[64,2048]{1,0:T(8,128)(2,1)} %refs_1_.7), channel_id=1, source_target_pairs={{0,2},{2,0},{4,6},{6,4},{8,10},{10,8},{12,14},{14,12},{1,3},{3,1},... | collective-permute-start | bytes 786440 | tf_op jit(solution)/shard_map/ppermute | solution.py:254
  23.6 14.8 %collective-permute-start.1 = (bf16[64,2048]{1,0:T(8,128)(2,1)}, bf16[64,2048]{1,0:T(8,128)(2,1)S(1)}, u32[]{:S(2)}, u32[]{:S(2)}) collective-permute-start(bf16[64,2048]{1,0:T(8,128)(2,1)} %refs_1_.7), channel_id=1, source_target_pairs={{0,4},{2,6},{4,8},{6,10},{8,12},{10,14},{12,0},{14,2},{1,5},{3,7},... | collective-permute-start | bytes 786440 | tf_op jit(solution)/shard_map/ppermute | solution.py:257
  28.3 10.1 %collective-permute-start.7 = (bf16[64,2048]{1,0:T(8,128)(2,1)S(1)}, bf16[64,2048]{1,0:T(8,128)(2,1)S(1)}, u32[]{:S(2)}, u32[]{:S(2)}) collective-permute-start(bf16[64,2048]{1,0:T(8,128)(2,1)S(1)} %collective-permute-done.4.refs_2_.refs_3_), channel_id=1, source_target_pairs={{0,2},{2,0},{4,6},{6,4},{8,10},{10,8},{12,14},{14,12},{1,3},{3,1},... | collective-permute-start | bytes 786440 | tf_op jit(solution)/shard_map/ppermute | solution.py:254
  29.8 12.2 %collective-permute-start.2 = (bf16[64,2048]{1,0:T(8,128)(2,1)}, bf16[64,2048]{1,0:T(8,128)(2,1)S(1)}, u32[]{:S(2)}, u32[]{:S(2)}) collective-permute-start(bf16[64,2048]{1,0:T(8,128)(2,1)} %refs_1_.7), channel_id=1, source_target_pairs={{0,12},{2,14},{4,0},{6,2},{8,4},{10,6},{12,8},{14,10},{1,13},{3,15... | collective-permute-start | bytes 786440 | tf_op jit(solution)/shard_map/ppermute | solution.py:257
  32.6 9.6 %collective-permute-start.9 = (bf16[64,2048]{1,0:T(8,128)(2,1)S(1)}, bf16[64,2048]{1,0:T(8,128)(2,1)S(1)}, u32[]{:S(2)}, u32[]{:S(2)}) collective-permute-start(bf16[64,2048]{1,0:T(8,128)(2,1)S(1)} %collective-permute-done.refs_3_.refs_4_), channel_id=1, source_target_pairs={{0,2},{2,0},{4,6},{6,4},{8,10},{10,8},{12,14},{14,12},{1,3},{3,1},... | collective-permute-start | bytes 786440 | tf_op jit(solution)/shard_map/ppermute | solution.py:254
  33.1 20.1 %collective-permute-start.10 = (bf16[64,2048]{1,0:T(8,128)(2,1)}, bf16[64,2048]{1,0:T(8,128)(2,1)S(1)}, u32[]{:S(2)}, u32[]{:S(2)}) collective-permute-start(bf16[64,2048]{1,0:T(8,128)(2,1)} %refs_1_.7), channel_id=1, source_target_pairs={{0,8},{2,10},{4,12},{6,14},{8,0},{10,2},{12,4},{14,6},{1,9},{3,11}... | collective-permute-start | bytes 786440 | tf_op jit(solution)/shard_map/ppermute | solution.py:257
  38.4 14.8 %collective-permute-start.11 = (bf16[64,2048]{1,0:T(8,128)(2,1)S(1)}, bf16[64,2048]{1,0:T(8,128)(2,1)S(1)}, u32[]{:S(2)}, u32[]{:S(2)}) collective-permute-start(bf16[64,2048]{1,0:T(8,128)(2,1)S(1)} %collective-permute-done.1.refs_1_.refs_2_), channel_id=1, source_target_pairs={{0,2},{2,0},{4,6},{6,4},{8,10},{10,8},{12,14},{14,12},{1,3},{3,1},... | collective-permute-start | bytes 786440 | tf_op jit(solution)/shard_map/ppermute | solution.py:254
  42.1 12.6 %collective-permute-start.12 = (bf16[64,2048]{1,0:T(8,128)(2,1)S(1)}, bf16[64,2048]{1,0:T(8,128)(2,1)S(1)}, u32[]{:S(2)}, u32[]{:S(2)}) collective-permute-start(bf16[64,2048]{1,0:T(8,128)(2,1)S(1)} %collective-permute-done.2.refs_2_.refs_3_), channel_id=1, source_target_pairs={{0,2},{2,0},{4,6},{6,4},{8,10},{10,8},{12,14},{14,12},{1,3},{3,1},... | collective-permute-start | bytes 786440 | tf_op jit(solution)/shard_map/ppermute | solution.py:254
  52.7 9.3 %collective-permute-start.14 = (bf16[512,2048]{1,0:T(8,128)(2,1)S(1)}, bf16[512,2048]{1,0:T(8,128)(2,1)S(1)}, u32[]{:S(2)}, u32[]{:S(2)}) collective-permute-start(bf16[512,2048]{1,0:T(8,128)(2,1)S(1)} %shard_map.67.refs_9_), channel_id=1, source_target_pairs={{0,1},{1,0},{2,3},{3,2},{4,5},{5,4},{6,7},{7,6},{8,9},{9,8},{10,11... | collective-permute-start | bytes 6291464 | tf_op jit(solution)/shard_map/ppermute | solution.py:251
  61.9 9.8 %collective-permute-start.15 = (bf16[512,2048]{1,0:T(8,128)(2,1)S(1)}, bf16[512,2048]{1,0:T(8,128)(2,1)S(1)}, u32[]{:S(2)}, u32[]{:S(2)}) collective-permute-start(bf16[512,2048]{1,0:T(8,128)(2,1)S(1)} %shard_map.68.refs_9_), channel_id=1, source_target_pairs={{0,1},{1,0},{2,3},{3,2},{4,5},{5,4},{6,7},{7,6},{8,9},{9,8},{10,11... | collective-permute-start | bytes 6291464 | tf_op jit(solution)/shard_map/ppermute | solution.py:251
  71.1 16.4 %collective-permute-start.16 = (bf16[512,2048]{1,0:T(8,128)(2,1)S(1)}, bf16[512,2048]{1,0:T(8,128)(2,1)S(1)}, u32[]{:S(2)}, u32[]{:S(2)}) collective-permute-start(bf16[512,2048]{1,0:T(8,128)(2,1)S(1)} %get-tuple-element.51.refs_0_), channel_id=1, source_target_pairs={{0,1},{1,0},{2,3},{3,2},{4,5},{5,4},{6,7},{7,6},{8,9},{9,8},{10,11... | collective-permute-start | bytes 6291464 | tf_op jit(solution)/shard_map/ppermute | solution.py:251
  95.7 16.0 %collective-permute-start.18 = (bf16[256,1024]{1,0:T(8,128)(2,1)S(1)}, bf16[256,1024]{1,0:T(8,128)(2,1)S(1)}, u32[]{:S(2)}, u32[]{:S(2)}) collective-permute-start(bf16[256,1024]{1,0:T(8,128)(2,1)S(1)} %get-tuple-element.53), channel_id=1, source_target_pairs={{0,2},{2,0},{4,6},{6,4},{8,10},{10,8},{12,14},{14,12},{1,3},{3,1},... | collective-permute-start | bytes 1572872 | tf_op jit(solution)/shard_map/ppermute | solution.py:254
  103.9 22.7 %collective-permute-start.19 = (bf16[256,1024]{1,0:T(8,128)(2,1)S(1)}, bf16[256,1024]{1,0:T(8,128)(2,1)S(1)}, u32[]{:S(2)}, u32[]{:S(2)}) collective-permute-start(bf16[256,1024]{1,0:T(8,128)(2,1)S(1)} %get-tuple-element.61), channel_id=1, source_target_pairs={{0,2},{2,0},{4,6},{6,4},{8,10},{10,8},{12,14},{14,12},{1,3},{3,1},... | collective-permute-start | bytes 1572872 | tf_op jit(solution)/shard_map/ppermute | solution.py:254
  112.0 25.7 %collective-permute-start.22 = (bf16[64,1024]{1,0:T(8,128)(2,1)S(1)}, bf16[64,1024]{1,0:T(8,128)(2,1)S(1)}, u32[]{:S(2)}, u32[]{:S(2)}) collective-permute-start(bf16[64,1024]{1,0:T(8,128)(2,1)S(1)} %get-tuple-element.76), channel_id=1, source_target_pairs={{0,8},{2,10},{4,12},{6,14},{8,0},{10,2},{12,4},{14,6},{1,9},{3,11}... | collective-permute-start | bytes 393224 | tf_op jit(solution)/shard_map/ppermute | solution.py:257
  116.1 21.5 %collective-permute-start.21 = (bf16[64,1024]{1,0:T(8,128)(2,1)S(1)}, bf16[64,1024]{1,0:T(8,128)(2,1)S(1)}, u32[]{:S(2)}, u32[]{:S(2)}) collective-permute-start(bf16[64,1024]{1,0:T(8,128)(2,1)S(1)} %get-tuple-element.77), channel_id=1, source_target_pairs={{0,4},{2,6},{4,8},{6,10},{8,12},{10,14},{12,0},{14,2},{1,5},{3,7},... | collective-permute-start | bytes 393224 | tf_op jit(solution)/shard_map/ppermute | solution.py:257
  116.2 12.0 %collective-permute-start.20 = (bf16[64,1024]{1,0:T(8,128)(2,1)S(1)}, bf16[64,1024]{1,0:T(8,128)(2,1)S(1)}, u32[]{:S(2)}, u32[]{:S(2)}) collective-permute-start(bf16[64,1024]{1,0:T(8,128)(2,1)S(1)} %get-tuple-element.78), channel_id=1, source_target_pairs={{0,12},{2,14},{4,0},{6,2},{8,4},{10,6},{12,8},{14,10},{1,13},{3,15... | collective-permute-start | bytes 393224 | tf_op jit(solution)/shard_map/ppermute | solution.py:257
  126.9 10.8 %collective-permute-start.25 = (bf16[64,1024]{1,0:T(8,128)(2,1)S(1)}, bf16[64,1024]{1,0:T(8,128)(2,1)S(1)}, u32[]{:S(2)}, u32[]{:S(2)}) collective-permute-start(bf16[64,1024]{1,0:T(8,128)(2,1)S(1)} %get-tuple-element.74), channel_id=1, source_target_pairs={{0,8},{2,10},{4,12},{6,14},{8,0},{10,2},{12,4},{14,6},{1,9},{3,11}... | collective-permute-start | bytes 393224 | tf_op jit(solution)/shard_map/ppermute | solution.py:257
  127.0 10.7 %collective-permute-start.24 = (bf16[64,1024]{1,0:T(8,128)(2,1)S(1)}, bf16[64,1024]{1,0:T(8,128)(2,1)S(1)}, u32[]{:S(2)}, u32[]{:S(2)}) collective-permute-start(bf16[64,1024]{1,0:T(8,128)(2,1)S(1)} %get-tuple-element.75), channel_id=1, source_target_pairs={{0,4},{2,6},{4,8},{6,10},{8,12},{10,14},{12,0},{14,2},{1,5},{3,7},... | collective-permute-start | bytes 393224 | tf_op jit(solution)/shard_map/ppermute | solution.py:257
  128.2 9.7 %collective-permute-start.23 = (bf16[64,1024]{1,0:T(8,128)(2,1)S(1)}, bf16[64,1024]{1,0:T(8,128)(2,1)S(1)}, u32[]{:S(2)}, u32[]{:S(2)}) collective-permute-start(bf16[64,1024]{1,0:T(8,128)(2,1)S(1)} %get-tuple-element.65), channel_id=1, source_target_pairs={{0,12},{2,14},{4,0},{6,2},{8,4},{10,6},{12,8},{14,10},{1,13},{3,15... | collective-permute-start | bytes 393224 | tf_op jit(solution)/shard_map/ppermute | solution.py:257
  (5 other events, 33.9 us)

commit v4 on v3

--- a/solution.py
+++ b/solution.py
@@ -9,7 +9,6 @@
 
 F32 = jnp.float32
 BF16 = jnp.bfloat16
-VMEM_LIMIT = 36 * 1024 * 1024
 NX = 2
 PARTS = 2
 SPLITS = 2
@@ -17,7 +16,7 @@
 X_AHEAD = 2
 PRE_TILE = 512
 BACK_TILE = 512
-IN_TILE = 256
+IN_TILE = 512
 NT = (((1,), (1,)), ((), ()))
 TN = (((0,), (0,)), ((), ()))
 
@@ -31,8 +30,8 @@
     return (preact * gate, factor)
 
 
-def params():
-    return pltpu.CompilerParams(vmem_limit_bytes=VMEM_LIMIT)
+def params(mib=36):
+    return pltpu.CompilerParams(vmem_limit_bytes=mib * 1024 * 1024)
 
 
 def cost(flops, moved, weight=1):
@@ -47,7 +46,9 @@
     return jnp.concatenate([r[...] for r in refs], axis=0)
 
 
-def call(kernel, steps, in_specs, out_specs, out_shape, estimate, args, scratch=()):
+def call(
+    kernel, steps, in_specs, out_specs, out_shape, estimate, args, scratch=(), mib=36
+):
     return pl.pallas_call(
         kernel,
         grid=(steps,),
@@ -55,7 +56,7 @@
         out_specs=out_specs,
         out_shape=out_shape,
         scratch_shapes=list(scratch),
-        compiler_params=params(),
+        compiler_params=params(mib),
         cost_estimate=estimate,
     )(*args)
 
@@ -176,6 +177,7 @@
         out_shape,
         cost(2 * m * hidden * count, 2 * count * hidden + 4 * m * hidden),
         (*deltas, up),
+        mib=24,
     )
     return got if parts else (*got, deltas[0])
 
@@ -202,9 +204,11 @@
         out_specs=pl.BlockSpec((tile, feats), lambda i: (part * steps + i, 0)),
         out_shape=jax.ShapeDtypeStruct((parts * each, feats), BF16),
         input_output_aliases={1 + n: 0} if extra else {},
-        compiler_params=params(),
+        compiler_params=params(20),
         cost_estimate=cost(
-            2 * m * each * feats, 2 * each * feats + 2 * m * (each + feats)
+            2 * m * each * feats,
+            2 * each * feats + 2 * m * (each + feats),
+            60 if into is None else 1,
         ),
     )(act, *cots, *extra)
 
@@ -232,7 +236,7 @@
         out_specs=pl.BlockSpec((feats, tile), lambda i: (0, part * steps + i)),
         out_shape=jax.ShapeDtypeStruct((feats, hidden), BF16),
         input_output_aliases={1 + n: 0} if extra else {},
-        compiler_params=params(),
+        compiler_params=params(36),
         cost_estimate=cost(
             2 * m * each * feats, 2 * each * feats + 2 * m * (each + feats)
         ),

time: 139 us -> 137 us (0.986)
  Pallas kernels: 74.5 us -> 69.8 us
  local copies, waits for them, and re-layouts: 1.06 us -> 3.23 us
    pallas_call x6, Pallas kernels: 47.7 us -> 43 us  [call(): pl.pallas_call(kernel, grid=(steps,), in_specs=in_specs, out_specs=out_sp...]
    unnamed x6 -> x14, local copies, waits for them, and re-layouts: 0.96 us -> 3.13 us
  transfers between devices with their start and end apart: 26 -> 26, of which waited for: 7 -> 8; matrix products, arithmetic and copies ran while one was open for 0% -> 0% of each run, Pallas kernels for 48% -> 47%
where the time goes in v4:
time: 137 us
  Pallas kernels  69.8 us (51%)
  starting transfers between devices  45.3 us (33%)
  waiting for transfers between devices  16.8 us (12%)
  local copies, waits for them, and re-layouts  3.23 us (2%)
    pallas_call x6, Pallas kernels, call(): pl.pallas_call(kernel, grid=(steps,), in_specs=in_specs, out_specs=out_sp...  43 us
    ppermute x12, starting transfers between devices, shift(): return lax.ppermute(x, 'row', [(r, (r + k * NX) % row) for r in range(row)])  31.3 us
    ppermute x12, waiting for transfers between devices, shift(): return lax.ppermute(x, 'row', [(r, (r + k * NX) % row) for r in range(row)])  15.5 us
    pallas_call x2, Pallas kernels, up_pass(): pl.pallas_call(kernel, grid=(steps,), in_specs=[pl.BlockSpec((m, tile), l...  13.4 us
    pallas_call x2, Pallas kernels, down_pass(): pl.pallas_call(kernel, grid=(steps,), in_specs=[pl.BlockSpec((m, tile), l...  13.4 us
    ppermute x10, starting transfers between devices, across(): return lax.ppermute(x, 'row', [(r, r ^ 1) for r in range(row)])  13.2 us
    unnamed x14, local copies, waits for them, and re-layouts  3.13 us
  transfers between devices with their start and end apart: 26, of which 8 were waited for; matrix products, arithmetic and copies ran while one was open for 0% of the time, Pallas kernels for 47%

profile of v4, /device:TPU:0, one launch (start us, length us, event | category | flops | bytes accessed | tf_op | source)
XLA Modules:
  0.0 137.2 jit_solution(10140016313724315640)
XLA Ops:
  0.6 3.1 %collective-permute-start.3 = (bf16[64,2048]{1,0:T(8,128)(2,1)}, bf16[64,2048]{1,0:T(8,128)(2,1)S(1)}, u32[]{:S(2)}, u32[]{:S(2)}) collective-permute-start(bf16[64,2048]{1,0:T(8,128)(2,1)} %refs_1_.9), channel_id=1, source_target_pairs={{0,4},{2,6},{4,8},{6,10},{8,12},{10,14},{12,0},{14,2},{1,5},{3,7},... | collective-permute-start | bytes 786440 | tf_op jit(solution)/shard_map/ppermute | solution.py:261
  5.2 2.6 %collective-permute-start = (bf16[64,2048]{1,0:T(8,128)(2,1)}, bf16[64,2048]{1,0:T(8,128)(2,1)S(1)}, u32[]{:S(2)}, u32[]{:S(2)}) collective-permute-start(bf16[64,2048]{1,0:T(8,128)(2,1)} %refs_1_.9), channel_id=1, source_target_pairs={{0,8},{2,10},{4,12},{6,14},{8,0},{10,2},{12,4},{14,6},{1,9},{3,11}... | collective-permute-start | bytes 786440 | tf_op jit(solution)/shard_map/ppermute | solution.py:261
  9.1 4.1 %collective-permute-done.3.refs_1_.refs_2_ = bf16[64,2048]{1,0:T(8,128)(2,1)S(1)} collective-permute-done((bf16[64,2048]{1,0:T(8,128)(2,1)}, bf16[64,2048]{1,0:T(8,128)(2,1)S(1)}, u32[]{:S(2)}, u32[]{:S(2)}) %collective-permute-start.3) | collective-permute-done | bytes 262176 | tf_op jit(solution)/shard_map/ppermute | solution.py:261
  13.2 1.7 %collective-permute-start.6 = (bf16[64,2048]{1,0:T(8,128)(2,1)S(1)}, bf16[64,2048]{1,0:T(8,128)(2,1)S(1)}, u32[]{:S(2)}, u32[]{:S(2)}) collective-permute-start(bf16[64,2048]{1,0:T(8,128)(2,1)S(1)} %collective-permute-done.3.refs_1_.refs_2_), channel_id=1, source_target_pairs={{0,2},{2,0},{4,6},{6,4},{8,10},{10,8},{12,14},{14,12},{1,3},{3,1},... | collective-permute-start | bytes 786440 | tf_op jit(solution)/shard_map/ppermute | solution.py:258
  15.3 8.4 %collective-permute-done.refs_3_.refs_4_ = bf16[64,2048]{1,0:T(8,128)(2,1)S(1)} collective-permute-done((bf16[64,2048]{1,0:T(8,128)(2,1)}, bf16[64,2048]{1,0:T(8,128)(2,1)S(1)}, u32[]{:S(2)}, u32[]{:S(2)}) %collective-permute-start) | collective-permute-done | bytes 262176 | tf_op jit(solution)/shard_map/ppermute | solution.py:261
  23.6 4.7 %collective-permute-start.1 = (bf16[64,2048]{1,0:T(8,128)(2,1)}, bf16[64,2048]{1,0:T(8,128)(2,1)S(1)}, u32[]{:S(2)}, u32[]{:S(2)}) collective-permute-start(bf16[64,2048]{1,0:T(8,128)(2,1)} %refs_1_.7), channel_id=1, source_target_pairs={{0,4},{2,6},{4,8},{6,10},{8,12},{10,14},{12,0},{14,2},{1,5},{3,7},... | collective-permute-start | bytes 786440 | tf_op jit(solution)/shard_map/ppermute | solution.py:261
  29.8 2.8 %collective-permute-start.2 = (bf16[64,2048]{1,0:T(8,128)(2,1)}, bf16[64,2048]{1,0:T(8,128)(2,1)S(1)}, u32[]{:S(2)}, u32[]{:S(2)}) collective-permute-start(bf16[64,2048]{1,0:T(8,128)(2,1)} %refs_1_.7), channel_id=1, source_target_pairs={{0,12},{2,14},{4,0},{6,2},{8,4},{10,6},{12,8},{14,10},{1,13},{3,15... | collective-permute-start | bytes 786440 | tf_op jit(solution)/shard_map/ppermute | solution.py:261
  33.1 4.8 %collective-permute-start.10 = (bf16[64,2048]{1,0:T(8,128)(2,1)}, bf16[64,2048]{1,0:T(8,128)(2,1)S(1)}, u32[]{:S(2)}, u32[]{:S(2)}) collective-permute-start(bf16[64,2048]{1,0:T(8,128)(2,1)} %refs_1_.7), channel_id=1, source_target_pairs={{0,8},{2,10},{4,12},{6,14},{8,0},{10,2},{12,4},{14,6},{1,9},{3,11}... | collective-permute-start | bytes 786440 | tf_op jit(solution)/shard_map/ppermute | solution.py:261
  38.4 1.5 %collective-permute-start.11 = (bf16[64,2048]{1,0:T(8,128)(2,1)S(1)}, bf16[64,2048]{1,0:T(8,128)(2,1)S(1)}, u32[]{:S(2)}, u32[]{:S(2)}) collective-permute-start(bf16[64,2048]{1,0:T(8,128)(2,1)S(1)} %collective-permute-done.1.refs_1_.refs_2_), channel_id=1, source_target_pairs={{0,2},{2,0},{4,6},{6,4},{8,10},{10,8},{12,14},{14,12},{1,3},{3,1},... | collective-permute-start | bytes 786440 | tf_op jit(solution)/shard_map/ppermute | solution.py:258
  40.0 2.0 %collective-permute-done.2.refs_2_.refs_3_ = bf16[64,2048]{1,0:T(8,128)(2,1)S(1)} collective-permute-done((bf16[64,2048]{1,0:T(8,128)(2,1)}, bf16[64,2048]{1,0:T(8,128)(2,1)S(1)}, u32[]{:S(2)}, u32[]{:S(2)}) %collective-permute-start.2) | collective-permute-done | bytes 262176 | tf_op jit(solution)/shard_map/ppermute | solution.py:261
  42.1 2.5 %collective-permute-start.12 = (bf16[64,2048]{1,0:T(8,128)(2,1)S(1)}, bf16[64,2048]{1,0:T(8,128)(2,1)S(1)}, u32[]{:S(2)}, u32[]{:S(2)}) collective-permute-start(bf16[64,2048]{1,0:T(8,128)(2,1)S(1)} %collective-permute-done.2.refs_2_.refs_3_), channel_id=1, source_target_pairs={{0,2},{2,0},{4,6},{6,4},{8,10},{10,8},{12,14},{14,12},{1,3},{3,1},... | collective-permute-start | bytes 786440 | tf_op jit(solution)/shard_map/ppermute | solution.py:258
  45.6 7.1 %shard_map.67.refs_9_ = bf16[512,2048]{1,0:T(8,128)(2,1)S(1)} custom-call(bf16[64,2048]{1,0:T(8,128)(2,1)S(1)} %copy-done, bf16[64,2048]{1,0:T(8,128)(2,1)S(1)} %collective-permute-done.3.refs_1_.refs_2_, bf16[64,2048]{1,0:T(8,128)(2,1)S(1)} %collective-permute-done.4.refs_2_.refs_3_, bf16[64,2048]{1,0:T(8,128)(2,1)S(1)} %collective-permute-done.refs_3_.refs_4_, ...), custom_call_target="tpu_custom_call" | custom-call | flops 214748368 | bytes 629145 | tf_op jit(solution)/shard_map/pallas_call | solution.py:52
  54.7 7.1 %shard_map.68.refs_9_ = bf16[512,2048]{1,0:T(8,128)(2,1)S(1)} custom-call(bf16[64,2048]{1,0:T(8,128)(2,1)S(1)} %copy-done, bf16[64,2048]{1,0:T(8,128)(2,1)S(1)} %collective-permute-done.3.refs_1_.refs_2_, bf16[64,2048]{1,0:T(8,128)(2,1)S(1)} %collective-permute-done.4.refs_2_.refs_3_, bf16[64,2048]{1,0:T(8,128)(2,1)S(1)} %collective-permute-done.refs_3_.refs_4_, ...), custom_call_target="tpu_custom_call" | custom-call | flops 21474836480 | bytes 62914560 | tf_op jit(solution)/shard_map/pallas_call | solution.py:52
  62.0 9.1 %shard_map.69 = (bf16[512,2048]{1,0:T(8,128)(2,1)S(1)}, bf16[512,2048]{1,0:T(8,128)(2,1)S(1)}) custom-call(bf16[64,2048]{1,0:T(8,128)(2,1)S(1)} %copy-done.2, bf16[64,2048]{1,0:T(8,128)(2,1)S(1)} %collective-permute-done.1.refs_1_.refs_2_, bf16[64,2048]{1,0:T(8,128)(2,1)S(1)} %collective-permute-done.2.refs_2_.refs_3_, ...), custom_call_target="tpu_custom_call" | custom-call | flops 21474836480 | bytes 94371840 | tf_op jit(solution)/shard_map/pallas_call | solution.py:52
  71.6 9.1 %shard_map.70 = (bf16[512,2048]{1,0:T(8,128)(2,1)S(1)}, bf16[512,2048]{1,0:T(8,128)(2,1)S(1)}) custom-call(bf16[64,2048]{1,0:T(8,128)(2,1)S(1)} %copy-done.2, bf16[64,2048]{1,0:T(8,128)(2,1)S(1)} %collective-permute-done.1.refs_1_.refs_2_, bf16[64,2048]{1,0:T(8,128)(2,1)S(1)} %collective-permute-done.2.refs_2_.refs_3_, ...), custom_call_target="tpu_custom_call" | custom-call | flops 214748368 | bytes 943718 | tf_op jit(solution)/shard_map/pallas_call | solution.py:52
  80.9 6.7 %shard_map.71.refs_9_ = bf16[4096,2048]{1,0:T(8,128)(2,1)} custom-call(bf16[512,2048]{1,0:T(8,128)(2,1)S(1)} %get-tuple-element.50.refs_0_, bf16[64,2048]{1,0:T(8,128)(2,1)S(1)} %copy-done.2, bf16[64,2048]{1,0:T(8,128)(2,1)S(1)} %collective-permute-done.1.refs_1_.refs_2_, bf16[64,2048]{1,0:T(8,128)(2,1)S(1)} %collective-permute-done.2.refs_2_.refs_3_, ...), custom_call_target="tpu_custom_call" | custom-call | flops 12884901888 | bytes 37748736 | tf_op jit(solution)/shard_map/pallas_call | solution.py:198
  89.7 5.8 %shard_map.72 = (f32[256,1024]{1,0:T(8,128)S(1)}, bf16[256,1024]{1,0:T(8,128)(2,1)S(1)}, bf16[512,4096]{1,0:T(8,128)(2,1)S(1)}) custom-call(bf16[512,2048]{1,0:T(8,128)(2,1)S(1)} %get-tuple-element.51.refs_0_, bf16[512,2048]{1,0:T(8,128)(2,1)S(1)} %get-tuple-element.49.refs_1_, bf16[512,2048]{1,0:T(8,128)(2,1)S(1)} %collective-permute-done.16.refs_2_, ...), custom_call_target="tpu_custom_call" | custom-call | flops 214748368 | bytes 838860 | tf_op jit(solution)/shard_map/pallas_call | solution.py:52
  96.5 4.8 %shard_map.73 = (f32[256,1024]{1,0:T(8,128)S(1)}, bf16[256,1024]{1,0:T(8,128)(2,1)S(1)}) custom-call(bf16[512,4096]{1,0:T(8,128)(2,1)S(1)} %get-tuple-element.66.refs_0_, bf16[2048,4096]{1,0:T(8,128)(2,1)S(1)} %bitcast.1), custom_call_target="tpu_custom_call" | custom-call | flops 214748368 | bytes 838860 | tf_op jit(solution)/shard_map/pallas_call | solution.py:52
  102.5 6.7 %shard_map.74 = bf16[4096,2048]{1,0:T(8,128)(2,1)} custom-call(bf16[512,2048]{1,0:T(8,128)(2,1)S(1)} %get-tuple-element.58.refs_0_, bf16[64,2048]{1,0:T(8,128)(2,1)S(1)} %copy-done.2, bf16[64,2048]{1,0:T(8,128)(2,1)S(1)} %collective-permute-done.1.refs_1_.refs_2_, ...), custom_call_target="tpu_custom_call", output_to_operand_aliasing={{}: (9, {})} | custom-call | flops 214748368 | bytes 629145 | tf_op jit(solution)/shard_map/pallas_call | solution.py:198
  110.6 4.2 %collective-permute-start.22 = (bf16[64,1024]{1,0:T(8,128)(2,1)S(1)}, bf16[64,1024]{1,0:T(8,128)(2,1)S(1)}, u32[]{:S(2)}, u32[]{:S(2)}) collective-permute-start(bf16[64,1024]{1,0:T(8,128)(2,1)S(1)} %get-tuple-element.76), channel_id=1, source_target_pairs={{0,8},{2,10},{4,12},{6,14},{8,0},{10,2},{12,4},{14,6},{1,9},{3,11}... | collective-permute-start | bytes 393224 | tf_op jit(solution)/shard_map/ppermute | solution.py:261
  115.0 3.5 %collective-permute-start.20 = (bf16[64,1024]{1,0:T(8,128)(2,1)S(1)}, bf16[64,1024]{1,0:T(8,128)(2,1)S(1)}, u32[]{:S(2)}, u32[]{:S(2)}) collective-permute-start(bf16[64,1024]{1,0:T(8,128)(2,1)S(1)} %get-tuple-element.78), channel_id=1, source_target_pairs={{0,12},{2,14},{4,0},{6,2},{8,4},{10,6},{12,8},{14,10},{1,13},{3,15... | collective-permute-start | bytes 393224 | tf_op jit(solution)/shard_map/ppermute | solution.py:261
  118.6 6.7 %shard_map.75.refs_9_ = bf16[2048,4096]{1,0:T(8,128)(2,1)} custom-call(bf16[512,4096]{1,0:T(8,128)(2,1)S(1)} %get-tuple-element.66.refs_0_, bf16[64,2048]{1,0:T(8,128)(2,1)S(1)} %copy-done.1, bf16[64,2048]{1,0:T(8,128)(2,1)S(1)} %collective-permute-done.3.refs_1_.refs_2_, bf16[64,2048]{1,0:T(8,128)(2,1)S(1)} %collective-permute-done.4.refs_2_.refs_3_, ...), custom_call_target="tpu_custom_call" | custom-call | flops 214748368 | bytes 629145 | tf_op jit(solution)/shard_map/pallas_call | solution.py:230
  126.8 2.8 %collective-permute-start.23 = (bf16[64,1024]{1,0:T(8,128)(2,1)S(1)}, bf16[64,1024]{1,0:T(8,128)(2,1)S(1)}, u32[]{:S(2)}, u32[]{:S(2)}) collective-permute-start(bf16[64,1024]{1,0:T(8,128)(2,1)S(1)} %get-tuple-element.65), channel_id=1, source_target_pairs={{0,12},{2,14},{4,0},{6,2},{8,4},{10,6},{12,8},{14,10},{1,13},{3,15... | collective-permute-start | bytes 393224 | tf_op jit(solution)/shard_map/ppermute | solution.py:261
  129.6 6.7 %shard_map.76 = bf16[2048,4096]{1,0:T(8,128)(2,1)} custom-call(bf16[512,4096]{1,0:T(8,128)(2,1)S(1)} %get-tuple-element.66.refs_0_, bf16[64,2048]{1,0:T(8,128)(2,1)S(1)} %copy-done.1, bf16[64,2048]{1,0:T(8,128)(2,1)S(1)} %collective-permute-done.3.refs_1_.refs_2_, ...), custom_call_target="tpu_custom_call", output_to_operand_aliasing={{}: (9, {})} | custom-call | flops 214748368 | bytes 629145 | tf_op jit(solution)/shard_map/pallas_call | solution.py:230
  (62 shorter events, 17.9 us)
Async XLA Ops:
  0.6 12.6 %collective-permute-start.3 = (bf16[64,2048]{1,0:T(8,128)(2,1)}, bf16[64,2048]{1,0:T(8,128)(2,1)S(1)}, u32[]{:S(2)}, u32[]{:S(2)}) collective-permute-start(bf16[64,2048]{1,0:T(8,128)(2,1)} %refs_1_.9), channel_id=1, source_target_pairs={{0,4},{2,6},{4,8},{6,10},{8,12},{10,14},{12,0},{14,2},{1,5},{3,7},... | collective-permute-start | bytes 786440 | tf_op jit(solution)/shard_map/ppermute | solution.py:261
  3.7 11.3 %collective-permute-start.5 = (bf16[64,2048]{1,0:T(8,128)(2,1)}, bf16[64,2048]{1,0:T(8,128)(2,1)S(1)}, u32[]{:S(2)}, u32[]{:S(2)}) collective-permute-start(bf16[64,2048]{1,0:T(8,128)(2,1)} %refs_1_.9), channel_id=1, source_target_pairs={{0,2},{2,0},{4,6},{6,4},{8,10},{10,8},{12,14},{14,12},{1,3},{3,1},... | collective-permute-start | bytes 786440 | tf_op jit(solution)/shard_map/ppermute | solution.py:258
  5.2 18.4 %collective-permute-start = (bf16[64,2048]{1,0:T(8,128)(2,1)}, bf16[64,2048]{1,0:T(8,128)(2,1)S(1)}, u32[]{:S(2)}, u32[]{:S(2)}) collective-permute-start(bf16[64,2048]{1,0:T(8,128)(2,1)} %refs_1_.9), channel_id=1, source_target_pairs={{0,8},{2,10},{4,12},{6,14},{8,0},{10,2},{12,4},{14,6},{1,9},{3,11}... | collective-permute-start | bytes 786440 | tf_op jit(solution)/shard_map/ppermute | solution.py:261
  7.8 20.5 %collective-permute-start.4 = (bf16[64,2048]{1,0:T(8,128)(2,1)}, bf16[64,2048]{1,0:T(8,128)(2,1)S(1)}, u32[]{:S(2)}, u32[]{:S(2)}) collective-permute-start(bf16[64,2048]{1,0:T(8,128)(2,1)} %refs_1_.9), channel_id=1, source_target_pairs={{0,12},{2,14},{4,0},{6,2},{8,4},{10,6},{12,8},{14,10},{1,13},{3,15... | collective-permute-start | bytes 786440 | tf_op jit(solution)/shard_map/ppermute | solution.py:261
  13.2 15.1 %collective-permute-start.6 = (bf16[64,2048]{1,0:T(8,128)(2,1)S(1)}, bf16[64,2048]{1,0:T(8,128)(2,1)S(1)}, u32[]{:S(2)}, u32[]{:S(2)}) collective-permute-start(bf16[64,2048]{1,0:T(8,128)(2,1)S(1)} %collective-permute-done.3.refs_1_.refs_2_), channel_id=1, source_target_pairs={{0,2},{2,0},{4,6},{6,4},{8,10},{10,8},{12,14},{14,12},{1,3},{3,1},... | collective-permute-start | bytes 786440 | tf_op jit(solution)/shard_map/ppermute | solution.py:258
  15.0 17.6 %collective-permute-start.8 = (bf16[64,2048]{1,0:T(8,128)(2,1)}, bf16[64,2048]{1,0:T(8,128)(2,1)S(1)}, u32[]{:S(2)}, u32[]{:S(2)}) collective-permute-start(bf16[64,2048]{1,0:T(8,128)(2,1)} %refs_1_.7), channel_id=1, source_target_pairs={{0,2},{2,0},{4,6},{6,4},{8,10},{10,8},{12,14},{14,12},{1,3},{3,1},... | collective-permute-start | bytes 786440 | tf_op jit(solution)/shard_map/ppermute | solution.py:258
  23.6 14.8 %collective-permute-start.1 = (bf16[64,2048]{1,0:T(8,128)(2,1)}, bf16[64,2048]{1,0:T(8,128)(2,1)S(1)}, u32[]{:S(2)}, u32[]{:S(2)}) collective-permute-start(bf16[64,2048]{1,0:T(8,128)(2,1)} %refs_1_.7), channel_id=1, source_target_pairs={{0,4},{2,6},{4,8},{6,10},{8,12},{10,14},{12,0},{14,2},{1,5},{3,7},... | collective-permute-start | bytes 786440 | tf_op jit(solution)/shard_map/ppermute | solution.py:261
  28.3 10.1 %collective-permute-start.7 = (bf16[64,2048]{1,0:T(8,128)(2,1)S(1)}, bf16[64,2048]{1,0:T(8,128)(2,1)S(1)}, u32[]{:S(2)}, u32[]{:S(2)}) collective-permute-start(bf16[64,2048]{1,0:T(8,128)(2,1)S(1)} %collective-permute-done.4.refs_2_.refs_3_), channel_id=1, source_target_pairs={{0,2},{2,0},{4,6},{6,4},{8,10},{10,8},{12,14},{14,12},{1,3},{3,1},... | collective-permute-start | bytes 786440 | tf_op jit(solution)/shard_map/ppermute | solution.py:258
  29.8 12.2 %collective-permute-start.2 = (bf16[64,2048]{1,0:T(8,128)(2,1)}, bf16[64,2048]{1,0:T(8,128)(2,1)S(1)}, u32[]{:S(2)}, u32[]{:S(2)}) collective-permute-start(bf16[64,2048]{1,0:T(8,128)(2,1)} %refs_1_.7), channel_id=1, source_target_pairs={{0,12},{2,14},{4,0},{6,2},{8,4},{10,6},{12,8},{14,10},{1,13},{3,15... | collective-permute-start | bytes 786440 | tf_op jit(solution)/shard_map/ppermute | solution.py:261
  32.6 9.6 %collective-permute-start.9 = (bf16[64,2048]{1,0:T(8,128)(2,1)S(1)}, bf16[64,2048]{1,0:T(8,128)(2,1)S(1)}, u32[]{:S(2)}, u32[]{:S(2)}) collective-permute-start(bf16[64,2048]{1,0:T(8,128)(2,1)S(1)} %collective-permute-done.refs_3_.refs_4_), channel_id=1, source_target_pairs={{0,2},{2,0},{4,6},{6,4},{8,10},{10,8},{12,14},{14,12},{1,3},{3,1},... | collective-permute-start | bytes 786440 | tf_op jit(solution)/shard_map/ppermute | solution.py:258
  33.1 20.1 %collective-permute-start.10 = (bf16[64,2048]{1,0:T(8,128)(2,1)}, bf16[64,2048]{1,0:T(8,128)(2,1)S(1)}, u32[]{:S(2)}, u32[]{:S(2)}) collective-permute-start(bf16[64,2048]{1,0:T(8,128)(2,1)} %refs_1_.7), channel_id=1, source_target_pairs={{0,8},{2,10},{4,12},{6,14},{8,0},{10,2},{12,4},{14,6},{1,9},{3,11}... | collective-permute-start | bytes 786440 | tf_op jit(solution)/shard_map/ppermute | solution.py:261
  38.4 14.8 %collective-permute-start.11 = (bf16[64,2048]{1,0:T(8,128)(2,1)S(1)}, bf16[64,2048]{1,0:T(8,128)(2,1)S(1)}, u32[]{:S(2)}, u32[]{:S(2)}) collective-permute-start(bf16[64,2048]{1,0:T(8,128)(2,1)S(1)} %collective-permute-done.1.refs_1_.refs_2_), channel_id=1, source_target_pairs={{0,2},{2,0},{4,6},{6,4},{8,10},{10,8},{12,14},{14,12},{1,3},{3,1},... | collective-permute-start | bytes 786440 | tf_op jit(solution)/shard_map/ppermute | solution.py:258
  42.1 12.6 %collective-permute-start.12 = (bf16[64,2048]{1,0:T(8,128)(2,1)S(1)}, bf16[64,2048]{1,0:T(8,128)(2,1)S(1)}, u32[]{:S(2)}, u32[]{:S(2)}) collective-permute-start(bf16[64,2048]{1,0:T(8,128)(2,1)S(1)} %collective-permute-done.2.refs_2_.refs_3_), channel_id=1, source_target_pairs={{0,2},{2,0},{4,6},{6,4},{8,10},{10,8},{12,14},{14,12},{1,3},{3,1},... | collective-permute-start | bytes 786440 | tf_op jit(solution)/shard_map/ppermute | solution.py:258
  52.7 9.3 %collective-permute-start.14 = (bf16[512,2048]{1,0:T(8,128)(2,1)S(1)}, bf16[512,2048]{1,0:T(8,128)(2,1)S(1)}, u32[]{:S(2)}, u32[]{:S(2)}) collective-permute-start(bf16[512,2048]{1,0:T(8,128)(2,1)S(1)} %shard_map.67.refs_9_), channel_id=1, source_target_pairs={{0,1},{1,0},{2,3},{3,2},{4,5},{5,4},{6,7},{7,6},{8,9},{9,8},{10,11... | collective-permute-start | bytes 6291464 | tf_op jit(solution)/shard_map/ppermute | solution.py:255
  61.9 9.8 %collective-permute-start.15 = (bf16[512,2048]{1,0:T(8,128)(2,1)S(1)}, bf16[512,2048]{1,0:T(8,128)(2,1)S(1)}, u32[]{:S(2)}, u32[]{:S(2)}) collective-permute-start(bf16[512,2048]{1,0:T(8,128)(2,1)S(1)} %shard_map.68.refs_9_), channel_id=1, source_target_pairs={{0,1},{1,0},{2,3},{3,2},{4,5},{5,4},{6,7},{7,6},{8,9},{9,8},{10,11... | collective-permute-start | bytes 6291464 | tf_op jit(solution)/shard_map/ppermute | solution.py:255
  71.1 16.5 %collective-permute-start.16 = (bf16[512,2048]{1,0:T(8,128)(2,1)S(1)}, bf16[512,2048]{1,0:T(8,128)(2,1)S(1)}, u32[]{:S(2)}, u32[]{:S(2)}) collective-permute-start(bf16[512,2048]{1,0:T(8,128)(2,1)S(1)} %get-tuple-element.51.refs_0_), channel_id=1, source_target_pairs={{0,1},{1,0},{2,3},{3,2},{4,5},{5,4},{6,7},{7,6},{8,9},{9,8},{10,11... | collective-permute-start | bytes 6291464 | tf_op jit(solution)/shard_map/ppermute | solution.py:255
  95.5 14.8 %collective-permute-start.18 = (bf16[256,1024]{1,0:T(8,128)(2,1)S(1)}, bf16[256,1024]{1,0:T(8,128)(2,1)S(1)}, u32[]{:S(2)}, u32[]{:S(2)}) collective-permute-start(bf16[256,1024]{1,0:T(8,128)(2,1)S(1)} %get-tuple-element.53), channel_id=1, source_target_pairs={{0,2},{2,0},{4,6},{6,4},{8,10},{10,8},{12,14},{14,12},{1,3},{3,1},... | collective-permute-start | bytes 1572872 | tf_op jit(solution)/shard_map/ppermute | solution.py:258
  101.4 23.9 %collective-permute-start.19 = (bf16[256,1024]{1,0:T(8,128)(2,1)S(1)}, bf16[256,1024]{1,0:T(8,128)(2,1)S(1)}, u32[]{:S(2)}, u32[]{:S(2)}) collective-permute-start(bf16[256,1024]{1,0:T(8,128)(2,1)S(1)} %get-tuple-element.61), channel_id=1, source_target_pairs={{0,2},{2,0},{4,6},{6,4},{8,10},{10,8},{12,14},{14,12},{1,3},{3,1},... | collective-permute-start | bytes 1572872 | tf_op jit(solution)/shard_map/ppermute | solution.py:258
  110.6 25.7 %collective-permute-start.22 = (bf16[64,1024]{1,0:T(8,128)(2,1)S(1)}, bf16[64,1024]{1,0:T(8,128)(2,1)S(1)}, u32[]{:S(2)}, u32[]{:S(2)}) collective-permute-start(bf16[64,1024]{1,0:T(8,128)(2,1)S(1)} %get-tuple-element.76), channel_id=1, source_target_pairs={{0,8},{2,10},{4,12},{6,14},{8,0},{10,2},{12,4},{14,6},{1,9},{3,11}... | collective-permute-start | bytes 393224 | tf_op jit(solution)/shard_map/ppermute | solution.py:261
  114.7 21.5 %collective-permute-start.21 = (bf16[64,1024]{1,0:T(8,128)(2,1)S(1)}, bf16[64,1024]{1,0:T(8,128)(2,1)S(1)}, u32[]{:S(2)}, u32[]{:S(2)}) collective-permute-start(bf16[64,1024]{1,0:T(8,128)(2,1)S(1)} %get-tuple-element.77), channel_id=1, source_target_pairs={{0,4},{2,6},{4,8},{6,10},{8,12},{10,14},{12,0},{14,2},{1,5},{3,7},... | collective-permute-start | bytes 393224 | tf_op jit(solution)/shard_map/ppermute | solution.py:261
  115.0 11.8 %collective-permute-start.20 = (bf16[64,1024]{1,0:T(8,128)(2,1)S(1)}, bf16[64,1024]{1,0:T(8,128)(2,1)S(1)}, u32[]{:S(2)}, u32[]{:S(2)}) collective-permute-start(bf16[64,1024]{1,0:T(8,128)(2,1)S(1)} %get-tuple-element.78), channel_id=1, source_target_pairs={{0,12},{2,14},{4,0},{6,2},{8,4},{10,6},{12,8},{14,10},{1,13},{3,15... | collective-permute-start | bytes 393224 | tf_op jit(solution)/shard_map/ppermute | solution.py:261
  125.5 10.9 %collective-permute-start.25 = (bf16[64,1024]{1,0:T(8,128)(2,1)S(1)}, bf16[64,1024]{1,0:T(8,128)(2,1)S(1)}, u32[]{:S(2)}, u32[]{:S(2)}) collective-permute-start(bf16[64,1024]{1,0:T(8,128)(2,1)S(1)} %get-tuple-element.74), channel_id=1, source_target_pairs={{0,8},{2,10},{4,12},{6,14},{8,0},{10,2},{12,4},{14,6},{1,9},{3,11}... | collective-permute-start | bytes 393224 | tf_op jit(solution)/shard_map/ppermute | solution.py:261
  125.6 10.8 %collective-permute-start.24 = (bf16[64,1024]{1,0:T(8,128)(2,1)S(1)}, bf16[64,1024]{1,0:T(8,128)(2,1)S(1)}, u32[]{:S(2)}, u32[]{:S(2)}) collective-permute-start(bf16[64,1024]{1,0:T(8,128)(2,1)S(1)} %get-tuple-element.75), channel_id=1, source_target_pairs={{0,4},{2,6},{4,8},{6,10},{8,12},{10,14},{12,0},{14,2},{1,5},{3,7},... | collective-permute-start | bytes 393224 | tf_op jit(solution)/shard_map/ppermute | solution.py:261
  126.8 9.6 %collective-permute-start.23 = (bf16[64,1024]{1,0:T(8,128)(2,1)S(1)}, bf16[64,1024]{1,0:T(8,128)(2,1)S(1)}, u32[]{:S(2)}, u32[]{:S(2)}) collective-permute-start(bf16[64,1024]{1,0:T(8,128)(2,1)S(1)} %get-tuple-element.65), channel_id=1, source_target_pairs={{0,12},{2,14},{4,0},{6,2},{8,4},{10,6},{12,8},{14,10},{1,13},{3,15... | collective-permute-start | bytes 393224 | tf_op jit(solution)/shard_map/ppermute | solution.py:261
  (9 other events, 65.1 us)

commit v5 on v4

--- a/solution.py
+++ b/solution.py
@@ -14,7 +14,7 @@
 SPLITS = 2
 Z_AHEAD = 3
 X_AHEAD = 2
-PRE_TILE = 512
+PRE_TILE = 1024
 BACK_TILE = 512
 IN_TILE = 512
 NT = (((1,), (1,)), ((), ()))
@@ -177,7 +177,7 @@
         out_shape,
         cost(2 * m * hidden * count, 2 * count * hidden + 4 * m * hidden),
         (*deltas, up),
-        mib=24,
+        mib=22,
     )
     return got if parts else (*got, deltas[0])
 
@@ -204,11 +204,11 @@
         out_specs=pl.BlockSpec((tile, feats), lambda i: (part * steps + i, 0)),
         out_shape=jax.ShapeDtypeStruct((parts * each, feats), BF16),
         input_output_aliases={1 + n: 0} if extra else {},
-        compiler_params=params(20),
+        compiler_params=params(16),
         cost_estimate=cost(
             2 * m * each * feats,
             2 * each * feats + 2 * m * (each + feats),
-            60 if into is None else 1,
+            100 if into is None else 1,
         ),
     )(act, *cots, *extra)
 

time: 137 us -> 137 us (level)
  no operation moved by 1% of the time
where the time goes in v5:
time: 137 us
  Pallas kernels  69.5 us (51%)
  starting transfers between devices  45.3 us (33%)
  waiting for transfers between devices  16.9 us (12%)
  local copies, waits for them, and re-layouts  3.23 us (2%)
    pallas_call x6, Pallas kernels, call(): pl.pallas_call(kernel, grid=(steps,), in_specs=in_specs, out_specs=out_sp...  42.8 us
    ppermute x12, starting transfers between devices, shift(): return lax.ppermute(x, 'row', [(r, (r + k * NX) % row) for r in range(row)])  31.3 us
    ppermute x12, waiting for transfers between devices, shift(): return lax.ppermute(x, 'row', [(r, (r + k * NX) % row) for r in range(row)])  15.6 us
    pallas_call x2, Pallas kernels, up_pass(): pl.pallas_call(kernel, grid=(steps,), in_specs=[pl.BlockSpec((m, tile), l...  13.4 us
    pallas_call x2, Pallas kernels, down_pass(): pl.pallas_call(kernel, grid=(steps,), in_specs=[pl.BlockSpec((m, tile), l...  13.4 us
    ppermute x10, starting transfers between devices, across(): return lax.ppermute(x, 'row', [(r, r ^ 1) for r in range(row)])  13.2 us
    unnamed x14, local copies, waits for them, and re-layouts  3.13 us
  transfers between devices with their start and end apart: 26, of which 8 were waited for; matrix products, arithmetic and copies ran while one was open for 0% of the time, Pallas kernels for 47%

profile of v5, /device:TPU:0, one launch (start us, length us, event | category | flops | bytes accessed | tf_op | source)
XLA Modules:
  0.0 137.1 jit_solution(9098634582303951892)
XLA Ops:
  0.6 3.1 %collective-permute-start.3 = (bf16[64,2048]{1,0:T(8,128)(2,1)}, bf16[64,2048]{1,0:T(8,128)(2,1)S(1)}, u32[]{:S(2)}, u32[]{:S(2)}) collective-permute-start(bf16[64,2048]{1,0:T(8,128)(2,1)} %refs_1_.9), channel_id=1, source_target_pairs={{0,4},{2,6},{4,8},{6,10},{8,12},{10,14},{12,0},{14,2},{1,5},{3,7},... | collective-permute-start | bytes 786440 | tf_op jit(solution)/shard_map/ppermute | solution.py:261
  5.2 2.6 %collective-permute-start = (bf16[64,2048]{1,0:T(8,128)(2,1)}, bf16[64,2048]{1,0:T(8,128)(2,1)S(1)}, u32[]{:S(2)}, u32[]{:S(2)}) collective-permute-start(bf16[64,2048]{1,0:T(8,128)(2,1)} %refs_1_.9), channel_id=1, source_target_pairs={{0,8},{2,10},{4,12},{6,14},{8,0},{10,2},{12,4},{14,6},{1,9},{3,11}... | collective-permute-start | bytes 786440 | tf_op jit(solution)/shard_map/ppermute | solution.py:261
  9.1 4.1 %collective-permute-done.3.refs_1_.refs_2_ = bf16[64,2048]{1,0:T(8,128)(2,1)S(1)} collective-permute-done((bf16[64,2048]{1,0:T(8,128)(2,1)}, bf16[64,2048]{1,0:T(8,128)(2,1)S(1)}, u32[]{:S(2)}, u32[]{:S(2)}) %collective-permute-start.3) | collective-permute-done | bytes 262176 | tf_op jit(solution)/shard_map/ppermute | solution.py:261
  13.2 1.7 %collective-permute-start.6 = (bf16[64,2048]{1,0:T(8,128)(2,1)S(1)}, bf16[64,2048]{1,0:T(8,128)(2,1)S(1)}, u32[]{:S(2)}, u32[]{:S(2)}) collective-permute-start(bf16[64,2048]{1,0:T(8,128)(2,1)S(1)} %collective-permute-done.3.refs_1_.refs_2_), channel_id=1, source_target_pairs={{0,2},{2,0},{4,6},{6,4},{8,10},{10,8},{12,14},{14,12},{1,3},{3,1},... | collective-permute-start | bytes 786440 | tf_op jit(solution)/shard_map/ppermute | solution.py:258
  15.3 8.4 %collective-permute-done.refs_3_.refs_4_ = bf16[64,2048]{1,0:T(8,128)(2,1)S(1)} collective-permute-done((bf16[64,2048]{1,0:T(8,128)(2,1)}, bf16[64,2048]{1,0:T(8,128)(2,1)S(1)}, u32[]{:S(2)}, u32[]{:S(2)}) %collective-permute-start) | collective-permute-done | bytes 262176 | tf_op jit(solution)/shard_map/ppermute | solution.py:261
  23.6 4.7 %collective-permute-start.1 = (bf16[64,2048]{1,0:T(8,128)(2,1)}, bf16[64,2048]{1,0:T(8,128)(2,1)S(1)}, u32[]{:S(2)}, u32[]{:S(2)}) collective-permute-start(bf16[64,2048]{1,0:T(8,128)(2,1)} %refs_1_.7), channel_id=1, source_target_pairs={{0,4},{2,6},{4,8},{6,10},{8,12},{10,14},{12,0},{14,2},{1,5},{3,7},... | collective-permute-start | bytes 786440 | tf_op jit(solution)/shard_map/ppermute | solution.py:261
  29.8 2.8 %collective-permute-start.2 = (bf16[64,2048]{1,0:T(8,128)(2,1)}, bf16[64,2048]{1,0:T(8,128)(2,1)S(1)}, u32[]{:S(2)}, u32[]{:S(2)}) collective-permute-start(bf16[64,2048]{1,0:T(8,128)(2,1)} %refs_1_.7), channel_id=1, source_target_pairs={{0,12},{2,14},{4,0},{6,2},{8,4},{10,6},{12,8},{14,10},{1,13},{3,15... | collective-permute-start | bytes 786440 | tf_op jit(solution)/shard_map/ppermute | solution.py:261
  33.1 4.8 %collective-permute-start.10 = (bf16[64,2048]{1,0:T(8,128)(2,1)}, bf16[64,2048]{1,0:T(8,128)(2,1)S(1)}, u32[]{:S(2)}, u32[]{:S(2)}) collective-permute-start(bf16[64,2048]{1,0:T(8,128)(2,1)} %refs_1_.7), channel_id=1, source_target_pairs={{0,8},{2,10},{4,12},{6,14},{8,0},{10,2},{12,4},{14,6},{1,9},{3,11}... | collective-permute-start | bytes 786440 | tf_op jit(solution)/shard_map/ppermute | solution.py:261
  38.4 1.5 %collective-permute-start.11 = (bf16[64,2048]{1,0:T(8,128)(2,1)S(1)}, bf16[64,2048]{1,0:T(8,128)(2,1)S(1)}, u32[]{:S(2)}, u32[]{:S(2)}) collective-permute-start(bf16[64,2048]{1,0:T(8,128)(2,1)S(1)} %collective-permute-done.1.refs_1_.refs_2_), channel_id=1, source_target_pairs={{0,2},{2,0},{4,6},{6,4},{8,10},{10,8},{12,14},{14,12},{1,3},{3,1},... | collective-permute-start | bytes 786440 | tf_op jit(solution)/shard_map/ppermute | solution.py:258
  40.0 2.0 %collective-permute-done.2.refs_2_.refs_3_ = bf16[64,2048]{1,0:T(8,128)(2,1)S(1)} collective-permute-done((bf16[64,2048]{1,0:T(8,128)(2,1)}, bf16[64,2048]{1,0:T(8,128)(2,1)S(1)}, u32[]{:S(2)}, u32[]{:S(2)}) %collective-permute-start.2) | collective-permute-done | bytes 262176 | tf_op jit(solution)/shard_map/ppermute | solution.py:261
  42.1 2.5 %collective-permute-start.12 = (bf16[64,2048]{1,0:T(8,128)(2,1)S(1)}, bf16[64,2048]{1,0:T(8,128)(2,1)S(1)}, u32[]{:S(2)}, u32[]{:S(2)}) collective-permute-start(bf16[64,2048]{1,0:T(8,128)(2,1)S(1)} %collective-permute-done.2.refs_2_.refs_3_), channel_id=1, source_target_pairs={{0,2},{2,0},{4,6},{6,4},{8,10},{10,8},{12,14},{14,12},{1,3},{3,1},... | collective-permute-start | bytes 786440 | tf_op jit(solution)/shard_map/ppermute | solution.py:258
  45.6 7.0 %shard_map.67.refs_9_ = bf16[512,2048]{1,0:T(8,128)(2,1)S(1)} custom-call(bf16[64,2048]{1,0:T(8,128)(2,1)S(1)} %copy-done, bf16[64,2048]{1,0:T(8,128)(2,1)S(1)} %collective-permute-done.3.refs_1_.refs_2_, bf16[64,2048]{1,0:T(8,128)(2,1)S(1)} %collective-permute-done.4.refs_2_.refs_3_, bf16[64,2048]{1,0:T(8,128)(2,1)S(1)} %collective-permute-done.refs_3_.refs_4_, ...), custom_call_target="tpu_custom_call" | custom-call | flops 214748368 | bytes 629145 | tf_op jit(solution)/shard_map/pallas_call | solution.py:52
  54.7 7.0 %shard_map.68.refs_9_ = bf16[512,2048]{1,0:T(8,128)(2,1)S(1)} custom-call(bf16[64,2048]{1,0:T(8,128)(2,1)S(1)} %copy-done, bf16[64,2048]{1,0:T(8,128)(2,1)S(1)} %collective-permute-done.3.refs_1_.refs_2_, bf16[64,2048]{1,0:T(8,128)(2,1)S(1)} %collective-permute-done.4.refs_2_.refs_3_, bf16[64,2048]{1,0:T(8,128)(2,1)S(1)} %collective-permute-done.refs_3_.refs_4_, ...), custom_call_target="tpu_custom_call" | custom-call | flops 21474836480 | bytes 62914560 | tf_op jit(solution)/shard_map/pallas_call | solution.py:52
  61.8 9.1 %shard_map.69 = (bf16[512,2048]{1,0:T(8,128)(2,1)S(1)}, bf16[512,2048]{1,0:T(8,128)(2,1)S(1)}) custom-call(bf16[64,2048]{1,0:T(8,128)(2,1)S(1)} %copy-done.2, bf16[64,2048]{1,0:T(8,128)(2,1)S(1)} %collective-permute-done.1.refs_1_.refs_2_, bf16[64,2048]{1,0:T(8,128)(2,1)S(1)} %collective-permute-done.2.refs_2_.refs_3_, ...), custom_call_target="tpu_custom_call" | custom-call | flops 21474836480 | bytes 94371840 | tf_op jit(solution)/shard_map/pallas_call | solution.py:52
  71.5 9.1 %shard_map.70 = (bf16[512,2048]{1,0:T(8,128)(2,1)S(1)}, bf16[512,2048]{1,0:T(8,128)(2,1)S(1)}) custom-call(bf16[64,2048]{1,0:T(8,128)(2,1)S(1)} %copy-done.2, bf16[64,2048]{1,0:T(8,128)(2,1)S(1)} %collective-permute-done.1.refs_1_.refs_2_, bf16[64,2048]{1,0:T(8,128)(2,1)S(1)} %collective-permute-done.2.refs_2_.refs_3_, ...), custom_call_target="tpu_custom_call" | custom-call | flops 214748368 | bytes 943718 | tf_op jit(solution)/shard_map/pallas_call | solution.py:52
  80.7 6.7 %shard_map.71.refs_9_ = bf16[4096,2048]{1,0:T(8,128)(2,1)} custom-call(bf16[512,2048]{1,0:T(8,128)(2,1)S(1)} %get-tuple-element.50.refs_0_, bf16[64,2048]{1,0:T(8,128)(2,1)S(1)} %copy-done.2, bf16[64,2048]{1,0:T(8,128)(2,1)S(1)} %collective-permute-done.1.refs_1_.refs_2_, bf16[64,2048]{1,0:T(8,128)(2,1)S(1)} %collective-permute-done.2.refs_2_.refs_3_, ...), custom_call_target="tpu_custom_call" | custom-call | flops 21474836480 | bytes 62914560 | tf_op jit(solution)/shard_map/pallas_call | solution.py:198
  89.6 5.8 %shard_map.72 = (f32[256,1024]{1,0:T(8,128)S(1)}, bf16[256,1024]{1,0:T(8,128)(2,1)S(1)}, bf16[512,4096]{1,0:T(8,128)(2,1)S(1)}) custom-call(bf16[512,2048]{1,0:T(8,128)(2,1)S(1)} %get-tuple-element.51.refs_0_, bf16[512,2048]{1,0:T(8,128)(2,1)S(1)} %get-tuple-element.49.refs_1_, bf16[512,2048]{1,0:T(8,128)(2,1)S(1)} %collective-permute-done.16.refs_2_, ...), custom_call_target="tpu_custom_call" | custom-call | flops 214748368 | bytes 838860 | tf_op jit(solution)/shard_map/pallas_call | solution.py:52
  96.5 4.8 %shard_map.73 = (f32[256,1024]{1,0:T(8,128)S(1)}, bf16[256,1024]{1,0:T(8,128)(2,1)S(1)}) custom-call(bf16[512,4096]{1,0:T(8,128)(2,1)S(1)} %get-tuple-element.66.refs_0_, bf16[2048,4096]{1,0:T(8,128)(2,1)S(1)} %bitcast.1), custom_call_target="tpu_custom_call" | custom-call | flops 214748368 | bytes 838860 | tf_op jit(solution)/shard_map/pallas_call | solution.py:52
  102.4 6.7 %shard_map.74 = bf16[4096,2048]{1,0:T(8,128)(2,1)} custom-call(bf16[512,2048]{1,0:T(8,128)(2,1)S(1)} %get-tuple-element.58.refs_0_, bf16[64,2048]{1,0:T(8,128)(2,1)S(1)} %copy-done.2, bf16[64,2048]{1,0:T(8,128)(2,1)S(1)} %collective-permute-done.1.refs_1_.refs_2_, ...), custom_call_target="tpu_custom_call", output_to_operand_aliasing={{}: (9, {})} | custom-call | flops 214748368 | bytes 629145 | tf_op jit(solution)/shard_map/pallas_call | solution.py:198
  110.4 4.2 %collective-permute-start.22 = (bf16[64,1024]{1,0:T(8,128)(2,1)S(1)}, bf16[64,1024]{1,0:T(8,128)(2,1)S(1)}, u32[]{:S(2)}, u32[]{:S(2)}) collective-permute-start(bf16[64,1024]{1,0:T(8,128)(2,1)S(1)} %get-tuple-element.76), channel_id=1, source_target_pairs={{0,8},{2,10},{4,12},{6,14},{8,0},{10,2},{12,4},{14,6},{1,9},{3,11}... | collective-permute-start | bytes 393224 | tf_op jit(solution)/shard_map/ppermute | solution.py:261
  114.6 3.8 %collective-permute-start.20 = (bf16[64,1024]{1,0:T(8,128)(2,1)S(1)}, bf16[64,1024]{1,0:T(8,128)(2,1)S(1)}, u32[]{:S(2)}, u32[]{:S(2)}) collective-permute-start(bf16[64,1024]{1,0:T(8,128)(2,1)S(1)} %get-tuple-element.78), channel_id=1, source_target_pairs={{0,12},{2,14},{4,0},{6,2},{8,4},{10,6},{12,8},{14,10},{1,13},{3,15... | collective-permute-start | bytes 393224 | tf_op jit(solution)/shard_map/ppermute | solution.py:261
  118.5 6.7 %shard_map.75.refs_9_ = bf16[2048,4096]{1,0:T(8,128)(2,1)} custom-call(bf16[512,4096]{1,0:T(8,128)(2,1)S(1)} %get-tuple-element.66.refs_0_, bf16[64,2048]{1,0:T(8,128)(2,1)S(1)} %copy-done.1, bf16[64,2048]{1,0:T(8,128)(2,1)S(1)} %collective-permute-done.3.refs_1_.refs_2_, bf16[64,2048]{1,0:T(8,128)(2,1)S(1)} %collective-permute-done.4.refs_2_.refs_3_, ...), custom_call_target="tpu_custom_call" | custom-call | flops 214748368 | bytes 629145 | tf_op jit(solution)/shard_map/pallas_call | solution.py:230
  126.6 2.9 %collective-permute-start.23 = (bf16[64,1024]{1,0:T(8,128)(2,1)S(1)}, bf16[64,1024]{1,0:T(8,128)(2,1)S(1)}, u32[]{:S(2)}, u32[]{:S(2)}) collective-permute-start(bf16[64,1024]{1,0:T(8,128)(2,1)S(1)} %get-tuple-element.65), channel_id=1, source_target_pairs={{0,12},{2,14},{4,0},{6,2},{8,4},{10,6},{12,8},{14,10},{1,13},{3,15... | collective-permute-start | bytes 393224 | tf_op jit(solution)/shard_map/ppermute | solution.py:261
  129.5 6.7 %shard_map.76 = bf16[2048,4096]{1,0:T(8,128)(2,1)} custom-call(bf16[512,4096]{1,0:T(8,128)(2,1)S(1)} %get-tuple-element.66.refs_0_, bf16[64,2048]{1,0:T(8,128)(2,1)S(1)} %copy-done.1, bf16[64,2048]{1,0:T(8,128)(2,1)S(1)} %collective-permute-done.3.refs_1_.refs_2_, ...), custom_call_target="tpu_custom_call", output_to_operand_aliasing={{}: (9, {})} | custom-call | flops 214748368 | bytes 629145 | tf_op jit(solution)/shard_map/pallas_call | solution.py:230
  (62 shorter events, 17.7 us)
Async XLA Ops:
  0.6 12.6 %collective-permute-start.3 = (bf16[64,2048]{1,0:T(8,128)(2,1)}, bf16[64,2048]{1,0:T(8,128)(2,1)S(1)}, u32[]{:S(2)}, u32[]{:S(2)}) collective-permute-start(bf16[64,2048]{1,0:T(8,128)(2,1)} %refs_1_.9), channel_id=1, source_target_pairs={{0,4},{2,6},{4,8},{6,10},{8,12},{10,14},{12,0},{14,2},{1,5},{3,7},... | collective-permute-start | bytes 786440 | tf_op jit(solution)/shard_map/ppermute | solution.py:261
  3.7 11.3 %collective-permute-start.5 = (bf16[64,2048]{1,0:T(8,128)(2,1)}, bf16[64,2048]{1,0:T(8,128)(2,1)S(1)}, u32[]{:S(2)}, u32[]{:S(2)}) collective-permute-start(bf16[64,2048]{1,0:T(8,128)(2,1)} %refs_1_.9), channel_id=1, source_target_pairs={{0,2},{2,0},{4,6},{6,4},{8,10},{10,8},{12,14},{14,12},{1,3},{3,1},... | collective-permute-start | bytes 786440 | tf_op jit(solution)/shard_map/ppermute | solution.py:258
  5.2 18.4 %collective-permute-start = (bf16[64,2048]{1,0:T(8,128)(2,1)}, bf16[64,2048]{1,0:T(8,128)(2,1)S(1)}, u32[]{:S(2)}, u32[]{:S(2)}) collective-permute-start(bf16[64,2048]{1,0:T(8,128)(2,1)} %refs_1_.9), channel_id=1, source_target_pairs={{0,8},{2,10},{4,12},{6,14},{8,0},{10,2},{12,4},{14,6},{1,9},{3,11}... | collective-permute-start | bytes 786440 | tf_op jit(solution)/shard_map/ppermute | solution.py:261
  7.8 20.5 %collective-permute-start.4 = (bf16[64,2048]{1,0:T(8,128)(2,1)}, bf16[64,2048]{1,0:T(8,128)(2,1)S(1)}, u32[]{:S(2)}, u32[]{:S(2)}) collective-permute-start(bf16[64,2048]{1,0:T(8,128)(2,1)} %refs_1_.9), channel_id=1, source_target_pairs={{0,12},{2,14},{4,0},{6,2},{8,4},{10,6},{12,8},{14,10},{1,13},{3,15... | collective-permute-start | bytes 786440 | tf_op jit(solution)/shard_map/ppermute | solution.py:261
  13.2 15.1 %collective-permute-start.6 = (bf16[64,2048]{1,0:T(8,128)(2,1)S(1)}, bf16[64,2048]{1,0:T(8,128)(2,1)S(1)}, u32[]{:S(2)}, u32[]{:S(2)}) collective-permute-start(bf16[64,2048]{1,0:T(8,128)(2,1)S(1)} %collective-permute-done.3.refs_1_.refs_2_), channel_id=1, source_target_pairs={{0,2},{2,0},{4,6},{6,4},{8,10},{10,8},{12,14},{14,12},{1,3},{3,1},... | collective-permute-start | bytes 786440 | tf_op jit(solution)/shard_map/ppermute | solution.py:258
  15.0 17.6 %collective-permute-start.8 = (bf16[64,2048]{1,0:T(8,128)(2,1)}, bf16[64,2048]{1,0:T(8,128)(2,1)S(1)}, u32[]{:S(2)}, u32[]{:S(2)}) collective-permute-start(bf16[64,2048]{1,0:T(8,128)(2,1)} %refs_1_.7), channel_id=1, source_target_pairs={{0,2},{2,0},{4,6},{6,4},{8,10},{10,8},{12,14},{14,12},{1,3},{3,1},... | collective-permute-start | bytes 786440 | tf_op jit(solution)/shard_map/ppermute | solution.py:258
  23.6 14.8 %collective-permute-start.1 = (bf16[64,2048]{1,0:T(8,128)(2,1)}, bf16[64,2048]{1,0:T(8,128)(2,1)S(1)}, u32[]{:S(2)}, u32[]{:S(2)}) collective-permute-start(bf16[64,2048]{1,0:T(8,128)(2,1)} %refs_1_.7), channel_id=1, source_target_pairs={{0,4},{2,6},{4,8},{6,10},{8,12},{10,14},{12,0},{14,2},{1,5},{3,7},... | collective-permute-start | bytes 786440 | tf_op jit(solution)/shard_map/ppermute | solution.py:261
  28.3 10.1 %collective-permute-start.7 = (bf16[64,2048]{1,0:T(8,128)(2,1)S(1)}, bf16[64,2048]{1,0:T(8,128)(2,1)S(1)}, u32[]{:S(2)}, u32[]{:S(2)}) collective-permute-start(bf16[64,2048]{1,0:T(8,128)(2,1)S(1)} %collective-permute-done.4.refs_2_.refs_3_), channel_id=1, source_target_pairs={{0,2},{2,0},{4,6},{6,4},{8,10},{10,8},{12,14},{14,12},{1,3},{3,1},... | collective-permute-start | bytes 786440 | tf_op jit(solution)/shard_map/ppermute | solution.py:258
  29.8 12.2 %collective-permute-start.2 = (bf16[64,2048]{1,0:T(8,128)(2,1)}, bf16[64,2048]{1,0:T(8,128)(2,1)S(1)}, u32[]{:S(2)}, u32[]{:S(2)}) collective-permute-start(bf16[64,2048]{1,0:T(8,128)(2,1)} %refs_1_.7), channel_id=1, source_target_pairs={{0,12},{2,14},{4,0},{6,2},{8,4},{10,6},{12,8},{14,10},{1,13},{3,15... | collective-permute-start | bytes 786440 | tf_op jit(solution)/shard_map/ppermute | solution.py:261
  32.6 9.6 %collective-permute-start.9 = (bf16[64,2048]{1,0:T(8,128)(2,1)S(1)}, bf16[64,2048]{1,0:T(8,128)(2,1)S(1)}, u32[]{:S(2)}, u32[]{:S(2)}) collective-permute-start(bf16[64,2048]{1,0:T(8,128)(2,1)S(1)} %collective-permute-done.refs_3_.refs_4_), channel_id=1, source_target_pairs={{0,2},{2,0},{4,6},{6,4},{8,10},{10,8},{12,14},{14,12},{1,3},{3,1},... | collective-permute-start | bytes 786440 | tf_op jit(solution)/shard_map/ppermute | solution.py:258
  33.1 20.1 %collective-permute-start.10 = (bf16[64,2048]{1,0:T(8,128)(2,1)}, bf16[64,2048]{1,0:T(8,128)(2,1)S(1)}, u32[]{:S(2)}, u32[]{:S(2)}) collective-permute-start(bf16[64,2048]{1,0:T(8,128)(2,1)} %refs_1_.7), channel_id=1, source_target_pairs={{0,8},{2,10},{4,12},{6,14},{8,0},{10,2},{12,4},{14,6},{1,9},{3,11}... | collective-permute-start | bytes 786440 | tf_op jit(solution)/shard_map/ppermute | solution.py:261
  38.4 14.8 %collective-permute-start.11 = (bf16[64,2048]{1,0:T(8,128)(2,1)S(1)}, bf16[64,2048]{1,0:T(8,128)(2,1)S(1)}, u32[]{:S(2)}, u32[]{:S(2)}) collective-permute-start(bf16[64,2048]{1,0:T(8,128)(2,1)S(1)} %collective-permute-done.1.refs_1_.refs_2_), channel_id=1, source_target_pairs={{0,2},{2,0},{4,6},{6,4},{8,10},{10,8},{12,14},{14,12},{1,3},{3,1},... | collective-permute-start | bytes 786440 | tf_op jit(solution)/shard_map/ppermute | solution.py:258
  42.1 12.6 %collective-permute-start.12 = (bf16[64,2048]{1,0:T(8,128)(2,1)S(1)}, bf16[64,2048]{1,0:T(8,128)(2,1)S(1)}, u32[]{:S(2)}, u32[]{:S(2)}) collective-permute-start(bf16[64,2048]{1,0:T(8,128)(2,1)S(1)} %collective-permute-done.2.refs_2_.refs_3_), channel_id=1, source_target_pairs={{0,2},{2,0},{4,6},{6,4},{8,10},{10,8},{12,14},{14,12},{1,3},{3,1},... | collective-permute-start | bytes 786440 | tf_op jit(solution)/shard_map/ppermute | solution.py:258
  52.6 9.3 %collective-permute-start.14 = (bf16[512,2048]{1,0:T(8,128)(2,1)S(1)}, bf16[512,2048]{1,0:T(8,128)(2,1)S(1)}, u32[]{:S(2)}, u32[]{:S(2)}) collective-permute-start(bf16[512,2048]{1,0:T(8,128)(2,1)S(1)} %shard_map.67.refs_9_), channel_id=1, source_target_pairs={{0,1},{1,0},{2,3},{3,2},{4,5},{5,4},{6,7},{7,6},{8,9},{9,8},{10,11... | collective-permute-start | bytes 6291464 | tf_op jit(solution)/shard_map/ppermute | solution.py:255
  61.7 9.8 %collective-permute-start.15 = (bf16[512,2048]{1,0:T(8,128)(2,1)S(1)}, bf16[512,2048]{1,0:T(8,128)(2,1)S(1)}, u32[]{:S(2)}, u32[]{:S(2)}) collective-permute-start(bf16[512,2048]{1,0:T(8,128)(2,1)S(1)} %shard_map.68.refs_9_), channel_id=1, source_target_pairs={{0,1},{1,0},{2,3},{3,2},{4,5},{5,4},{6,7},{7,6},{8,9},{9,8},{10,11... | collective-permute-start | bytes 6291464 | tf_op jit(solution)/shard_map/ppermute | solution.py:255
  71.0 16.5 %collective-permute-start.16 = (bf16[512,2048]{1,0:T(8,128)(2,1)S(1)}, bf16[512,2048]{1,0:T(8,128)(2,1)S(1)}, u32[]{:S(2)}, u32[]{:S(2)}) collective-permute-start(bf16[512,2048]{1,0:T(8,128)(2,1)S(1)} %get-tuple-element.51.refs_0_), channel_id=1, source_target_pairs={{0,1},{1,0},{2,3},{3,2},{4,5},{5,4},{6,7},{7,6},{8,9},{9,8},{10,11... | collective-permute-start | bytes 6291464 | tf_op jit(solution)/shard_map/ppermute | solution.py:255
  95.4 14.8 %collective-permute-start.18 = (bf16[256,1024]{1,0:T(8,128)(2,1)S(1)}, bf16[256,1024]{1,0:T(8,128)(2,1)S(1)}, u32[]{:S(2)}, u32[]{:S(2)}) collective-permute-start(bf16[256,1024]{1,0:T(8,128)(2,1)S(1)} %get-tuple-element.53), channel_id=1, source_target_pairs={{0,2},{2,0},{4,6},{6,4},{8,10},{10,8},{12,14},{14,12},{1,3},{3,1},... | collective-permute-start | bytes 1572872 | tf_op jit(solution)/shard_map/ppermute | solution.py:258
  101.4 23.8 %collective-permute-start.19 = (bf16[256,1024]{1,0:T(8,128)(2,1)S(1)}, bf16[256,1024]{1,0:T(8,128)(2,1)S(1)}, u32[]{:S(2)}, u32[]{:S(2)}) collective-permute-start(bf16[256,1024]{1,0:T(8,128)(2,1)S(1)} %get-tuple-element.61), channel_id=1, source_target_pairs={{0,2},{2,0},{4,6},{6,4},{8,10},{10,8},{12,14},{14,12},{1,3},{3,1},... | collective-permute-start | bytes 1572872 | tf_op jit(solution)/shard_map/ppermute | solution.py:258
  110.4 25.7 %collective-permute-start.22 = (bf16[64,1024]{1,0:T(8,128)(2,1)S(1)}, bf16[64,1024]{1,0:T(8,128)(2,1)S(1)}, u32[]{:S(2)}, u32[]{:S(2)}) collective-permute-start(bf16[64,1024]{1,0:T(8,128)(2,1)S(1)} %get-tuple-element.76), channel_id=1, source_target_pairs={{0,8},{2,10},{4,12},{6,14},{8,0},{10,2},{12,4},{14,6},{1,9},{3,11}... | collective-permute-start | bytes 393224 | tf_op jit(solution)/shard_map/ppermute | solution.py:261
  114.6 21.5 %collective-permute-start.21 = (bf16[64,1024]{1,0:T(8,128)(2,1)S(1)}, bf16[64,1024]{1,0:T(8,128)(2,1)S(1)}, u32[]{:S(2)}, u32[]{:S(2)}) collective-permute-start(bf16[64,1024]{1,0:T(8,128)(2,1)S(1)} %get-tuple-element.77), channel_id=1, source_target_pairs={{0,4},{2,6},{4,8},{6,10},{8,12},{10,14},{12,0},{14,2},{1,5},{3,7},... | collective-permute-start | bytes 393224 | tf_op jit(solution)/shard_map/ppermute | solution.py:261
  114.6 12.0 %collective-permute-start.20 = (bf16[64,1024]{1,0:T(8,128)(2,1)S(1)}, bf16[64,1024]{1,0:T(8,128)(2,1)S(1)}, u32[]{:S(2)}, u32[]{:S(2)}) collective-permute-start(bf16[64,1024]{1,0:T(8,128)(2,1)S(1)} %get-tuple-element.78), channel_id=1, source_target_pairs={{0,12},{2,14},{4,0},{6,2},{8,4},{10,6},{12,8},{14,10},{1,13},{3,15... | collective-permute-start | bytes 393224 | tf_op jit(solution)/shard_map/ppermute | solution.py:261
  125.4 10.9 %collective-permute-start.25 = (bf16[64,1024]{1,0:T(8,128)(2,1)S(1)}, bf16[64,1024]{1,0:T(8,128)(2,1)S(1)}, u32[]{:S(2)}, u32[]{:S(2)}) collective-permute-start(bf16[64,1024]{1,0:T(8,128)(2,1)S(1)} %get-tuple-element.74), channel_id=1, source_target_pairs={{0,8},{2,10},{4,12},{6,14},{8,0},{10,2},{12,4},{14,6},{1,9},{3,11}... | collective-permute-start | bytes 393224 | tf_op jit(solution)/shard_map/ppermute | solution.py:261
  125.5 10.8 %collective-permute-start.24 = (bf16[64,1024]{1,0:T(8,128)(2,1)S(1)}, bf16[64,1024]{1,0:T(8,128)(2,1)S(1)}, u32[]{:S(2)}, u32[]{:S(2)}) collective-permute-start(bf16[64,1024]{1,0:T(8,128)(2,1)S(1)} %get-tuple-element.75), channel_id=1, source_target_pairs={{0,4},{2,6},{4,8},{6,10},{8,12},{10,14},{12,0},{14,2},{1,5},{3,7},... | collective-permute-start | bytes 393224 | tf_op jit(solution)/shard_map/ppermute | solution.py:261
  126.6 9.7 %collective-permute-start.23 = (bf16[64,1024]{1,0:T(8,128)(2,1)S(1)}, bf16[64,1024]{1,0:T(8,128)(2,1)S(1)}, u32[]{:S(2)}, u32[]{:S(2)}) collective-permute-start(bf16[64,1024]{1,0:T(8,128)(2,1)S(1)} %get-tuple-element.65), channel_id=1, source_target_pairs={{0,12},{2,14},{4,0},{6,2},{8,4},{10,6},{12,8},{14,10},{1,13},{3,15... | collective-permute-start | bytes 393224 | tf_op jit(solution)/shard_map/ppermute | solution.py:261
  (9 other events, 65.0 us)

commit v6 on v5

--- a/solution.py
+++ b/solution.py
@@ -236,7 +236,7 @@
         out_specs=pl.BlockSpec((feats, tile), lambda i: (0, part * steps + i)),
         out_shape=jax.ShapeDtypeStruct((feats, hidden), BF16),
         input_output_aliases={1 + n: 0} if extra else {},
-        compiler_params=params(36),
+        compiler_params=params(24),
         cost_estimate=cost(
             2 * m * each * feats, 2 * each * feats + 2 * m * (each + feats)
         ),
@@ -318,7 +318,7 @@
         blocks = [total[at * mine : (at + 1) * mine] for at in range(nz)]
         sends = [b.astype(BF16) for b in blocks[1:]]
         if columns:
-            sends[0] = tied(sends[0], columns[-1][1][0])
+            sends[0] = tied(sends[0], columns[-1][1][1])
         columns.append((blocks[0], [shift(b, -k) for k, b in zip(order[1:], sends)]))
         grad_up = up_pass(tied(delta, *sends), all_tokens, s, SPLITS, grad_up)
         last = grad_up

time: 137 us -> 137 us (level)
  no operation moved by 1% of the time
where the time goes in v6:
time: 137 us
  Pallas kernels  69.5 us (51%)
  starting transfers between devices  45.3 us (33%)
  waiting for transfers between devices  16.9 us (12%)
  local copies, waits for them, and re-layouts  3.23 us (2%)
    pallas_call x6, Pallas kernels, call(): pl.pallas_call(kernel, grid=(steps,), in_specs=in_specs, out_specs=out_sp...  42.8 us
    ppermute x12, starting transfers between devices, shift(): return lax.ppermute(x, 'row', [(r, (r + k * NX) % row) for r in range(row)])  31.3 us
    ppermute x12, waiting for transfers between devices, shift(): return lax.ppermute(x, 'row', [(r, (r + k * NX) % row) for r in range(row)])  15.6 us
    pallas_call x2, Pallas kernels, up_pass(): pl.pallas_call(kernel, grid=(steps,), in_specs=[pl.BlockSpec((m, tile), l...  13.4 us
    pallas_call x2, Pallas kernels, down_pass(): pl.pallas_call(kernel, grid=(steps,), in_specs=[pl.BlockSpec((m, tile), l...  13.4 us
    ppermute x10, starting transfers between devices, across(): return lax.ppermute(x, 'row', [(r, r ^ 1) for r in range(row)])  13.2 us
    unnamed x14, local copies, waits for them, and re-layouts  3.13 us
  transfers between devices with their start and end apart: 26, of which 8 were waited for; matrix products, arithmetic and copies ran while one was open for 0% of the time, Pallas kernels for 47%

profile of v6, /device:TPU:0, one launch (start us, length us, event | category | flops | bytes accessed | tf_op | source)
XLA Modules:
  0.0 137.1 jit_solution(1525810050622513629)
XLA Ops:
  0.6 3.1 %collective-permute-start.3 = (bf16[64,2048]{1,0:T(8,128)(2,1)}, bf16[64,2048]{1,0:T(8,128)(2,1)S(1)}, u32[]{:S(2)}, u32[]{:S(2)}) collective-permute-start(bf16[64,2048]{1,0:T(8,128)(2,1)} %refs_1_.9), channel_id=1, source_target_pairs={{0,4},{2,6},{4,8},{6,10},{8,12},{10,14},{12,0},{14,2},{1,5},{3,7},... | collective-permute-start | bytes 786440 | tf_op jit(solution)/shard_map/ppermute | solution.py:261
  5.2 2.6 %collective-permute-start = (bf16[64,2048]{1,0:T(8,128)(2,1)}, bf16[64,2048]{1,0:T(8,128)(2,1)S(1)}, u32[]{:S(2)}, u32[]{:S(2)}) collective-permute-start(bf16[64,2048]{1,0:T(8,128)(2,1)} %refs_1_.9), channel_id=1, source_target_pairs={{0,8},{2,10},{4,12},{6,14},{8,0},{10,2},{12,4},{14,6},{1,9},{3,11}... | collective-permute-start | bytes 786440 | tf_op jit(solution)/shard_map/ppermute | solution.py:261
  9.1 4.1 %collective-permute-done.3.refs_1_.refs_2_ = bf16[64,2048]{1,0:T(8,128)(2,1)S(1)} collective-permute-done((bf16[64,2048]{1,0:T(8,128)(2,1)}, bf16[64,2048]{1,0:T(8,128)(2,1)S(1)}, u32[]{:S(2)}, u32[]{:S(2)}) %collective-permute-start.3) | collective-permute-done | bytes 262176 | tf_op jit(solution)/shard_map/ppermute | solution.py:261
  13.2 1.7 %collective-permute-start.6 = (bf16[64,2048]{1,0:T(8,128)(2,1)S(1)}, bf16[64,2048]{1,0:T(8,128)(2,1)S(1)}, u32[]{:S(2)}, u32[]{:S(2)}) collective-permute-start(bf16[64,2048]{1,0:T(8,128)(2,1)S(1)} %collective-permute-done.3.refs_1_.refs_2_), channel_id=1, source_target_pairs={{0,2},{2,0},{4,6},{6,4},{8,10},{10,8},{12,14},{14,12},{1,3},{3,1},... | collective-permute-start | bytes 786440 | tf_op jit(solution)/shard_map/ppermute | solution.py:258
  15.3 8.4 %collective-permute-done.refs_3_.refs_4_ = bf16[64,2048]{1,0:T(8,128)(2,1)S(1)} collective-permute-done((bf16[64,2048]{1,0:T(8,128)(2,1)}, bf16[64,2048]{1,0:T(8,128)(2,1)S(1)}, u32[]{:S(2)}, u32[]{:S(2)}) %collective-permute-start) | collective-permute-done | bytes 262176 | tf_op jit(solution)/shard_map/ppermute | solution.py:261
  23.6 4.7 %collective-permute-start.1 = (bf16[64,2048]{1,0:T(8,128)(2,1)}, bf16[64,2048]{1,0:T(8,128)(2,1)S(1)}, u32[]{:S(2)}, u32[]{:S(2)}) collective-permute-start(bf16[64,2048]{1,0:T(8,128)(2,1)} %refs_1_.7), channel_id=1, source_target_pairs={{0,4},{2,6},{4,8},{6,10},{8,12},{10,14},{12,0},{14,2},{1,5},{3,7},... | collective-permute-start | bytes 786440 | tf_op jit(solution)/shard_map/ppermute | solution.py:261
  29.8 2.8 %collective-permute-start.2 = (bf16[64,2048]{1,0:T(8,128)(2,1)}, bf16[64,2048]{1,0:T(8,128)(2,1)S(1)}, u32[]{:S(2)}, u32[]{:S(2)}) collective-permute-start(bf16[64,2048]{1,0:T(8,128)(2,1)} %refs_1_.7), channel_id=1, source_target_pairs={{0,12},{2,14},{4,0},{6,2},{8,4},{10,6},{12,8},{14,10},{1,13},{3,15... | collective-permute-start | bytes 786440 | tf_op jit(solution)/shard_map/ppermute | solution.py:261
  33.1 4.8 %collective-permute-start.10 = (bf16[64,2048]{1,0:T(8,128)(2,1)}, bf16[64,2048]{1,0:T(8,128)(2,1)S(1)}, u32[]{:S(2)}, u32[]{:S(2)}) collective-permute-start(bf16[64,2048]{1,0:T(8,128)(2,1)} %refs_1_.7), channel_id=1, source_target_pairs={{0,8},{2,10},{4,12},{6,14},{8,0},{10,2},{12,4},{14,6},{1,9},{3,11}... | collective-permute-start | bytes 786440 | tf_op jit(solution)/shard_map/ppermute | solution.py:261
  38.4 1.5 %collective-permute-start.11 = (bf16[64,2048]{1,0:T(8,128)(2,1)S(1)}, bf16[64,2048]{1,0:T(8,128)(2,1)S(1)}, u32[]{:S(2)}, u32[]{:S(2)}) collective-permute-start(bf16[64,2048]{1,0:T(8,128)(2,1)S(1)} %collective-permute-done.1.refs_1_.refs_2_), channel_id=1, source_target_pairs={{0,2},{2,0},{4,6},{6,4},{8,10},{10,8},{12,14},{14,12},{1,3},{3,1},... | collective-permute-start | bytes 786440 | tf_op jit(solution)/shard_map/ppermute | solution.py:258
  40.0 2.0 %collective-permute-done.2.refs_2_.refs_3_ = bf16[64,2048]{1,0:T(8,128)(2,1)S(1)} collective-permute-done((bf16[64,2048]{1,0:T(8,128)(2,1)}, bf16[64,2048]{1,0:T(8,128)(2,1)S(1)}, u32[]{:S(2)}, u32[]{:S(2)}) %collective-permute-start.2) | collective-permute-done | bytes 262176 | tf_op jit(solution)/shard_map/ppermute | solution.py:261
  42.1 2.5 %collective-permute-start.12 = (bf16[64,2048]{1,0:T(8,128)(2,1)S(1)}, bf16[64,2048]{1,0:T(8,128)(2,1)S(1)}, u32[]{:S(2)}, u32[]{:S(2)}) collective-permute-start(bf16[64,2048]{1,0:T(8,128)(2,1)S(1)} %collective-permute-done.2.refs_2_.refs_3_), channel_id=1, source_target_pairs={{0,2},{2,0},{4,6},{6,4},{8,10},{10,8},{12,14},{14,12},{1,3},{3,1},... | collective-permute-start | bytes 786440 | tf_op jit(solution)/shard_map/ppermute | solution.py:258
  45.6 7.0 %shard_map.67.refs_9_ = bf16[512,2048]{1,0:T(8,128)(2,1)S(1)} custom-call(bf16[64,2048]{1,0:T(8,128)(2,1)S(1)} %copy-done, bf16[64,2048]{1,0:T(8,128)(2,1)S(1)} %collective-permute-done.3.refs_1_.refs_2_, bf16[64,2048]{1,0:T(8,128)(2,1)S(1)} %collective-permute-done.4.refs_2_.refs_3_, bf16[64,2048]{1,0:T(8,128)(2,1)S(1)} %collective-permute-done.refs_3_.refs_4_, ...), custom_call_target="tpu_custom_call" | custom-call | flops 214748368 | bytes 629145 | tf_op jit(solution)/shard_map/pallas_call | solution.py:52
  54.7 7.0 %shard_map.68.refs_9_ = bf16[512,2048]{1,0:T(8,128)(2,1)S(1)} custom-call(bf16[64,2048]{1,0:T(8,128)(2,1)S(1)} %copy-done, bf16[64,2048]{1,0:T(8,128)(2,1)S(1)} %collective-permute-done.3.refs_1_.refs_2_, bf16[64,2048]{1,0:T(8,128)(2,1)S(1)} %collective-permute-done.4.refs_2_.refs_3_, bf16[64,2048]{1,0:T(8,128)(2,1)S(1)} %collective-permute-done.refs_3_.refs_4_, ...), custom_call_target="tpu_custom_call" | custom-call | flops 21474836480 | bytes 62914560 | tf_op jit(solution)/shard_map/pallas_call | solution.py:52
  61.8 9.1 %shard_map.69 = (bf16[512,2048]{1,0:T(8,128)(2,1)S(1)}, bf16[512,2048]{1,0:T(8,128)(2,1)S(1)}) custom-call(bf16[64,2048]{1,0:T(8,128)(2,1)S(1)} %copy-done.2, bf16[64,2048]{1,0:T(8,128)(2,1)S(1)} %collective-permute-done.1.refs_1_.refs_2_, bf16[64,2048]{1,0:T(8,128)(2,1)S(1)} %collective-permute-done.2.refs_2_.refs_3_, ...), custom_call_target="tpu_custom_call" | custom-call | flops 21474836480 | bytes 94371840 | tf_op jit(solution)/shard_map/pallas_call | solution.py:52
  71.5 9.1 %shard_map.70 = (bf16[512,2048]{1,0:T(8,128)(2,1)S(1)}, bf16[512,2048]{1,0:T(8,128)(2,1)S(1)}) custom-call(bf16[64,2048]{1,0:T(8,128)(2,1)S(1)} %copy-done.2, bf16[64,2048]{1,0:T(8,128)(2,1)S(1)} %collective-permute-done.1.refs_1_.refs_2_, bf16[64,2048]{1,0:T(8,128)(2,1)S(1)} %collective-permute-done.2.refs_2_.refs_3_, ...), custom_call_target="tpu_custom_call" | custom-call | flops 214748368 | bytes 943718 | tf_op jit(solution)/shard_map/pallas_call | solution.py:52
  80.7 6.7 %shard_map.71.refs_9_ = bf16[4096,2048]{1,0:T(8,128)(2,1)} custom-call(bf16[512,2048]{1,0:T(8,128)(2,1)S(1)} %get-tuple-element.50.refs_0_, bf16[64,2048]{1,0:T(8,128)(2,1)S(1)} %copy-done.2, bf16[64,2048]{1,0:T(8,128)(2,1)S(1)} %collective-permute-done.1.refs_1_.refs_2_, bf16[64,2048]{1,0:T(8,128)(2,1)S(1)} %collective-permute-done.2.refs_2_.refs_3_, ...), custom_call_target="tpu_custom_call" | custom-call | flops 21474836480 | bytes 62914560 | tf_op jit(solution)/shard_map/pallas_call | solution.py:198
  89.6 5.8 %shard_map.72 = (f32[256,1024]{1,0:T(8,128)S(1)}, bf16[256,1024]{1,0:T(8,128)(2,1)S(1)}, bf16[512,4096]{1,0:T(8,128)(2,1)S(1)}) custom-call(bf16[512,2048]{1,0:T(8,128)(2,1)S(1)} %get-tuple-element.51.refs_0_, bf16[512,2048]{1,0:T(8,128)(2,1)S(1)} %get-tuple-element.49.refs_1_, bf16[512,2048]{1,0:T(8,128)(2,1)S(1)} %collective-permute-done.16.refs_2_, ...), custom_call_target="tpu_custom_call" | custom-call | flops 214748368 | bytes 838860 | tf_op jit(solution)/shard_map/pallas_call | solution.py:52
  96.5 4.8 %shard_map.73 = (f32[256,1024]{1,0:T(8,128)S(1)}, bf16[256,1024]{1,0:T(8,128)(2,1)S(1)}) custom-call(bf16[512,4096]{1,0:T(8,128)(2,1)S(1)} %get-tuple-element.66.refs_0_, bf16[2048,4096]{1,0:T(8,128)(2,1)S(1)} %bitcast.1), custom_call_target="tpu_custom_call" | custom-call | flops 214748368 | bytes 838860 | tf_op jit(solution)/shard_map/pallas_call | solution.py:52
  102.4 6.7 %shard_map.74 = bf16[4096,2048]{1,0:T(8,128)(2,1)} custom-call(bf16[512,2048]{1,0:T(8,128)(2,1)S(1)} %get-tuple-element.58.refs_0_, bf16[64,2048]{1,0:T(8,128)(2,1)S(1)} %copy-done.2, bf16[64,2048]{1,0:T(8,128)(2,1)S(1)} %collective-permute-done.1.refs_1_.refs_2_, ...), custom_call_target="tpu_custom_call", output_to_operand_aliasing={{}: (9, {})} | custom-call | flops 214748368 | bytes 629145 | tf_op jit(solution)/shard_map/pallas_call | solution.py:198
  110.4 4.2 %collective-permute-start.22 = (bf16[64,1024]{1,0:T(8,128)(2,1)S(1)}, bf16[64,1024]{1,0:T(8,128)(2,1)S(1)}, u32[]{:S(2)}, u32[]{:S(2)}) collective-permute-start(bf16[64,1024]{1,0:T(8,128)(2,1)S(1)} %get-tuple-element.76), channel_id=1, source_target_pairs={{0,8},{2,10},{4,12},{6,14},{8,0},{10,2},{12,4},{14,6},{1,9},{3,11}... | collective-permute-start | bytes 393224 | tf_op jit(solution)/shard_map/ppermute | solution.py:261
  114.6 3.8 %collective-permute-start.21 = (bf16[64,1024]{1,0:T(8,128)(2,1)S(1)}, bf16[64,1024]{1,0:T(8,128)(2,1)S(1)}, u32[]{:S(2)}, u32[]{:S(2)}) collective-permute-start(bf16[64,1024]{1,0:T(8,128)(2,1)S(1)} %get-tuple-element.78), channel_id=1, source_target_pairs={{0,12},{2,14},{4,0},{6,2},{8,4},{10,6},{12,8},{14,10},{1,13},{3,15... | collective-permute-start | bytes 393224 | tf_op jit(solution)/shard_map/ppermute | solution.py:261
  118.5 6.7 %shard_map.75.refs_9_ = bf16[2048,4096]{1,0:T(8,128)(2,1)} custom-call(bf16[512,4096]{1,0:T(8,128)(2,1)S(1)} %get-tuple-element.66.refs_0_, bf16[64,2048]{1,0:T(8,128)(2,1)S(1)} %copy-done.1, bf16[64,2048]{1,0:T(8,128)(2,1)S(1)} %collective-permute-done.3.refs_1_.refs_2_, bf16[64,2048]{1,0:T(8,128)(2,1)S(1)} %collective-permute-done.4.refs_2_.refs_3_, ...), custom_call_target="tpu_custom_call" | custom-call | flops 214748368 | bytes 629145 | tf_op jit(solution)/shard_map/pallas_call | solution.py:230
  126.6 2.9 %collective-permute-start.23 = (bf16[64,1024]{1,0:T(8,128)(2,1)S(1)}, bf16[64,1024]{1,0:T(8,128)(2,1)S(1)}, u32[]{:S(2)}, u32[]{:S(2)}) collective-permute-start(bf16[64,1024]{1,0:T(8,128)(2,1)S(1)} %get-tuple-element.65), channel_id=1, source_target_pairs={{0,12},{2,14},{4,0},{6,2},{8,4},{10,6},{12,8},{14,10},{1,13},{3,15... | collective-permute-start | bytes 393224 | tf_op jit(solution)/shard_map/ppermute | solution.py:261
  129.5 6.7 %shard_map.76 = bf16[2048,4096]{1,0:T(8,128)(2,1)} custom-call(bf16[512,4096]{1,0:T(8,128)(2,1)S(1)} %get-tuple-element.66.refs_0_, bf16[64,2048]{1,0:T(8,128)(2,1)S(1)} %copy-done.1, bf16[64,2048]{1,0:T(8,128)(2,1)S(1)} %collective-permute-done.3.refs_1_.refs_2_, ...), custom_call_target="tpu_custom_call", output_to_operand_aliasing={{}: (9, {})} | custom-call | flops 214748368 | bytes 629145 | tf_op jit(solution)/shard_map/pallas_call | solution.py:230
  (62 shorter events, 17.7 us)
Async XLA Ops:
  0.6 12.6 %collective-permute-start.3 = (bf16[64,2048]{1,0:T(8,128)(2,1)}, bf16[64,2048]{1,0:T(8,128)(2,1)S(1)}, u32[]{:S(2)}, u32[]{:S(2)}) collective-permute-start(bf16[64,2048]{1,0:T(8,128)(2,1)} %refs_1_.9), channel_id=1, source_target_pairs={{0,4},{2,6},{4,8},{6,10},{8,12},{10,14},{12,0},{14,2},{1,5},{3,7},... | collective-permute-start | bytes 786440 | tf_op jit(solution)/shard_map/ppermute | solution.py:261
  3.7 11.3 %collective-permute-start.5 = (bf16[64,2048]{1,0:T(8,128)(2,1)}, bf16[64,2048]{1,0:T(8,128)(2,1)S(1)}, u32[]{:S(2)}, u32[]{:S(2)}) collective-permute-start(bf16[64,2048]{1,0:T(8,128)(2,1)} %refs_1_.9), channel_id=1, source_target_pairs={{0,2},{2,0},{4,6},{6,4},{8,10},{10,8},{12,14},{14,12},{1,3},{3,1},... | collective-permute-start | bytes 786440 | tf_op jit(solution)/shard_map/ppermute | solution.py:258
  5.2 18.4 %collective-permute-start = (bf16[64,2048]{1,0:T(8,128)(2,1)}, bf16[64,2048]{1,0:T(8,128)(2,1)S(1)}, u32[]{:S(2)}, u32[]{:S(2)}) collective-permute-start(bf16[64,2048]{1,0:T(8,128)(2,1)} %refs_1_.9), channel_id=1, source_target_pairs={{0,8},{2,10},{4,12},{6,14},{8,0},{10,2},{12,4},{14,6},{1,9},{3,11}... | collective-permute-start | bytes 786440 | tf_op jit(solution)/shard_map/ppermute | solution.py:261
  7.8 20.5 %collective-permute-start.4 = (bf16[64,2048]{1,0:T(8,128)(2,1)}, bf16[64,2048]{1,0:T(8,128)(2,1)S(1)}, u32[]{:S(2)}, u32[]{:S(2)}) collective-permute-start(bf16[64,2048]{1,0:T(8,128)(2,1)} %refs_1_.9), channel_id=1, source_target_pairs={{0,12},{2,14},{4,0},{6,2},{8,4},{10,6},{12,8},{14,10},{1,13},{3,15... | collective-permute-start | bytes 786440 | tf_op jit(solution)/shard_map/ppermute | solution.py:261
  13.2 15.1 %collective-permute-start.6 = (bf16[64,2048]{1,0:T(8,128)(2,1)S(1)}, bf16[64,2048]{1,0:T(8,128)(2,1)S(1)}, u32[]{:S(2)}, u32[]{:S(2)}) collective-permute-start(bf16[64,2048]{1,0:T(8,128)(2,1)S(1)} %collective-permute-done.3.refs_1_.refs_2_), channel_id=1, source_target_pairs={{0,2},{2,0},{4,6},{6,4},{8,10},{10,8},{12,14},{14,12},{1,3},{3,1},... | collective-permute-start | bytes 786440 | tf_op jit(solution)/shard_map/ppermute | solution.py:258
  15.0 17.6 %collective-permute-start.8 = (bf16[64,2048]{1,0:T(8,128)(2,1)}, bf16[64,2048]{1,0:T(8,128)(2,1)S(1)}, u32[]{:S(2)}, u32[]{:S(2)}) collective-permute-start(bf16[64,2048]{1,0:T(8,128)(2,1)} %refs_1_.7), channel_id=1, source_target_pairs={{0,2},{2,0},{4,6},{6,4},{8,10},{10,8},{12,14},{14,12},{1,3},{3,1},... | collective-permute-start | bytes 786440 | tf_op jit(solution)/shard_map/ppermute | solution.py:258
  23.6 14.8 %collective-permute-start.1 = (bf16[64,2048]{1,0:T(8,128)(2,1)}, bf16[64,2048]{1,0:T(8,128)(2,1)S(1)}, u32[]{:S(2)}, u32[]{:S(2)}) collective-permute-start(bf16[64,2048]{1,0:T(8,128)(2,1)} %refs_1_.7), channel_id=1, source_target_pairs={{0,4},{2,6},{4,8},{6,10},{8,12},{10,14},{12,0},{14,2},{1,5},{3,7},... | collective-permute-start | bytes 786440 | tf_op jit(solution)/shard_map/ppermute | solution.py:261
  28.3 10.1 %collective-permute-start.7 = (bf16[64,2048]{1,0:T(8,128)(2,1)S(1)}, bf16[64,2048]{1,0:T(8,128)(2,1)S(1)}, u32[]{:S(2)}, u32[]{:S(2)}) collective-permute-start(bf16[64,2048]{1,0:T(8,128)(2,1)S(1)} %collective-permute-done.4.refs_2_.refs_3_), channel_id=1, source_target_pairs={{0,2},{2,0},{4,6},{6,4},{8,10},{10,8},{12,14},{14,12},{1,3},{3,1},... | collective-permute-start | bytes 786440 | tf_op jit(solution)/shard_map/ppermute | solution.py:258
  29.8 12.2 %collective-permute-start.2 = (bf16[64,2048]{1,0:T(8,128)(2,1)}, bf16[64,2048]{1,0:T(8,128)(2,1)S(1)}, u32[]{:S(2)}, u32[]{:S(2)}) collective-permute-start(bf16[64,2048]{1,0:T(8,128)(2,1)} %refs_1_.7), channel_id=1, source_target_pairs={{0,12},{2,14},{4,0},{6,2},{8,4},{10,6},{12,8},{14,10},{1,13},{3,15... | collective-permute-start | bytes 786440 | tf_op jit(solution)/shard_map/ppermute | solution.py:261
  32.6 9.6 %collective-permute-start.9 = (bf16[64,2048]{1,0:T(8,128)(2,1)S(1)}, bf16[64,2048]{1,0:T(8,128)(2,1)S(1)}, u32[]{:S(2)}, u32[]{:S(2)}) collective-permute-start(bf16[64,2048]{1,0:T(8,128)(2,1)S(1)} %collective-permute-done.refs_3_.refs_4_), channel_id=1, source_target_pairs={{0,2},{2,0},{4,6},{6,4},{8,10},{10,8},{12,14},{14,12},{1,3},{3,1},... | collective-permute-start | bytes 786440 | tf_op jit(solution)/shard_map/ppermute | solution.py:258
  33.1 20.1 %collective-permute-start.10 = (bf16[64,2048]{1,0:T(8,128)(2,1)}, bf16[64,2048]{1,0:T(8,128)(2,1)S(1)}, u32[]{:S(2)}, u32[]{:S(2)}) collective-permute-start(bf16[64,2048]{1,0:T(8,128)(2,1)} %refs_1_.7), channel_id=1, source_target_pairs={{0,8},{2,10},{4,12},{6,14},{8,0},{10,2},{12,4},{14,6},{1,9},{3,11}... | collective-permute-start | bytes 786440 | tf_op jit(solution)/shard_map/ppermute | solution.py:261
  38.4 14.8 %collective-permute-start.11 = (bf16[64,2048]{1,0:T(8,128)(2,1)S(1)}, bf16[64,2048]{1,0:T(8,128)(2,1)S(1)}, u32[]{:S(2)}, u32[]{:S(2)}) collective-permute-start(bf16[64,2048]{1,0:T(8,128)(2,1)S(1)} %collective-permute-done.1.refs_1_.refs_2_), channel_id=1, source_target_pairs={{0,2},{2,0},{4,6},{6,4},{8,10},{10,8},{12,14},{14,12},{1,3},{3,1},... | collective-permute-start | bytes 786440 | tf_op jit(solution)/shard_map/ppermute | solution.py:258
  42.1 12.6 %collective-permute-start.12 = (bf16[64,2048]{1,0:T(8,128)(2,1)S(1)}, bf16[64,2048]{1,0:T(8,128)(2,1)S(1)}, u32[]{:S(2)}, u32[]{:S(2)}) collective-permute-start(bf16[64,2048]{1,0:T(8,128)(2,1)S(1)} %collective-permute-done.2.refs_2_.refs_3_), channel_id=1, source_target_pairs={{0,2},{2,0},{4,6},{6,4},{8,10},{10,8},{12,14},{14,12},{1,3},{3,1},... | collective-permute-start | bytes 786440 | tf_op jit(solution)/shard_map/ppermute | solution.py:258
  52.6 9.3 %collective-permute-start.14 = (bf16[512,2048]{1,0:T(8,128)(2,1)S(1)}, bf16[512,2048]{1,0:T(8,128)(2,1)S(1)}, u32[]{:S(2)}, u32[]{:S(2)}) collective-permute-start(bf16[512,2048]{1,0:T(8,128)(2,1)S(1)} %shard_map.67.refs_9_), channel_id=1, source_target_pairs={{0,1},{1,0},{2,3},{3,2},{4,5},{5,4},{6,7},{7,6},{8,9},{9,8},{10,11... | collective-permute-start | bytes 6291464 | tf_op jit(solution)/shard_map/ppermute | solution.py:255
  61.7 9.8 %collective-permute-start.15 = (bf16[512,2048]{1,0:T(8,128)(2,1)S(1)}, bf16[512,2048]{1,0:T(8,128)(2,1)S(1)}, u32[]{:S(2)}, u32[]{:S(2)}) collective-permute-start(bf16[512,2048]{1,0:T(8,128)(2,1)S(1)} %shard_map.68.refs_9_), channel_id=1, source_target_pairs={{0,1},{1,0},{2,3},{3,2},{4,5},{5,4},{6,7},{7,6},{8,9},{9,8},{10,11... | collective-permute-start | bytes 6291464 | tf_op jit(solution)/shard_map/ppermute | solution.py:255
  71.0 16.5 %collective-permute-start.16 = (bf16[512,2048]{1,0:T(8,128)(2,1)S(1)}, bf16[512,2048]{1,0:T(8,128)(2,1)S(1)}, u32[]{:S(2)}, u32[]{:S(2)}) collective-permute-start(bf16[512,2048]{1,0:T(8,128)(2,1)S(1)} %get-tuple-element.51.refs_0_), channel_id=1, source_target_pairs={{0,1},{1,0},{2,3},{3,2},{4,5},{5,4},{6,7},{7,6},{8,9},{9,8},{10,11... | collective-permute-start | bytes 6291464 | tf_op jit(solution)/shard_map/ppermute | solution.py:255
  95.4 14.8 %collective-permute-start.18 = (bf16[256,1024]{1,0:T(8,128)(2,1)S(1)}, bf16[256,1024]{1,0:T(8,128)(2,1)S(1)}, u32[]{:S(2)}, u32[]{:S(2)}) collective-permute-start(bf16[256,1024]{1,0:T(8,128)(2,1)S(1)} %get-tuple-element.53), channel_id=1, source_target_pairs={{0,2},{2,0},{4,6},{6,4},{8,10},{10,8},{12,14},{14,12},{1,3},{3,1},... | collective-permute-start | bytes 1572872 | tf_op jit(solution)/shard_map/ppermute | solution.py:258
  101.4 23.8 %collective-permute-start.19 = (bf16[256,1024]{1,0:T(8,128)(2,1)S(1)}, bf16[256,1024]{1,0:T(8,128)(2,1)S(1)}, u32[]{:S(2)}, u32[]{:S(2)}) collective-permute-start(bf16[256,1024]{1,0:T(8,128)(2,1)S(1)} %get-tuple-element.61), channel_id=1, source_target_pairs={{0,2},{2,0},{4,6},{6,4},{8,10},{10,8},{12,14},{14,12},{1,3},{3,1},... | collective-permute-start | bytes 1572872 | tf_op jit(solution)/shard_map/ppermute | solution.py:258
  110.4 25.7 %collective-permute-start.22 = (bf16[64,1024]{1,0:T(8,128)(2,1)S(1)}, bf16[64,1024]{1,0:T(8,128)(2,1)S(1)}, u32[]{:S(2)}, u32[]{:S(2)}) collective-permute-start(bf16[64,1024]{1,0:T(8,128)(2,1)S(1)} %get-tuple-element.76), channel_id=1, source_target_pairs={{0,8},{2,10},{4,12},{6,14},{8,0},{10,2},{12,4},{14,6},{1,9},{3,11}... | collective-permute-start | bytes 393224 | tf_op jit(solution)/shard_map/ppermute | solution.py:261
  114.6 12.0 %collective-permute-start.20 = (bf16[64,1024]{1,0:T(8,128)(2,1)S(1)}, bf16[64,1024]{1,0:T(8,128)(2,1)S(1)}, u32[]{:S(2)}, u32[]{:S(2)}) collective-permute-start(bf16[64,1024]{1,0:T(8,128)(2,1)S(1)} %get-tuple-element.77), channel_id=1, source_target_pairs={{0,4},{2,6},{4,8},{6,10},{8,12},{10,14},{12,0},{14,2},{1,5},{3,7},... | collective-permute-start | bytes 393224 | tf_op jit(solution)/shard_map/ppermute | solution.py:261
  114.6 21.5 %collective-permute-start.21 = (bf16[64,1024]{1,0:T(8,128)(2,1)S(1)}, bf16[64,1024]{1,0:T(8,128)(2,1)S(1)}, u32[]{:S(2)}, u32[]{:S(2)}) collective-permute-start(bf16[64,1024]{1,0:T(8,128)(2,1)S(1)} %get-tuple-element.78), channel_id=1, source_target_pairs={{0,12},{2,14},{4,0},{6,2},{8,4},{10,6},{12,8},{14,10},{1,13},{3,15... | collective-permute-start | bytes 393224 | tf_op jit(solution)/shard_map/ppermute | solution.py:261
  125.4 10.9 %collective-permute-start.25 = (bf16[64,1024]{1,0:T(8,128)(2,1)S(1)}, bf16[64,1024]{1,0:T(8,128)(2,1)S(1)}, u32[]{:S(2)}, u32[]{:S(2)}) collective-permute-start(bf16[64,1024]{1,0:T(8,128)(2,1)S(1)} %get-tuple-element.74), channel_id=1, source_target_pairs={{0,8},{2,10},{4,12},{6,14},{8,0},{10,2},{12,4},{14,6},{1,9},{3,11}... | collective-permute-start | bytes 393224 | tf_op jit(solution)/shard_map/ppermute | solution.py:261
  125.5 10.8 %collective-permute-start.24 = (bf16[64,1024]{1,0:T(8,128)(2,1)S(1)}, bf16[64,1024]{1,0:T(8,128)(2,1)S(1)}, u32[]{:S(2)}, u32[]{:S(2)}) collective-permute-start(bf16[64,1024]{1,0:T(8,128)(2,1)S(1)} %get-tuple-element.75), channel_id=1, source_target_pairs={{0,4},{2,6},{4,8},{6,10},{8,12},{10,14},{12,0},{14,2},{1,5},{3,7},... | collective-permute-start | bytes 393224 | tf_op jit(solution)/shard_map/ppermute | solution.py:261
  126.6 9.7 %collective-permute-start.23 = (bf16[64,1024]{1,0:T(8,128)(2,1)S(1)}, bf16[64,1024]{1,0:T(8,128)(2,1)S(1)}, u32[]{:S(2)}, u32[]{:S(2)}) collective-permute-start(bf16[64,1024]{1,0:T(8,128)(2,1)S(1)} %get-tuple-element.65), channel_id=1, source_target_pairs={{0,12},{2,14},{4,0},{6,2},{8,4},{10,6},{12,8},{14,10},{1,13},{3,15... | collective-permute-start | bytes 393224 | tf_op jit(solution)/shard_map/ppermute | solution.py:261
  (9 other events, 65.0 us)
